TPU v7x, 32 devices: a whole 2x2x4 slice. The times are simulated.
32 devices in a mesh: rows: 8 (over y, x, core), grp: 4 (over z).
Axes of the slice: x: 2, y: 2, z: 4, core: 2. Of those that a mesh axis runs over, the one named last changes fastest.
Arguments:
- hc_edge: bfloat16 [65536, 512], P(('rows', 'grp')), may hold values from -6 to 6
- hp_edge: bfloat16 [65536, 512], P(('rows', 'grp')), may hold values from -6 to 6
- cust_count: int32 [32, 32], P(('rows', 'grp')), may hold values from 0 to 64, as said below
- recv_key: int32 [65536], P(('rows', 'grp')), may hold values from 0 to 2047
- prod_key: int32 [65536], P(('rows', 'grp')), may hold values from 0 to 255
- cust_grad: bfloat16 [65536, 512], P(('rows', 'grp')), may hold values from -6 to 6
- prod_grad: bfloat16 [256, 512], P(('rows', 'grp')), may hold values from -6 to 6
- w_cust: bfloat16 [512, 512], replicated, may hold values from -0.25 to 0.25
- w_prod: bfloat16 [512, 512], replicated, may hold values from -0.25 to 0.25
Outputs:
- cust_table_grad: float32 [65536, 512], P(('rows', 'grp'))
- prod_table_grad: float32 [256, 512], P(('rows', 'grp'))
- w_cust_grad: float32 [512, 512], replicated
- w_prod_grad: float32 [512, 512], replicated
Inputs may be any that keep to these rules, and one draw needn't show every extreme that they name: `cust_count`: entry [i, j] counts the live slots of device i's block for owner j; every device fills its block to 64 for one or more owners, which differ between draws. `recv_key`: keys of slots past a block's count are ignored. `prod_key`: ids of slots that are not live are ignored.
All inputs are finite; a program needn't handle non-finite values.
Results may differ from a plain program's by a relative error of at most 0.0034.
Values may be sent and summed in bfloat16 or wider, within the bound.
No kernel may reach another device: no remote copies, remote signals or barrier semaphores. Data moves between devices by JAX's collectives and lax.ppermute only.
A program may use at most 64 MiB of HBM per device.

v0:
```python
import math

import jax
import jax.numpy as jnp
from jax import lax
from jax.sharding import PartitionSpec as P


def body(hc_edge, hp_edge, cust_count, recv_key, prod_key, cust_grad, prod_grad, w_cust, w_prod):
    devices = lax.axis_size(("rows", "grp"))
    slot_count, feature_width = hc_edge.shape
    capacity = slot_count // devices
    live_mask = (
        jnp.arange(capacity, dtype=jnp.int32)[None, :] < cust_count.reshape(devices, 1)
    ).reshape(slot_count)
    owned_rows = jnp.take(cust_grad, recv_key, axis=0)
    fetched = lax.all_to_all(
        owned_rows.reshape(devices, capacity, feature_width),
        ("rows", "grp"),
        split_axis=0,
        concat_axis=0,
        tiled=True,
    )
    fetched = fetched.reshape(slot_count, feature_width)
    product_table = lax.all_gather(prod_grad, ("rows", "grp"), axis=0, tiled=True)
    product_rows = jnp.take(product_table, prod_key, axis=0)
    preact = jnp.dot(hc_edge, w_cust, preferred_element_type=jnp.float32) + jnp.dot(
        hp_edge, w_prod, preferred_element_type=jnp.float32
    )
    squashed = jax.nn.sigmoid(preact)
    upstream = jnp.where(
        live_mask[:, None],
        fetched.astype(jnp.float32) + product_rows.astype(jnp.float32),
        jnp.float32(0.0),
    )
    delta = (upstream * squashed * (1.0 + preact * (1.0 - squashed))).astype(jnp.bfloat16)
    returned = lax.all_to_all(
        delta.reshape(devices, capacity, feature_width),
        ("rows", "grp"),
        split_axis=0,
        concat_axis=0,
        tiled=True,
    )
    returned = returned.reshape(slot_count, feature_width)
    owned_count = cust_grad.shape[0]
    one_hot = (recv_key[None, :] == jnp.arange(owned_count, dtype=jnp.int32)[:, None]).astype(
        jnp.bfloat16
    )
    cust_sum = jnp.dot(one_hot, returned, preferred_element_type=jnp.float32).astype(jnp.bfloat16)
    cust_table_grad = lax.dot_general(
        cust_sum, w_cust, (((1,), (1,)), ((), ())), preferred_element_type=jnp.float32
    )
    product_count = prod_grad.shape[0]
    wanted = jnp.arange(lax.axis_size(("rows", "grp")) * product_count, dtype=jnp.int32)
    product_hot = (prod_key[None, :] == wanted[:, None]).astype(jnp.bfloat16)
    prod_sum = lax.psum_scatter(
        jnp.dot(product_hot, delta, preferred_element_type=jnp.float32),
        ("rows", "grp"),
        scatter_dimension=0,
        tiled=True,
    ).astype(jnp.bfloat16)
    prod_table_grad = lax.dot_general(
        prod_sum, w_prod, (((1,), (1,)), ((), ())), preferred_element_type=jnp.float32
    ) * math.sqrt(product_count / slot_count)
    weight_terms = (
        lax.dot_general(
            hc_edge, delta, (((0,), (0,)), ((), ())), preferred_element_type=jnp.float32
        ),
        lax.dot_general(
            hp_edge, delta, (((0,), (0,)), ((), ())), preferred_element_type=jnp.float32
        ),
    )
    cust_weight, prod_weight = lax.psum((weight_terms[0], weight_terms[1]), ("rows", "grp"))
    grad_scale = 1.0 / math.sqrt(slot_count * devices)
    return (cust_table_grad, prod_table_grad, cust_weight * grad_scale, prod_weight * grad_scale)


def solution(mesh):
    placed = (
        P(("rows", "grp"), None),
        P(("rows", "grp"), None),
        P(("rows", "grp"), None),
        P(("rows", "grp")),
        P(("rows", "grp")),
        P(("rows", "grp"), None),
        P(("rows", "grp"), None),
        P(),
        P(),
    )
    return jax.shard_map(
        body,
        mesh=mesh,
        in_specs=placed,
        out_specs=(P(("rows", "grp"), None), P(("rows", "grp"), None), P(), P()),
        check_vma=False,
    )
```

profile of v0, /device:TPU:1, one launch (start us, length us, event | category | flops | bytes accessed | tf_op | source)
XLA Modules:
  0.0 469.9 jit_solution(7425684962800656621)
XLA Ops:
  7.2 0.0 copy-start
  7.2 0.9 compare_and_fusion.1
  8.0 0.7 fusion.11
  8.7 0.1 broadcast_in_dim.44
  8.8 11.1 %gather_fusion = bf16[2048,512]{1,0:T(8,128)(2,1)} fusion(bf16[2048,512]{1,0:T(8,128)(2,1)} %param.14, s32[2048]{0:T(1024)S(1)} %fusion.11), kind=kCustom, calls=%fused_computation | custom fusion | bytes 4202496 | tf_op jit(solution)/shard_map/jit(_take)/gather | solution.py:16
  19.9 2.8 broadcast_select_fusion
  22.7 7.2 %all-to-all-start = ((bf16[32,64,512]{2,1,0:T(8,128)(2,1)}), bf16[32,64,512]{2,1,0:T(8,128)(2,1)}, u32[]{:S(2)}, u32[]{:S(2)}) async-start(bf16[32,64,512]{2,1,0:T(8,128)(2,1)} %broadcast_select_fusion), calls=%async_computation | async-start | bytes 4194304 | tf_op jit(solution)/shard_map/all_to_all | solution.py:17
  29.9 0.1 iota_compare_fusion.8
  29.9 0.1 lt.40
  30.0 103.4 %all_gather.3 = bf16[256,512]{1,0:T(8,128)(2,1)S(1)} all-gather(bf16[8,512]{1,0:T(8,128)(2,1)S(1)} %copy-done.7), channel_id=1, replica_groups=mesh['rows'=8,'grp'=4] {'rows','grp'}, dimensions={0}, use_global_device_ids=true | all-gather | bytes 270336 | tf_op jit(solution)/shard_map/all_gather | solution.py:25
  133.5 0.0 copy-start.3
  133.5 9.2 %gather_fusion.1 = bf16[2048,512]{1,0:T(8,128)(2,1)} fusion(bf16[256,512]{1,0:T(8,128)(2,1)S(1)} %all_gather.3, s32[2048]{0:T(1024)S(1)} %fusion.12), kind=kCustom, calls=%fused_computation.1 | custom fusion | bytes 4202496 | tf_op jit(solution)/shard_map/jit(_take)/gather | solution.py:26
  142.7 0.0 copy-start.4
  142.7 4.9 %fusion.13 = f32[2048,512]{1,0:T(8,128)} fusion(bf16[2048,512]{1,0:T(8,128)(2,1)} %param.9, bf16[512,512]{1,0:T(8,128)(2,1)S(1)} %copy-done.3), kind=kOutput, calls=%fused_computation.29 | convolution fusion | flops 1073741824 | bytes 6815744 | tf_op jit(solution)/shard_map/dot_general | solution.py:27
  147.7 0.0 all-to-all-done
  147.7 6.9 %fusion.5 = bf16[2048,512]{1,0:T(8,128)(2,1)} fusion(bf16[2048,512]{1,0:T(8,128)(2,1)} %bitcast.7, f32[2048,512]{1,0:T(8,128)} %fusion.13, bf16[2048,512]{1,0:T(8,128)(2,1)S(1)} %copy-done, bf16[512,512]{1,0:T(8,128)(2,1)S(1)} %copy-done.4, bf16[2048,512]{1,0:T(8,128)(2,1)} %gather_fusion.1, pred[2048]{0:T(1024)(128)(4,1)S(1)} %compare_and_fusion, ...), kind=kOutput, calls=%fused_computation.9 | convolution fusion | flops 1089470464 | bytes 13111296 | tf_op jit(solution)/shard_map/dot_general | solution.py:27
  154.6 8.4 %all-to-all-start.1 = ((bf16[32,64,512]{2,1,0:T(8,128)(2,1)}), bf16[32,64,512]{2,1,0:T(8,128)(2,1)}, u32[]{:S(2)}, u32[]{:S(2)}) async-start(bf16[32,64,512]{2,1,0:T(8,128)(2,1)} %bitcast.23), calls=%async_computation.1 | async-start | bytes 4194304 | tf_op jit(solution)/shard_map/all_to_all | solution.py:37
  163.0 0.0 all-reduce.3.cloned.1.call-start
  163.1 0.0 copy-start.1
  163.1 4.0 convolution_bitcast_fusion
  167.1 2.2 convolution_bitcast_fusion.1
  169.3 0.0 all-reduce.3.cloned.1.call-update
  169.3 0.2 reduce-scatter.2.cloned.1.call-start
  169.6 3.1 fusion.7
  172.7 0.0 reduce-scatter.2.cloned.1.call-update
  172.7 146.7 %all-reduce.3.cloned.1.call-done = (f32[512,512]{0,1:T(8,128)}, f32[512,512]{0,1:T(8,128)}) async-done(((f32[512,512]{0,1:T(8,128)}, f32[512,512]{0,1:T(8,128)}), (f32[512,512]{0,1:T(8,128)}, f32[512,512]{0,1:T(8,128)})) %all-reduce.3.cloned.1.call-update) | async-done | bytes 2097168 | tf_op jit(solution)/shard_map/psum | solution.py:73
  319.4 2.8 broadcast_multiply_fusion
  322.2 2.5 copy.14
  324.8 1.3 copy.13
  326.1 125.8 %reduce-scatter.2.cloned.1.call-done = f32[8,512]{1,0:T(8,128)} async-done(((f32[256,512]{1,0:T(8,128)}), f32[8,512]{1,0:T(8,128)}) %reduce-scatter.2.cloned.1.call-update) | async-done | bytes 16400 | tf_op jit(solution)/shard_map/reduce_scatter | solution.py:56
  451.9 1.9 convolution_multiply_fusion
  453.8 9.3 %fusion.8 = f32[2048,512]{1,0:T(8,128)} fusion(bf16[512,512]{1,0:T(8,128)(2,1)} %param.16, bf16[2048,512]{1,0:T(8,128)(2,1)} %bitcast.4, s32[2048]{0:T(1024)S(1)} %copy-done.6), kind=kOutput, calls=%fused_computation.16 | convolution fusion | flops 5373952000 | bytes 6823936 | tf_op jit(solution)/shard_map/dot_general | solution.py:50
  (17 shorter events, 0.0 us)
Async XLA Ops:
  7.2 140.5 %copy-start = (bf16[2048,512]{1,0:T(8,128)(2,1)S(1)}, bf16[2048,512]{1,0:T(8,128)(2,1)}, u32[]{:S(2)}) copy-start(bf16[2048,512]{1,0:T(8,128)(2,1)} %param.10) | copy-start | bytes 6291460
  22.7 7.2 %copy-start.8 = (s32[1,32]{1,0:T(1,128)S(1)}, s32[1,32]{1,0:T(1,128)}, u32[]{:S(2)}) copy-start(s32[1,32]{1,0:T(1,128)} %param.11) | copy-start | bytes 388
  22.7 7.3 %copy-start.7 = (bf16[8,512]{1,0:T(8,128)(2,1)S(1)}, bf16[8,512]{1,0:T(8,128)(2,1)}, u32[]{:S(2)}) copy-start(bf16[8,512]{1,0:T(8,128)(2,1)} %param.15) | copy-start | bytes 24580
  22.7 110.8 %copy-start.5 = (s32[2048]{0:T(1024)S(1)}, s32[2048]{0:T(1024)}, u32[]{:S(2)}) copy-start(s32[2048]{0:T(1024)} %param.13) | copy-start | bytes 24580
  22.7 124.9 %all-to-all-start = ((bf16[32,64,512]{2,1,0:T(8,128)(2,1)}), bf16[32,64,512]{2,1,0:T(8,128)(2,1)}, u32[]{:S(2)}, u32[]{:S(2)}) async-start(bf16[32,64,512]{2,1,0:T(8,128)(2,1)} %broadcast_select_fusion), calls=%async_computation | async-start | bytes 4194304 | tf_op jit(solution)/shard_map/all_to_all | solution.py:17
  133.5 9.2 %copy-start.3 = (bf16[512,512]{1,0:T(8,128)(2,1)S(1)}, bf16[512,512]{1,0:T(8,128)(2,1)}, u32[]{:S(2)}) copy-start(bf16[512,512]{1,0:T(8,128)(2,1)} %param.16) | copy-start | bytes 1572868
  142.7 4.9 %copy-start.4 = (bf16[512,512]{1,0:T(8,128)(2,1)S(1)}, bf16[512,512]{1,0:T(8,128)(2,1)}, u32[]{:S(2)}) copy-start(bf16[512,512]{1,0:T(8,128)(2,1)} %param.17) | copy-start | bytes 1572868
  154.6 299.2 %all-to-all-start.1 = ((bf16[32,64,512]{2,1,0:T(8,128)(2,1)}), bf16[32,64,512]{2,1,0:T(8,128)(2,1)}, u32[]{:S(2)}, u32[]{:S(2)}) async-start(bf16[32,64,512]{2,1,0:T(8,128)(2,1)} %bitcast.23), calls=%async_computation.1 | async-start | bytes 4194304 | tf_op jit(solution)/shard_map/all_to_all | solution.py:37
  163.0 156.4 %all-reduce.3.cloned.1.call-start = ((), (), s32[]{:S(2)}) async-start(), calls=%async_computation.4 | async-start | bytes 4194304 | tf_op jit(solution)/shard_map/psum | solution.py:73
  163.1 4.0 copy-start.1
  163.1 4.0 copy-start.2
  169.3 282.5 %reduce-scatter.2.cloned.1.call-start = ((), (), s32[]{:S(2)}) async-start(), calls=%async_computation.3 | async-start | bytes 540672 | tf_op jit(solution)/shard_map/reduce_scatter | solution.py:56
  322.2 131.6 %copy-start.6 = (s32[2048]{0:T(1024)S(1)}, s32[2048]{0:T(1024)}, u32[]{:S(2)}) copy-start(s32[2048]{0:T(1024)} %param.12) | copy-start | bytes 24580
Sparse Core Ops, SparseCore 0:
  169.9 149.4 all-reduce.2
  322.3 129.5 reduce-scatter.1
where the time goes:
time: 476 us; the launch traced here: 470 us
  waiting for transfers between devices  273 us (57%)
  blocking collectives  103 us (22%)
  matrix products  32.4 us (7%)
  local copies, waits for them, and re-layouts  24.4 us (5%)
  starting transfers between devices  15.8 us (3%)
  between operations  14.1 us (3%)
  other arithmetic  7.22 us (2%)
    psum x1, waiting for transfers between devices, body(): lax.psum((weight_terms[0], weight_terms[1]), ('rows', 'grp'))  147 us
    reduce_scatter x1, waiting for transfers between devices, body(): lax.psum_scatter(jnp.dot(product_hot, delta, preferred_element_type=jnp.f...  126 us
    all_gather x1, blocking collectives, body(): lax.all_gather(prod_grad, ('rows', 'grp'), axis=0, tiled=True)  103 us
    gather x1, local copies, waits for them, and re-layouts, body(): owned_rows = jnp.take(cust_grad, recv_key, axis=0)  11.1 us
  transfers between devices with their start and end apart: 4, of which 2 were waited for; matrix products, arithmetic and copies ran while one was open for 7% of the time, Pallas kernels for 0%

commit v1 on v0

v1 whole, which is shorter than its diff:
```python
import math

import jax
import jax.numpy as jnp
from jax import lax
from jax.sharding import PartitionSpec as P

AXES = ("rows", "grp")


def shift_rows(value, mask):
    size = lax.axis_size("rows")
    return lax.ppermute(value, "rows", [(i, i ^ mask) for i in range(size)])


def shift_grp(value, mask):
    size = lax.axis_size("grp")
    return lax.ppermute(value, "grp", [(i, i ^ mask) for i in range(size)])


def place():
    row = lax.axis_index("rows")
    return row % 2, row // 2, lax.axis_index("grp")


def spread(mine, shift, size, step, here):
    blocks = [mine] + [shift(mine, step * k) for k in range(1, size)]
    stacked = jnp.zeros((size,) + mine.shape, mine.dtype)
    for k, block in enumerate(blocks):
        stacked = lax.dynamic_update_index_in_dim(stacked, block, here ^ k, 0)
    return stacked


def gather_all(mine):
    core, plane, grp = place()
    planes = lax.axis_size("rows") // 2
    own = spread(mine, shift_grp, lax.axis_size("grp"), 1, grp)
    own = spread(own, shift_rows, planes, 2, plane)
    other = shift_rows(own, 1)
    first = core == 0
    return jnp.stack([jnp.where(first, own, other), jnp.where(first, other, own)])


def fold(terms, shift, size, step, here):
    total = lax.dynamic_index_in_dim(terms, here, 0, False)
    leaving = terms.astype(jnp.bfloat16)
    for k in range(1, size):
        sent = lax.dynamic_index_in_dim(leaving, here ^ k, 0, False)
        total = total + shift(sent, step * k).astype(jnp.float32)
    return total


def reduce_all(terms):
    core, plane, grp = place()
    sent = lax.dynamic_index_in_dim(terms, 1 - core, 0, False)
    kept = lax.dynamic_index_in_dim(terms, core, 0, False) + shift_rows(sent, 1)
    kept = fold(kept, shift_rows, lax.axis_size("rows") // 2, 2, plane)
    return fold(kept, shift_grp, lax.axis_size("grp"), 1, grp)


def body(hc_edge, hp_edge, cust_count, recv_key, prod_key, cust_grad, prod_grad, w_cust, w_prod):
    devices = lax.axis_size(AXES)
    grps = lax.axis_size("grp")
    planes = lax.axis_size("rows") // 2
    slot_count, width = hc_edge.shape
    capacity = slot_count // devices
    product_count = prod_grad.shape[0]
    grid = (2, planes, grps)

    owned_rows = jnp.take(cust_grad, recv_key, axis=0, mode="clip")
    fetched = lax.all_to_all(
        owned_rows.reshape(devices, capacity, width), AXES, split_axis=0, concat_axis=0, tiled=True
    ).reshape(slot_count, width)

    owner, low = prod_key // product_count, prod_key % product_count
    row, grp = owner // grps, owner % grps
    prod_at = (((row % 2) * planes + row // 2) * grps + grp) * product_count + low
    product_table = gather_all(prod_grad).reshape(devices * product_count, width)
    product_rows = jnp.take(product_table, prod_at, axis=0, mode="clip")

    preact = jnp.dot(hc_edge, w_cust, preferred_element_type=jnp.float32) + jnp.dot(
        hp_edge, w_prod, preferred_element_type=jnp.float32
    )
    squashed = jax.nn.sigmoid(preact)
    live_mask = (
        jnp.arange(capacity, dtype=jnp.int32)[None, :] < cust_count.reshape(devices, 1)
    ).reshape(slot_count)
    gate = jnp.where(live_mask[:, None], squashed * (1.0 + preact * (1.0 - squashed)), 0.0)
    gate, product_rows = lax.optimization_barrier((gate, product_rows))

    upstream = fetched.astype(jnp.float32) + product_rows.astype(jnp.float32)
    delta = (upstream * gate).astype(jnp.bfloat16)

    returned = lax.all_to_all(
        delta.reshape(devices, capacity, width), AXES, split_axis=0, concat_axis=0, tiled=True
    ).reshape(slot_count, width)

    wanted = jnp.arange(devices * product_count, dtype=jnp.int32)
    product_hot = (prod_at[None, :] == wanted[:, None]).astype(jnp.bfloat16)
    contract = (((0,), (0,)), ((), ()))
    terms = jnp.concatenate(
        [
            jnp.dot(product_hot, delta, preferred_element_type=jnp.float32).reshape(*grid, -1, width),
            lax.dot_general(
                hc_edge, delta, contract, preferred_element_type=jnp.float32
            ).reshape(*grid, -1, width),
            lax.dot_general(
                hp_edge, delta, contract, preferred_element_type=jnp.float32
            ).reshape(*grid, -1, width),
        ],
        axis=3,
    )
    mine = reduce_all(terms)
    prod_table_grad = lax.dot_general(
        mine[:product_count],
        w_prod.astype(jnp.float32),
        (((1,), (1,)), ((), ())),
        precision=lax.Precision.HIGHEST,
        preferred_element_type=jnp.float32,
    ) * math.sqrt(product_count / slot_count)
    grad_scale = 1.0 / math.sqrt(slot_count * devices)
    share = width // devices
    weights = gather_all(mine[product_count:].astype(jnp.bfloat16)).astype(jnp.float32) * grad_scale
    cust_weight = weights[..., :share, :].reshape(width, width)
    prod_weight = weights[..., share:, :].reshape(width, width)

    owned_count = cust_grad.shape[0]
    one_hot = (recv_key[None, :] == jnp.arange(owned_count, dtype=jnp.int32)[:, None]).astype(
        jnp.bfloat16
    )
    cust_sum = jnp.dot(one_hot, returned, preferred_element_type=jnp.float32).astype(jnp.bfloat16)
    cust_table_grad = lax.dot_general(
        cust_sum, w_cust, (((1,), (1,)), ((), ())), preferred_element_type=jnp.float32
    )
    return cust_table_grad, prod_table_grad, cust_weight, prod_weight


def solution(mesh):
    rows = P(AXES, None)
    placed = (rows, rows, rows, P(AXES), P(AXES), rows, rows, P(), P())
    return jax.shard_map(
        body,
        mesh=mesh,
        in_specs=placed,
        out_specs=(rows, rows, P(), P()),
        check_vma=False,
    )
```

time: 476 us -> 185 us (0.39); the launches traced: 470 us -> 184 us
  waiting for transfers between devices: 273 us -> 92.3 us
  blocking collectives: 103 us -> 0 us
  starting transfers between devices: 15.8 us -> 38.1 us
  matrix products: 32.4 us -> 18.6 us
  between operations: 14.1 us -> 0.94 us
    psum x1 -> x0, waiting for transfers between devices: 147 us -> none  [body(): lax.psum((weight_terms[0], weight_terms[1]), ('rows', 'grp'))]
    reduce_scatter x1 -> x0, waiting for transfers between devices: 126 us -> none  [body(): lax.psum_scatter(jnp.dot(product_hot, delta, preferred_element_type=jnp.f...]
    all_gather x1 -> x0, blocking collectives: 103 us -> none  [body(): lax.all_gather(prod_grad, ('rows', 'grp'), axis=0, tiled=True)]
    ppermute x0 -> x21, waiting for transfers between devices: none -> 92.3 us  [the longest x9 60.4 us: shift_grp(): return lax.ppermute(value, 'grp', [(i, i ^ mask) for i in range(size)])]
    ppermute x0 -> x21, starting transfers between devices: none -> 27.6 us  [the longest x12 16.1 us: shift_rows(): return lax.ppermute(value, 'rows', [(i, i ^ mask) for i in range(size)])]
    convert_element_type x0 -> x3, other arithmetic: none -> 6.05 us  [the longest x1 4.31 us: body(): delta = (upstream * gate).astype(jnp.bfloat16)]
    all_to_all x2, starting transfers between devices: 15.6 us -> 10.6 us  [the longest x1 7.15 us: body(): lax.all_to_all(owned_rows.reshape(devices, capacity, width), AXES, split_...]
  transfers between devices with their start and end apart: 4 -> 23, of which waited for: 2 -> 16; matrix products, arithmetic and copies ran while one was open for 7% -> 11% of each run, Pallas kernels for 0% -> 0%
where the time goes in v1:
time: 185 us; the launch traced here: 184 us
  waiting for transfers between devices  92.3 us (50%)
  starting transfers between devices  38.1 us (21%)
  local copies, waits for them, and re-layouts  26.5 us (14%)
  matrix products  18.6 us (10%)
  other arithmetic  7.75 us (4%)
    ppermute x9, waiting for transfers between devices, shift_grp(): return lax.ppermute(value, 'grp', [(i, i ^ mask) for i in range(size)])  60.4 us
    ppermute x12, waiting for transfers between devices, shift_rows(): return lax.ppermute(value, 'rows', [(i, i ^ mask) for i in range(size)])  31.9 us
    ppermute x12, starting transfers between devices, shift_rows(): return lax.ppermute(value, 'rows', [(i, i ^ mask) for i in range(size)])  16.1 us
    ppermute x9, starting transfers between devices, shift_grp(): return lax.ppermute(value, 'grp', [(i, i ^ mask) for i in range(size)])  11.4 us
    gather x1, local copies, waits for them, and re-layouts, body(): owned_rows = jnp.take(cust_grad, recv_key, axis=0, mode='clip')  11.1 us
    dot_general x1, matrix products, body(): lax.dot_general(cust_sum, w_cust, (((1,), (1,)), ((), ())), preferred_ele...  9.21 us
    gather x1, local copies, waits for them, and re-layouts, body(): product_rows = jnp.take(product_table, prod_at, axis=0, mode='clip')  9.18 us
    all_to_all x1, starting transfers between devices, body(): lax.all_to_all(owned_rows.reshape(devices, capacity, width), AXES, split_...  7.15 us
  transfers between devices with their start and end apart: 23, of which 16 were waited for; matrix products, arithmetic and copies ran while one was open for 11% of the time, Pallas kernels for 0%

profile of v1, /device:TPU:1, one launch (start us, length us, event | category | flops | bytes accessed | tf_op | source)
XLA Modules:
  0.0 184.2 jit_solution(6071105018635223586)
XLA Ops:
  1.5 11.1 %gather_fusion = bf16[2048,512]{1,0:T(8,128)(2,1)} fusion(bf16[2048,512]{1,0:T(8,128)(2,1)} %param.14, s32[2048]{0:T(1024)S(1)} %broadcast_clamp_fusion.1), kind=kCustom, calls=%fused_computation | custom fusion | bytes 4202496 | tf_op jit(solution)/shard_map/jit(_take)/gather | solution.py:70
  12.6 7.2 %all-to-all-start = ((bf16[32,64,512]{2,1,0:T(8,128)(2,1)}), bf16[32,64,512]{2,1,0:T(8,128)(2,1)}, u32[]{:S(2)}, u32[]{:S(2)}) async-start(bf16[32,64,512]{2,1,0:T(8,128)(2,1)} %bitcast.100), calls=%async_computation | async-start | bytes 4194304 | tf_op jit(solution)/shard_map/all_to_all | solution.py:71
  19.8 1.5 collective-permute-start
  21.3 2.1 %collective-permute-start.1 = (bf16[8,512]{1,0:T(8,128)(2,1)S(1)}, bf16[8,512]{1,0:T(8,128)(2,1)S(1)}, u32[]{:S(2)}, u32[]{:S(2)}) collective-permute-start(bf16[8,512]{1,0:T(8,128)(2,1)S(1)} %copy-done.8), channel_id=1, source_target_pairs={{0,2},{1,3},{2,0},{3,1},{4,6},{5,7},{6,4},{7,5},{8,10},{9,11},{10,... | collective-permute-start | bytes 24584 | tf_op jit(solution)/shard_map/ppermute | solution.py:18
  23.6 1.3 fusion.31
  25.4 3.7 %multiply_select_fusion = f32[2048,512]{1,0:T(8,128)} fusion(f32[2048,512]{1,0:T(8,128)S(1)} %fusion.31, bf16[2048,512]{1,0:T(8,128)(2,1)S(1)} %copy-done.11, bf16[512,512]{1,0:T(8,128)(2,1)S(1)} %copy-done.5, pred[2048]{0:T(1024)(128)(4,1)S(1)} %lt.105), kind=kOutput, calls=%fused_computation.8 | convolution fusion | flops 1083179008 | bytes 11012096 | tf_op jit(solution)/shard_map/dot_general | solution.py:81
  29.1 25.2 %collective-permute-done = bf16[8,512]{1,0:T(8,128)(2,1)S(1)} collective-permute-done((bf16[8,512]{1,0:T(8,128)(2,1)S(1)}, bf16[8,512]{1,0:T(8,128)(2,1)S(1)}, u32[]{:S(2)}, u32[]{:S(2)}) %collective-permute-start) | collective-permute-done | bytes 8224 | tf_op jit(solution)/shard_map/ppermute | solution.py:18
  54.3 14.4 %collective-permute-done.1 = bf16[8,512]{1,0:T(8,128)(2,1)S(1)} collective-permute-done((bf16[8,512]{1,0:T(8,128)(2,1)S(1)}, bf16[8,512]{1,0:T(8,128)(2,1)S(1)}, u32[]{:S(2)}, u32[]{:S(2)}) %collective-permute-start.1) | collective-permute-done | bytes 8224 | tf_op jit(solution)/shard_map/ppermute | solution.py:18
  69.3 1.2 collective-permute-start.4
  72.1 2.4 %collective-permute-done.5 = bf16[4,8,512]{2,1,0:T(8,128)(2,1)S(1)} collective-permute-done((bf16[4,8,512]{2,1,0:T(8,128)(2,1)S(1)}, bf16[4,8,512]{2,1,0:T(8,128)(2,1)S(1)}, u32[]{:S(2)}, u32[]{:S(2)}) %collective-permute-start.5) | collective-permute-done | bytes 32800 | tf_op jit(solution)/shard_map/ppermute | solution.py:13
  74.5 2.6 %collective-permute-start.6 = (bf16[4,4,8,512]{3,2,1,0:T(8,128)(2,1)S(1)}, bf16[4,4,8,512]{3,2,1,0:T(8,128)(2,1)S(1)}, u32[]{:S(2)}, u32[]{:S(2)}) collective-permute-start(bf16[4,4,8,512]{3,2,1,0:T(8,128)(2,1)S(1)} %bitcast_dynamic-update-slice_fusion.8), channel_id=1, source_target_pairs={{0,4},{4,0},{8,12},{12,8},{16,20},{20,16},{24,28},{28,24},{1,5},{5... | collective-permute-start | bytes 393224 | tf_op jit(solution)/shard_map/ppermute | solution.py:13
  78.2 9.2 %gather_fusion.1 = bf16[2048,512]{1,0:T(8,128)(2,1)} fusion(bf16[256,512]{1,0:T(8,128)(2,1)S(1)} %bitcast.99, s32[2048]{0:T(1024)S(1)} %get-tuple-element.14), kind=kCustom, calls=%fused_computation.1 | custom fusion | bytes 4202496 | tf_op jit(solution)/shard_map/jit(_take)/gather | solution.py:79
  87.4 4.3 %fusion.3 = bf16[2048,512]{1,0:T(8,128)(2,1)S(1)} fusion(f32[2048,512]{1,0:T(8,128)} %multiply_select_fusion, bf16[2048,512]{1,0:T(8,128)(2,1)} %gather_fusion.1, bf16[32,64,512]{2,1,0:T(8,128)(2,1)} %all-to-all-done), kind=kLoop, calls=%fused_computation.7 | loop fusion | flops 5242880 | bytes 10485760 | tf_op jit(solution)/shard_map/convert_element_type | solution.py:92
  91.7 1.3 fusion.32
  94.1 1.3 fusion.33
  96.4 1.5 copy-done.1
  99.5 3.4 %all-to-all-start.1 = ((bf16[32,64,512]{2,1,0:T(8,128)(2,1)}), bf16[32,64,512]{2,1,0:T(8,128)(2,1)}, u32[]{:S(2)}, u32[]{:S(2)}) async-start(bf16[32,64,512]{2,1,0:T(8,128)(2,1)} %bitcast.101), calls=%async_computation.1 | async-start | bytes 4194304 | tf_op jit(solution)/shard_map/all_to_all | solution.py:94
  102.9 1.6 fusion.28
  104.6 2.2 %collective-permute-start.10 = (bf16[4,40,512]{2,1,0:T(8,128)(2,1)S(1)}, bf16[4,40,512]{2,1,0:T(8,128)(2,1)S(1)}, u32[]{:S(2)}, u32[]{:S(2)}) collective-permute-start(bf16[4,40,512]{2,1,0:T(8,128)(2,1)S(1)} %get-tuple-element.21), channel_id=1, source_target_pairs={{0,24},{4,28},{8,16},{12,20},{16,8},{20,12},{24,0},{28,4},{1,25},{... | collective-permute-start | bytes 491528 | tf_op jit(solution)/shard_map/ppermute | solution.py:13
  107.3 18.7 %collective-permute-done.10 = bf16[4,40,512]{2,1,0:T(8,128)(2,1)S(1)} collective-permute-done((bf16[4,40,512]{2,1,0:T(8,128)(2,1)S(1)}, bf16[4,40,512]{2,1,0:T(8,128)(2,1)S(1)}, u32[]{:S(2)}, u32[]{:S(2)}) %collective-permute-start.10) | collective-permute-done | bytes 163872 | tf_op jit(solution)/shard_map/ppermute | solution.py:13
  126.0 5.0 %collective-permute-done.8 = bf16[4,40,512]{2,1,0:T(8,128)(2,1)S(1)} collective-permute-done((bf16[4,40,512]{2,1,0:T(8,128)(2,1)S(1)}, bf16[4,40,512]{2,1,0:T(8,128)(2,1)S(1)}, u32[]{:S(2)}, u32[]{:S(2)}) %collective-permute-start.8) | collective-permute-done | bytes 163872 | tf_op jit(solution)/shard_map/ppermute | solution.py:13
  131.2 4.1 %collective-permute-start.12 = (bf16[40,512]{1,0:T(8,128)(2,1)S(1)}, bf16[40,512]{1,0:T(8,128)(2,1)S(1)}, u32[]{:S(2)}, u32[]{:S(2)}) collective-permute-start(bf16[40,512]{1,0:T(8,128)(2,1)S(1)} %get-tuple-element.27), channel_id=1, source_target_pairs={{0,2},{1,3},{2,0},{3,1},{4,6},{5,7},{6,4},{7,5},{8,10},{9,11},{10,... | collective-permute-start | bytes 122888 | tf_op jit(solution)/shard_map/ppermute | solution.py:18
  135.3 2.6 %collective-permute-done.11 = bf16[40,512]{1,0:T(8,128)(2,1)S(1)} collective-permute-done((bf16[40,512]{1,0:T(8,128)(2,1)S(1)}, bf16[40,512]{1,0:T(8,128)(2,1)S(1)}, u32[]{:S(2)}, u32[]{:S(2)}) %collective-permute-start.11) | collective-permute-done | bytes 40992 | tf_op jit(solution)/shard_map/ppermute | solution.py:18
  137.9 16.0 %collective-permute-done.12 = bf16[40,512]{1,0:T(8,128)(2,1)S(1)} collective-permute-done((bf16[40,512]{1,0:T(8,128)(2,1)S(1)}, bf16[40,512]{1,0:T(8,128)(2,1)S(1)}, u32[]{:S(2)}, u32[]{:S(2)}) %collective-permute-start.12) | collective-permute-done | bytes 40992 | tf_op jit(solution)/shard_map/ppermute | solution.py:18
  153.9 1.2 collective-permute-start.14
  155.1 2.4 %collective-permute-start.16 = (bf16[32,512]{1,0:T(8,128)(2,1)S(1)}, bf16[32,512]{1,0:T(8,128)(2,1)S(1)}, u32[]{:S(2)}, u32[]{:S(2)}) collective-permute-start(bf16[32,512]{1,0:T(8,128)(2,1)S(1)} %get-tuple-element.9), channel_id=1, source_target_pairs={{0,3},{1,2},{2,1},{3,0},{4,7},{5,6},{6,5},{7,4},{8,11},{9,10},{10,... | collective-permute-start | bytes 98312 | tf_op jit(solution)/shard_map/ppermute | solution.py:18
  157.5 1.6 collective-permute-done.15
  160.5 1.2 collective-permute-start.18
  164.3 2.1 %collective-permute-done.19 = bf16[4,32,512]{2,1,0:T(8,128)(2,1)S(1)} collective-permute-done((bf16[4,32,512]{2,1,0:T(8,128)(2,1)S(1)}, bf16[4,32,512]{2,1,0:T(8,128)(2,1)S(1)}, u32[]{:S(2)}, u32[]{:S(2)}) %collective-permute-start.19) | collective-permute-done | bytes 131104 | tf_op jit(solution)/shard_map/ppermute | solution.py:13
  166.4 5.0 %collective-permute-start.20 = (bf16[4,4,32,512]{3,2,1,0:T(8,128)(2,1)S(1)}, bf16[4,4,32,512]{3,2,1,0:T(8,128)(2,1)S(1)}, u32[]{:S(2)}, u32[]{:S(2)}) collective-permute-start(bf16[4,4,32,512]{3,2,1,0:T(8,128)(2,1)S(1)} %bitcast_dynamic-update-slice_fusion), channel_id=1, source_target_pairs={{0,4},{4,0},{8,12},{12,8},{16,20},{20,16},{24,28},{28,24},{1,5},{5... | collective-permute-start | bytes 1572872 | tf_op jit(solution)/shard_map/ppermute | solution.py:13
  173.4 1.6 fusion.30
  175.0 9.2 %fusion.6 = f32[2048,512]{1,0:T(8,128)} fusion(bf16[512,512]{1,0:T(8,128)(2,1)S(1)} %copy-done.4, bf16[2048,512]{1,0:T(8,128)(2,1)} %bitcast.15, s32[2048]{0:T(1024)S(1)} %copy-done.9), kind=kOutput, calls=%fused_computation.16 | convolution fusion | flops 5373952000 | bytes 6823936 | tf_op jit(solution)/shard_map/dot_general | solution.py:132
  (86 shorter events, 15.0 us)
Async XLA Ops:
  0.6 23.0 %copy-start = (bf16[2048,512]{1,0:T(8,128)(2,1)S(1)}, bf16[2048,512]{1,0:T(8,128)(2,1)}, u32[]{:S(2)}) copy-start(bf16[2048,512]{1,0:T(8,128)(2,1)} %param.9) | copy-start | bytes 6291460
  12.6 7.2 %copy-start.8 = (bf16[8,512]{1,0:T(8,128)(2,1)S(1)}, bf16[8,512]{1,0:T(8,128)(2,1)}, u32[]{:S(2)}) copy-start(bf16[8,512]{1,0:T(8,128)(2,1)} %param.15) | copy-start | bytes 24580
  12.6 10.8 %copy-start.10 = (s32[1,32]{1,0:T(1,128)S(1)}, s32[1,32]{1,0:T(1,128)}, u32[]{:S(2)}) copy-start(s32[1,32]{1,0:T(1,128)} %param.11) | copy-start | bytes 388
  12.6 11.0 %copy-start.3 = (bf16[512,512]{1,0:T(8,128)(2,1)S(1)}, bf16[512,512]{1,0:T(8,128)(2,1)}, u32[]{:S(2)}) copy-start(bf16[512,512]{1,0:T(8,128)(2,1)} %param.16) | copy-start | bytes 1572868
  12.6 74.8 %all-to-all-start = ((bf16[32,64,512]{2,1,0:T(8,128)(2,1)}), bf16[32,64,512]{2,1,0:T(8,128)(2,1)}, u32[]{:S(2)}, u32[]{:S(2)}) async-start(bf16[32,64,512]{2,1,0:T(8,128)(2,1)} %bitcast.100), calls=%async_computation | async-start | bytes 4194304 | tf_op jit(solution)/shard_map/all_to_all | solution.py:71
  19.8 34.5 %collective-permute-start = (bf16[8,512]{1,0:T(8,128)(2,1)S(1)}, bf16[8,512]{1,0:T(8,128)(2,1)S(1)}, u32[]{:S(2)}, u32[]{:S(2)}) collective-permute-start(bf16[8,512]{1,0:T(8,128)(2,1)S(1)} %copy-done.8), channel_id=1, source_target_pairs={{0,1},{1,0},{2,3},{3,2},{4,5},{5,4},{6,7},{7,6},{8,9},{9,8},{10,11... | collective-permute-start | bytes 24584 | tf_op jit(solution)/shard_map/ppermute | solution.py:18
  21.3 47.5 %collective-permute-start.1 = (bf16[8,512]{1,0:T(8,128)(2,1)S(1)}, bf16[8,512]{1,0:T(8,128)(2,1)S(1)}, u32[]{:S(2)}, u32[]{:S(2)}) collective-permute-start(bf16[8,512]{1,0:T(8,128)(2,1)S(1)} %copy-done.8), channel_id=1, source_target_pairs={{0,2},{1,3},{2,0},{3,1},{4,6},{5,7},{6,4},{7,5},{8,10},{9,11},{10,... | collective-permute-start | bytes 24584 | tf_op jit(solution)/shard_map/ppermute | solution.py:18
  23.4 45.4 %collective-permute-start.2 = (bf16[8,512]{1,0:T(8,128)(2,1)S(1)}, bf16[8,512]{1,0:T(8,128)(2,1)S(1)}, u32[]{:S(2)}, u32[]{:S(2)}) collective-permute-start(bf16[8,512]{1,0:T(8,128)(2,1)S(1)} %copy-done.8), channel_id=1, source_target_pairs={{0,3},{1,2},{2,1},{3,0},{4,7},{5,6},{6,5},{7,4},{8,11},{9,10},{10,... | collective-permute-start | bytes 24584 | tf_op jit(solution)/shard_map/ppermute | solution.py:18
  23.6 1.8 copy-start.11
  25.4 51.8 %copy-start.7 = (s32[2048]{0:T(1024)S(1)}, s32[2048]{0:T(1024)}, u32[]{:S(2)}) copy-start(s32[2048]{0:T(1024)} %param.13) | copy-start | bytes 24580
  68.8 2.8 %collective-permute-start.3 = (bf16[4,8,512]{2,1,0:T(8,128)(2,1)S(1)}, bf16[4,8,512]{2,1,0:T(8,128)(2,1)S(1)}, u32[]{:S(2)}, u32[]{:S(2)}) collective-permute-start(bf16[4,8,512]{2,1,0:T(8,128)(2,1)S(1)} %bitcast_dynamic-update-slice_fusion.12), channel_id=1, source_target_pairs={{0,8},{4,12},{8,0},{12,4},{16,24},{20,28},{24,16},{28,20},{1,9},{5... | collective-permute-start | bytes 98312 | tf_op jit(solution)/shard_map/ppermute | solution.py:13
  69.3 2.8 %collective-permute-start.4 = (bf16[4,8,512]{2,1,0:T(8,128)(2,1)S(1)}, bf16[4,8,512]{2,1,0:T(8,128)(2,1)S(1)}, u32[]{:S(2)}, u32[]{:S(2)}) collective-permute-start(bf16[4,8,512]{2,1,0:T(8,128)(2,1)S(1)} %bitcast_dynamic-update-slice_fusion.12), channel_id=1, source_target_pairs={{0,16},{4,20},{8,24},{12,28},{16,0},{20,4},{24,8},{28,12},{1,17},{... | collective-permute-start | bytes 98312 | tf_op jit(solution)/shard_map/ppermute | solution.py:13
  70.5 4.0 %collective-permute-start.5 = (bf16[4,8,512]{2,1,0:T(8,128)(2,1)S(1)}, bf16[4,8,512]{2,1,0:T(8,128)(2,1)S(1)}, u32[]{:S(2)}, u32[]{:S(2)}) collective-permute-start(bf16[4,8,512]{2,1,0:T(8,128)(2,1)S(1)} %bitcast_dynamic-update-slice_fusion.12), channel_id=1, source_target_pairs={{0,24},{4,28},{8,16},{12,20},{16,8},{20,12},{24,0},{28,4},{1,25},{... | collective-permute-start | bytes 98312 | tf_op jit(solution)/shard_map/ppermute | solution.py:13
  74.5 3.6 %collective-permute-start.6 = (bf16[4,4,8,512]{3,2,1,0:T(8,128)(2,1)S(1)}, bf16[4,4,8,512]{3,2,1,0:T(8,128)(2,1)S(1)}, u32[]{:S(2)}, u32[]{:S(2)}) collective-permute-start(bf16[4,4,8,512]{3,2,1,0:T(8,128)(2,1)S(1)} %bitcast_dynamic-update-slice_fusion.8), channel_id=1, source_target_pairs={{0,4},{4,0},{8,12},{12,8},{16,20},{20,16},{24,28},{28,24},{1,5},{5... | collective-permute-start | bytes 393224 | tf_op jit(solution)/shard_map/ppermute | solution.py:13
  91.7 3.7 %copy-start.2 = (bf16[2048,512]{1,0:T(8,128)(2,1)}, bf16[2048,512]{1,0:T(8,128)(2,1)S(1)}, u32[]{:S(2)}) copy-start(bf16[2048,512]{1,0:T(8,128)(2,1)S(1)} %fusion.3) | copy-start | bytes 6291460
  91.7 2.4 %copy-start.12 = (bf16[2048,512]{1,0:T(8,128)(2,1)S(1)}, bf16[2048,512]{1,0:T(8,128)(2,1)}, u32[]{:S(2)}) copy-start(bf16[2048,512]{1,0:T(8,128)(2,1)} %param.10) | copy-start | bytes 6291460
  99.1 3.8 %collective-permute-start.7 = (f32[4,4,40,512]{3,2,1,0:T(8,128)}, f32[4,4,40,512]{3,2,1,0:T(8,128)S(1)}, u32[]{:S(2)}, u32[]{:S(2)}) collective-permute-start(f32[4,4,40,512]{3,2,1,0:T(8,128)} %dynamic-slice_bitcast_fusion), channel_id=1, source_target_pairs={{0,4},{4,0},{8,12},{12,8},{16,20},{20,16},{24,28},{28,24},{1,5},{5... | collective-permute-start | bytes 3932168 | tf_op jit(solution)/shard_map/ppermute | solution.py:13
  99.5 75.5 %all-to-all-start.1 = ((bf16[32,64,512]{2,1,0:T(8,128)(2,1)}), bf16[32,64,512]{2,1,0:T(8,128)(2,1)}, u32[]{:S(2)}, u32[]{:S(2)}) async-start(bf16[32,64,512]{2,1,0:T(8,128)(2,1)} %bitcast.101), calls=%async_computation.1 | async-start | bytes 4194304 | tf_op jit(solution)/shard_map/all_to_all | solution.py:94
  104.6 66.9 %copy-start.6 = (bf16[512,512]{1,0:T(8,128)(2,1)S(1)}, bf16[512,512]{1,0:T(8,128)(2,1)}, u32[]{:S(2)}) copy-start(bf16[512,512]{1,0:T(8,128)(2,1)} %param.17) | copy-start | bytes 1572868
  104.6 21.4 %collective-permute-start.10 = (bf16[4,40,512]{2,1,0:T(8,128)(2,1)S(1)}, bf16[4,40,512]{2,1,0:T(8,128)(2,1)S(1)}, u32[]{:S(2)}, u32[]{:S(2)}) collective-permute-start(bf16[4,40,512]{2,1,0:T(8,128)(2,1)S(1)} %get-tuple-element.21), channel_id=1, source_target_pairs={{0,24},{4,28},{8,16},{12,20},{16,8},{20,12},{24,0},{28,4},{1,25},{... | collective-permute-start | bytes 491528 | tf_op jit(solution)/shard_map/ppermute | solution.py:13
  106.8 24.2 %collective-permute-start.8 = (bf16[4,40,512]{2,1,0:T(8,128)(2,1)S(1)}, bf16[4,40,512]{2,1,0:T(8,128)(2,1)S(1)}, u32[]{:S(2)}, u32[]{:S(2)}) collective-permute-start(bf16[4,40,512]{2,1,0:T(8,128)(2,1)S(1)} %get-tuple-element.20), channel_id=1, source_target_pairs={{0,8},{4,12},{8,0},{12,4},{16,24},{20,28},{24,16},{28,20},{1,9},{5... | collective-permute-start | bytes 491528 | tf_op jit(solution)/shard_map/ppermute | solution.py:13
  107.0 23.9 %collective-permute-start.9 = (bf16[4,40,512]{2,1,0:T(8,128)(2,1)S(1)}, bf16[4,40,512]{2,1,0:T(8,128)(2,1)S(1)}, u32[]{:S(2)}, u32[]{:S(2)}) collective-permute-start(bf16[4,40,512]{2,1,0:T(8,128)(2,1)S(1)} %get-tuple-element.22), channel_id=1, source_target_pairs={{0,16},{4,20},{8,24},{12,28},{16,0},{20,4},{24,8},{28,12},{1,17},{... | collective-permute-start | bytes 491528 | tf_op jit(solution)/shard_map/ppermute | solution.py:13
  131.1 6.8 %collective-permute-start.11 = (bf16[40,512]{1,0:T(8,128)(2,1)S(1)}, bf16[40,512]{1,0:T(8,128)(2,1)S(1)}, u32[]{:S(2)}, u32[]{:S(2)}) collective-permute-start(bf16[40,512]{1,0:T(8,128)(2,1)S(1)} %get-tuple-element.25), channel_id=1, source_target_pairs={{0,1},{1,0},{2,3},{3,2},{4,5},{5,4},{6,7},{7,6},{8,9},{9,8},{10,11... | collective-permute-start | bytes 122888 | tf_op jit(solution)/shard_map/ppermute | solution.py:18
  131.2 22.7 %collective-permute-start.12 = (bf16[40,512]{1,0:T(8,128)(2,1)S(1)}, bf16[40,512]{1,0:T(8,128)(2,1)S(1)}, u32[]{:S(2)}, u32[]{:S(2)}) collective-permute-start(bf16[40,512]{1,0:T(8,128)(2,1)S(1)} %get-tuple-element.27), channel_id=1, source_target_pairs={{0,2},{1,3},{2,0},{3,1},{4,6},{5,7},{6,4},{7,5},{8,10},{9,11},{10,... | collective-permute-start | bytes 122888 | tf_op jit(solution)/shard_map/ppermute | solution.py:18
  135.3 18.5 %collective-permute-start.13 = (bf16[40,512]{1,0:T(8,128)(2,1)S(1)}, bf16[40,512]{1,0:T(8,128)(2,1)S(1)}, u32[]{:S(2)}, u32[]{:S(2)}) collective-permute-start(bf16[40,512]{1,0:T(8,128)(2,1)S(1)} %get-tuple-element.26), channel_id=1, source_target_pairs={{0,3},{1,2},{2,1},{3,0},{4,7},{5,6},{6,5},{7,4},{8,11},{9,10},{10,... | collective-permute-start | bytes 122888 | tf_op jit(solution)/shard_map/ppermute | solution.py:18
  153.9 3.6 %collective-permute-start.14 = (bf16[32,512]{1,0:T(8,128)(2,1)S(1)}, bf16[32,512]{1,0:T(8,128)(2,1)S(1)}, u32[]{:S(2)}, u32[]{:S(2)}) collective-permute-start(bf16[32,512]{1,0:T(8,128)(2,1)S(1)} %get-tuple-element.9), channel_id=1, source_target_pairs={{0,1},{1,0},{2,3},{3,2},{4,5},{5,4},{6,7},{7,6},{8,9},{9,8},{10,11... | collective-permute-start | bytes 98312 | tf_op jit(solution)/shard_map/ppermute | solution.py:18
  155.1 4.0 %collective-permute-start.15 = (bf16[32,512]{1,0:T(8,128)(2,1)S(1)}, bf16[32,512]{1,0:T(8,128)(2,1)S(1)}, u32[]{:S(2)}, u32[]{:S(2)}) collective-permute-start(bf16[32,512]{1,0:T(8,128)(2,1)S(1)} %get-tuple-element.9), channel_id=1, source_target_pairs={{0,2},{1,3},{2,0},{3,1},{4,6},{5,7},{6,4},{7,5},{8,10},{9,11},{10,... | collective-permute-start | bytes 98312 | tf_op jit(solution)/shard_map/ppermute | solution.py:18
  155.1 4.6 %collective-permute-start.16 = (bf16[32,512]{1,0:T(8,128)(2,1)S(1)}, bf16[32,512]{1,0:T(8,128)(2,1)S(1)}, u32[]{:S(2)}, u32[]{:S(2)}) collective-permute-start(bf16[32,512]{1,0:T(8,128)(2,1)S(1)} %get-tuple-element.9), channel_id=1, source_target_pairs={{0,3},{1,2},{2,1},{3,0},{4,7},{5,6},{6,5},{7,4},{8,11},{9,10},{10,... | collective-permute-start | bytes 98312 | tf_op jit(solution)/shard_map/ppermute | solution.py:18
  159.8 3.8 %collective-permute-start.17 = (bf16[4,32,512]{2,1,0:T(8,128)(2,1)S(1)}, bf16[4,32,512]{2,1,0:T(8,128)(2,1)S(1)}, u32[]{:S(2)}, u32[]{:S(2)}) collective-permute-start(bf16[4,32,512]{2,1,0:T(8,128)(2,1)S(1)} %bitcast_dynamic-update-slice_fusion.4), channel_id=1, source_target_pairs={{0,8},{4,12},{8,0},{12,4},{16,24},{20,28},{24,16},{28,20},{1,9},{5... | collective-permute-start | bytes 393224 | tf_op jit(solution)/shard_map/ppermute | solution.py:13
  160.5 3.8 %collective-permute-start.18 = (bf16[4,32,512]{2,1,0:T(8,128)(2,1)S(1)}, bf16[4,32,512]{2,1,0:T(8,128)(2,1)S(1)}, u32[]{:S(2)}, u32[]{:S(2)}) collective-permute-start(bf16[4,32,512]{2,1,0:T(8,128)(2,1)S(1)} %bitcast_dynamic-update-slice_fusion.4), channel_id=1, source_target_pairs={{0,16},{4,20},{8,24},{12,28},{16,0},{20,4},{24,8},{28,12},{1,17},{... | collective-permute-start | bytes 393224 | tf_op jit(solution)/shard_map/ppermute | solution.py:13
  161.7 4.7 %collective-permute-start.19 = (bf16[4,32,512]{2,1,0:T(8,128)(2,1)S(1)}, bf16[4,32,512]{2,1,0:T(8,128)(2,1)S(1)}, u32[]{:S(2)}, u32[]{:S(2)}) collective-permute-start(bf16[4,32,512]{2,1,0:T(8,128)(2,1)S(1)} %bitcast_dynamic-update-slice_fusion.4), channel_id=1, source_target_pairs={{0,24},{4,28},{8,16},{12,20},{16,8},{20,12},{24,0},{28,4},{1,25},{... | collective-permute-start | bytes 393224 | tf_op jit(solution)/shard_map/ppermute | solution.py:13
  166.4 6.6 %collective-permute-start.20 = (bf16[4,4,32,512]{3,2,1,0:T(8,128)(2,1)S(1)}, bf16[4,4,32,512]{3,2,1,0:T(8,128)(2,1)S(1)}, u32[]{:S(2)}, u32[]{:S(2)}) collective-permute-start(bf16[4,4,32,512]{3,2,1,0:T(8,128)(2,1)S(1)} %bitcast_dynamic-update-slice_fusion), channel_id=1, source_target_pairs={{0,4},{4,0},{8,12},{12,8},{16,20},{20,16},{24,28},{28,24},{1,5},{5... | collective-permute-start | bytes 1572872 | tf_op jit(solution)/shard_map/ppermute | solution.py:13
  (4 other events, 6.0 us)

commit v2 on v1

--- a/solution.py
+++ b/solution.py
@@ -3,6 +3,8 @@
 import jax
 import jax.numpy as jnp
 from jax import lax
+from jax.experimental import pallas as pl
+from jax.experimental.pallas import tpu as pltpu
 from jax.sharding import PartitionSpec as P
 
 AXES = ("rows", "grp")
@@ -16,6 +18,42 @@
 def shift_grp(value, mask):
     size = lax.axis_size("grp")
     return lax.ppermute(value, "grp", [(i, i ^ mask) for i in range(size)])
+
+
+def pick_kernel(key_ref, table_ref, out_ref):
+    tile, length = key_ref.shape[1], table_ref.shape[0]
+    keys = jnp.transpose(jnp.broadcast_to(key_ref[...], (128, tile)))
+    lane = lax.broadcasted_iota(jnp.int32, (tile, 128), 1)
+    one, zero = jnp.bfloat16(1), jnp.bfloat16(0)
+    hot = jnp.concatenate(
+        [jnp.where(keys == lane + at, one, zero) for at in range(0, length, 128)], axis=1
+    )
+    out_ref[...] = jnp.dot(hot, table_ref[...], preferred_element_type=jnp.float32).astype(
+        jnp.bfloat16
+    )
+
+
+def pick(table, keys, tile=512):
+    length, width = table.shape
+    count = keys.shape[0]
+    tile = min(tile, count)
+    return pl.pallas_call(
+        pick_kernel,
+        grid=(count // tile,),
+        out_shape=jax.ShapeDtypeStruct((count, width), jnp.bfloat16),
+        in_specs=[
+            pl.BlockSpec((1, tile), lambda i: (0, i)),
+            pl.BlockSpec((length, width), lambda i: (0, 0)),
+        ],
+        out_specs=pl.BlockSpec((tile, width), lambda i: (i, 0)),
+        compiler_params=pltpu.CompilerParams(vmem_limit_bytes=32 << 20),
+        cost_estimate=pl.CostEstimate(
+            flops=2 * count * length * width,
+            bytes_accessed=2 * (length + count) * width,
+            transcendentals=0,
+        ),
+        name="pick_rows",
+    )(keys.reshape(1, count), table)
 
 
 def place():
@@ -31,11 +69,13 @@
     return stacked
 
 
-def gather_all(mine):
+def gather_grp(mine):
+    return spread(mine, shift_grp, lax.axis_size("grp"), 1, lax.axis_index("grp"))
+
+
+def gather_rows(own):
     core, plane, grp = place()
-    planes = lax.axis_size("rows") // 2
-    own = spread(mine, shift_grp, lax.axis_size("grp"), 1, grp)
-    own = spread(own, shift_rows, planes, 2, plane)
+    own = spread(own, shift_rows, lax.axis_size("rows") // 2, 2, plane)
     other = shift_rows(own, 1)
     first = core == 0
     return jnp.stack([jnp.where(first, own, other), jnp.where(first, other, own)])
@@ -67,7 +107,9 @@
     product_count = prod_grad.shape[0]
     grid = (2, planes, grps)
 
-    owned_rows = jnp.take(cust_grad, recv_key, axis=0, mode="clip")
+    products = gather_grp(prod_grad)
+    owned_rows = pick(cust_grad, recv_key)
+    owned_rows, products = lax.optimization_barrier((owned_rows, products))
     fetched = lax.all_to_all(
         owned_rows.reshape(devices, capacity, width), AXES, split_axis=0, concat_axis=0, tiled=True
     ).reshape(slot_count, width)
@@ -75,8 +117,8 @@
     owner, low = prod_key // product_count, prod_key % product_count
     row, grp = owner // grps, owner % grps
     prod_at = (((row % 2) * planes + row // 2) * grps + grp) * product_count + low
-    product_table = gather_all(prod_grad).reshape(devices * product_count, width)
-    product_rows = jnp.take(product_table, prod_at, axis=0, mode="clip")
+    product_table = gather_rows(products).reshape(devices * product_count, width)
+    product_rows = pick(product_table, prod_at)
 
     preact = jnp.dot(hc_edge, w_cust, preferred_element_type=jnp.float32) + jnp.dot(
         hp_edge, w_prod, preferred_element_type=jnp.float32
@@ -95,6 +137,8 @@
         delta.reshape(devices, capacity, width), AXES, split_axis=0, concat_axis=0, tiled=True
     ).reshape(slot_count, width)
 
+    edge = shift_rows(delta[:16], 1)
+    delta, edge = lax.optimization_barrier((delta, edge))
     wanted = jnp.arange(devices * product_count, dtype=jnp.int32)
     product_hot = (prod_at[None, :] == wanted[:, None]).astype(jnp.bfloat16)
     contract = (((0,), (0,)), ((), ()))
@@ -111,6 +155,7 @@
         axis=3,
     )
     mine = reduce_all(terms)
+    mine, returned = lax.optimization_barrier((mine, returned))
     prod_table_grad = lax.dot_general(
         mine[:product_count],
         w_prod.astype(jnp.float32),
@@ -120,19 +165,28 @@
     ) * math.sqrt(product_count / slot_count)
     grad_scale = 1.0 / math.sqrt(slot_count * devices)
     share = width // devices
-    weights = gather_all(mine[product_count:].astype(jnp.bfloat16)).astype(jnp.float32) * grad_scale
-    cust_weight = weights[..., :share, :].reshape(width, width)
-    prod_weight = weights[..., share:, :].reshape(width, width)
-
-    owned_count = cust_grad.shape[0]
-    one_hot = (recv_key[None, :] == jnp.arange(owned_count, dtype=jnp.int32)[:, None]).astype(
-        jnp.bfloat16
-    )
+    own = gather_grp(mine[product_count:].astype(jnp.bfloat16))
+    wanted = jnp.arange(cust_grad.shape[0], dtype=jnp.int32)
+    one_hot = (recv_key[None, :] == wanted[:, None]).astype(jnp.bfloat16)
     cust_sum = jnp.dot(one_hot, returned, preferred_element_type=jnp.float32).astype(jnp.bfloat16)
+    own, cust_sum = lax.optimization_barrier((own, cust_sum))
+    own = spread(own, shift_rows, planes, 2, lax.axis_index("rows") // 2)
     cust_table_grad = lax.dot_general(
         cust_sum, w_cust, (((1,), (1,)), ((), ())), preferred_element_type=jnp.float32
     )
-    return cust_table_grad, prod_table_grad, cust_weight, prod_weight
+    own, prod_table_grad, cust_table_grad = lax.optimization_barrier(
+        (own, prod_table_grad, cust_table_grad)
+    )
+    other = shift_rows(own, 1)
+
+    def whole(share_at):
+        pick_share = slice(share_at, share_at + share)
+        mine_part, other_part = own[:, :, pick_share], other[:, :, pick_share]
+        first = lax.axis_index("rows") % 2 == 0
+        both = [jnp.where(first, mine_part, other_part), jnp.where(first, other_part, mine_part)]
+        return jnp.stack(both).astype(jnp.float32).reshape(width, width) * grad_scale
+
+    return cust_table_grad, prod_table_grad, whole(0), whole(share)
 
 
 def solution(mesh):

time: 185 us -> 156 us (0.84)
  waiting for transfers between devices: 92.3 us -> 67.1 us
  local copies, waits for them, and re-layouts: 26.5 us -> 8.85 us
  Pallas kernels: 0 us -> 6.64 us
  starting transfers between devices: 38.1 us -> 40.4 us
  other arithmetic: 7.75 us -> 9.97 us
  matrix products: 18.6 us -> 20.8 us
    ppermute x9, waiting for transfers between devices: 60.4 us -> 13.8 us  [shift_grp(): return lax.ppermute(value, 'grp', [(i, i ^ mask) for i in range(size)])]
    all_to_all x1, waiting for transfers between devices: 0.01 us -> 26.1 us  [body(): lax.all_to_all(owned_rows.reshape(devices, capacity, width), AXES, split_...]
    gather x2 -> x0, local copies, waits for them, and re-layouts: 20.3 us -> none  [the longest x1 11.1 us: body(): owned_rows = jnp.take(cust_grad, recv_key, axis=0, mode='clip')]
    pallas_call x0 -> x2, Pallas kernels: none -> 6.64 us  [pick(): pl.pallas_call(pick_kernel, grid=(count // tile,), out_shape=jax.ShapeDty...]
    dot_general x0 -> x1, matrix products: none -> 6.27 us  [body(): jnp.dot(one_hot, returned, preferred_element_type=jnp.float32)]
    dot_general x1, matrix products: 9.21 us -> 3.36 us  [body(): lax.dot_general(cust_sum, w_cust, (((1,), (1,)), ((), ())), preferred_ele...]
    ppermute x12, waiting for transfers between devices: 31.9 us -> 27.2 us  [shift_rows(): return lax.ppermute(value, 'rows', [(i, i ^ mask) for i in range(size)])]
    unnamed x26 -> x30, local copies, waits for them, and re-layouts: 3.05 us -> 7.27 us
  transfers between devices with their start and end apart: 23 -> 23, of which waited for: 16 -> 10; matrix products, arithmetic and copies ran while one was open for 11% -> 16% of each run, Pallas kernels for 0% -> 4%
where the time goes in v2:
time: 156 us; the launch traced here: 155 us
  waiting for transfers between devices  67.1 us (43%)
  starting transfers between devices  40.4 us (26%)
  matrix products  20.8 us (13%)
  other arithmetic  9.97 us (6%)
  local copies, waits for them, and re-layouts  8.85 us (6%)
  Pallas kernels  6.64 us (4%)
    ppermute x12, waiting for transfers between devices, shift_rows(): return lax.ppermute(value, 'rows', [(i, i ^ mask) for i in range(size)])  27.2 us
    all_to_all x1, waiting for transfers between devices, body(): lax.all_to_all(owned_rows.reshape(devices, capacity, width), AXES, split_...  26.1 us
    ppermute x9, starting transfers between devices, shift_grp(): return lax.ppermute(value, 'grp', [(i, i ^ mask) for i in range(size)])  15.3 us
    ppermute x12, starting transfers between devices, shift_rows(): return lax.ppermute(value, 'rows', [(i, i ^ mask) for i in range(size)])  14.5 us
    ppermute x9, waiting for transfers between devices, shift_grp(): return lax.ppermute(value, 'grp', [(i, i ^ mask) for i in range(size)])  13.8 us
    unnamed x30, local copies, waits for them, and re-layouts  7.27 us
    all_to_all x1, starting transfers between devices, body(): lax.all_to_all(owned_rows.reshape(devices, capacity, width), AXES, split_...  7.1 us
    pallas_call x2, Pallas kernels, pick(): pl.pallas_call(pick_kernel, grid=(count // tile,), out_shape=jax.ShapeDty...  6.64 us
  transfers between devices with their start and end apart: 23, of which 10 were waited for; matrix products, arithmetic and copies ran while one was open for 16% of the time, Pallas kernels for 4%

profile of v2, /device:TPU:1, one launch (start us, length us, event | category | flops | bytes accessed | tf_op | source)
XLA Modules:
  0.0 154.8 jit_solution(1955052031730814653)
XLA Ops:
  0.6 2.2 %collective-permute-start = (bf16[8,512]{1,0:T(8,128)(2,1)}, bf16[8,512]{1,0:T(8,128)(2,1)S(1)}, u32[]{:S(2)}, u32[]{:S(2)}) collective-permute-start(bf16[8,512]{1,0:T(8,128)(2,1)} %param.15), channel_id=1, source_target_pairs={{0,1},{1,0},{2,3},{3,2},{4,5},{5,4},{6,7},{7,6},{8,9},{9,8},{10,11... | collective-permute-start | bytes 24584 | tf_op jit(solution)/shard_map/ppermute | solution.py:20
  2.8 2.3 %collective-permute-start.1 = (bf16[8,512]{1,0:T(8,128)(2,1)}, bf16[8,512]{1,0:T(8,128)(2,1)S(1)}, u32[]{:S(2)}, u32[]{:S(2)}) collective-permute-start(bf16[8,512]{1,0:T(8,128)(2,1)} %param.15), channel_id=1, source_target_pairs={{0,2},{1,3},{2,0},{3,1},{4,6},{5,7},{6,4},{7,5},{8,10},{9,11},{10,... | collective-permute-start | bytes 24584 | tf_op jit(solution)/shard_map/ppermute | solution.py:20
  5.2 1.6 %copy-done.3 = bf16[2048,512]{1,0:T(8,128)(2,1)S(1)} copy-done((bf16[2048,512]{1,0:T(8,128)(2,1)S(1)}, bf16[2048,512]{1,0:T(8,128)(2,1)}, u32[]{:S(2)}) %copy-start.3) | copy-done | bytes 2097176
  7.4 5.2 %pick_rows.2 = bf16[2048,512]{1,0:T(8,128)(2,1)S(1)} custom-call(s32[1,2048]{1,0:T(1,128)S(1)} %bitcast.109, bf16[2048,512]{1,0:T(8,128)(2,1)S(1)} %copy-done.3), custom_call_target="tpu_custom_call" | custom-call | flops 4294967296 | bytes 4194304 | tf_op jit(solution)/shard_map/pick_rows/pallas_call | solution.py:40
  14.1 7.1 %all-to-all-start = ((bf16[32,64,512]{2,1,0:T(8,128)(2,1)}), bf16[32,64,512]{2,1,0:T(8,128)(2,1)}, u32[]{:S(2)}, u32[]{:S(2)}) async-start(bf16[32,64,512]{2,1,0:T(8,128)(2,1)} %bitcast.106), calls=%async_computation | async-start | bytes 4194304 | tf_op jit(solution)/shard_map/all_to_all | solution.py:113
  23.2 3.7 %multiply_select_fusion = f32[2048,512]{1,0:T(8,128)} fusion(f32[2048,512]{1,0:T(8,128)S(1)} %fusion.28, bf16[2048,512]{1,0:T(8,128)(2,1)S(1)} %copy-done.13, bf16[512,512]{1,0:T(8,128)(2,1)S(1)} %copy-done.9, pred[2048]{0:T(1024)(128)(4,1)S(1)} %lt.114), kind=kOutput, calls=%fused_computation.6 | convolution fusion | flops 1083179008 | bytes 11012096 | tf_op jit(solution)/shard_map/dot_general | solution.py:123
  27.0 1.4 collective-permute-start.3
  29.6 5.8 %collective-permute-done.3 = bf16[4,8,512]{2,1,0:T(8,128)(2,1)S(1)} collective-permute-done((bf16[4,8,512]{2,1,0:T(8,128)(2,1)S(1)}, bf16[4,8,512]{2,1,0:T(8,128)(2,1)S(1)}, u32[]{:S(2)}, u32[]{:S(2)}) %collective-permute-start.3) | collective-permute-done | bytes 32800 | tf_op jit(solution)/shard_map/ppermute | solution.py:15
  35.5 2.6 %collective-permute-done.5 = bf16[4,8,512]{2,1,0:T(8,128)(2,1)S(1)} collective-permute-done((bf16[4,8,512]{2,1,0:T(8,128)(2,1)S(1)}, bf16[4,8,512]{2,1,0:T(8,128)(2,1)S(1)}, u32[]{:S(2)}, u32[]{:S(2)}) %collective-permute-start.5) | collective-permute-done | bytes 32800 | tf_op jit(solution)/shard_map/ppermute | solution.py:15
  38.1 1.5 collective-permute-start.6
  40.7 1.4 pick_rows.3
  42.1 1.4 copy-done.1
  43.5 26.1 %all-to-all-done = bf16[32,64,512]{2,1,0:T(8,128)(2,1)} async-done(((bf16[32,64,512]{2,1,0:T(8,128)(2,1)}), bf16[32,64,512]{2,1,0:T(8,128)(2,1)}, u32[]{:S(2)}, u32[]{:S(2)}) %all-to-all-start) | async-done | bytes 2097184 | tf_op jit(solution)/shard_map/all_to_all | solution.py:113
  69.6 5.7 %fusion.3 = bf16[2048,512]{1,0:T(8,128)(2,1)} fusion(f32[2048,512]{1,0:T(8,128)} %multiply_select_fusion, bf16[2048,512]{1,0:T(8,128)(2,1)} %copy-done.1, bf16[32,64,512]{2,1,0:T(8,128)(2,1)} %all-to-all-done), kind=kLoop, calls=%fused_computation.5 | loop fusion | flops 5242880 | bytes 10485760 | tf_op jit(solution)/shard_map/convert_element_type | solution.py:134
  75.2 3.4 %all-to-all-start.1 = ((bf16[32,64,512]{2,1,0:T(8,128)(2,1)}), bf16[32,64,512]{2,1,0:T(8,128)(2,1)}, u32[]{:S(2)}, u32[]{:S(2)}) async-start(bf16[32,64,512]{2,1,0:T(8,128)(2,1)} %bitcast.110), calls=%async_computation.1 | async-start | bytes 4194304 | tf_op jit(solution)/shard_map/all_to_all | solution.py:136
  78.7 2.4 %fusion.5 = f32[256,512]{1,0:T(8,128)S(1)} fusion(bf16[2048,512]{1,0:T(8,128)(2,1)} %fusion.3, s32[2048]{0:T(1024)S(1)} %fusion.17), kind=kOutput, calls=%fused_computation.10 | convolution fusion | flops 537395200 | bytes 2629632 | tf_op jit(solution)/shard_map/dot_general | solution.py:147
  84.3 1.5 copy-done.6
  87.5 3.0 %collective-permute-done.7 = f32[4,4,40,512]{3,2,1,0:T(8,128)} collective-permute-done((f32[4,4,40,512]{3,2,1,0:T(8,128)}, f32[4,4,40,512]{3,2,1,0:T(8,128)}, u32[]{:S(2)}, u32[]{:S(2)}) %collective-permute-start.7) | collective-permute-done | bytes 1310752 | tf_op jit(solution)/shard_map/ppermute | solution.py:15
  90.5 2.0 %fusion.27 = (bf16[4,4,40,512]{3,2,1,0:T(8,128)(2,1)S(1)}, f32[4,4,40,512]{3,2,1,0:T(8,128)S(1)}) fusion(f32[4,4,40,512]{3,2,1,0:T(8,128)} %collective-permute-done.7, f32[2,4,4,40,512]{4,3,2,1,0:T(8,128)} %copy-done.6, s32[]{:T(128)S(6)} %select_n.155), kind=kLoop, calls=%fused_computation.87 | loop fusion | flops 655360 | bytes 4587524 | tf_op jit(solution)/shard_map/convert_element_type | solution.py:86
  92.6 2.2 %collective-permute-start.10 = (bf16[4,40,512]{2,1,0:T(8,128)(2,1)S(1)}, bf16[4,40,512]{2,1,0:T(8,128)(2,1)S(1)}, u32[]{:S(2)}, u32[]{:S(2)}) collective-permute-start(bf16[4,40,512]{2,1,0:T(8,128)(2,1)S(1)} %get-tuple-element.37), channel_id=1, source_target_pairs={{0,24},{4,28},{8,16},{12,20},{16,8},{20,12},{24,0},{28,4},{1,25},{... | collective-permute-start | bytes 491528 | tf_op jit(solution)/shard_map/ppermute | solution.py:15
  95.6 7.2 %collective-permute-done.10 = bf16[4,40,512]{2,1,0:T(8,128)(2,1)S(1)} collective-permute-done((bf16[4,40,512]{2,1,0:T(8,128)(2,1)S(1)}, bf16[4,40,512]{2,1,0:T(8,128)(2,1)S(1)}, u32[]{:S(2)}, u32[]{:S(2)}) %collective-permute-start.10) | collective-permute-done | bytes 163872 | tf_op jit(solution)/shard_map/ppermute | solution.py:15
  102.8 5.3 %collective-permute-done.8 = bf16[4,40,512]{2,1,0:T(8,128)(2,1)S(1)} collective-permute-done((bf16[4,40,512]{2,1,0:T(8,128)(2,1)S(1)}, bf16[4,40,512]{2,1,0:T(8,128)(2,1)S(1)}, u32[]{:S(2)}, u32[]{:S(2)}) %collective-permute-start.8) | collective-permute-done | bytes 163872 | tf_op jit(solution)/shard_map/ppermute | solution.py:15
  108.6 5.7 %collective-permute-start.12 = (bf16[40,512]{1,0:T(8,128)(2,1)S(1)}, bf16[40,512]{1,0:T(8,128)(2,1)S(1)}, u32[]{:S(2)}, u32[]{:S(2)}) collective-permute-start(bf16[40,512]{1,0:T(8,128)(2,1)S(1)} %get-tuple-element.43), channel_id=1, source_target_pairs={{0,2},{1,3},{2,0},{3,1},{4,6},{5,7},{6,4},{7,5},{8,10},{9,11},{10,... | collective-permute-start | bytes 122888 | tf_op jit(solution)/shard_map/ppermute | solution.py:20
  115.4 13.8 %collective-permute-done.12 = bf16[40,512]{1,0:T(8,128)(2,1)S(1)} collective-permute-done((bf16[40,512]{1,0:T(8,128)(2,1)S(1)}, bf16[40,512]{1,0:T(8,128)(2,1)S(1)}, u32[]{:S(2)}, u32[]{:S(2)}) %collective-permute-start.12) | collective-permute-done | bytes 40992 | tf_op jit(solution)/shard_map/ppermute | solution.py:20
  129.3 1.5 collective-permute-start.14
  130.8 2.2 %collective-permute-start.16 = (bf16[32,512]{1,0:T(8,128)(2,1)S(1)}, bf16[32,512]{1,0:T(8,128)(2,1)S(1)}, u32[]{:S(2)}, u32[]{:S(2)}) collective-permute-start(bf16[32,512]{1,0:T(8,128)(2,1)S(1)} %get-tuple-element.27), channel_id=1, source_target_pairs={{0,3},{1,2},{2,1},{3,0},{4,7},{5,6},{6,5},{7,4},{8,11},{9,10},{10,... | collective-permute-start | bytes 98312 | tf_op jit(solution)/shard_map/ppermute | solution.py:20
  132.9 6.3 %fusion.4 = bf16[2048,512]{1,0:T(8,128)(2,1)S(1)} fusion(bf16[2048,512]{1,0:T(8,128)(2,1)} %bitcast.32, s32[2048]{0:T(1024)S(1)} %copy-done.5), kind=kOutput, calls=%fused_computation.7 | convolution fusion | flops 4300210176 | bytes 4202496 | tf_op jit(solution)/shard_map/dot_general | solution.py:171
  140.4 1.3 collective-permute-start.17
  143.3 3.4 %fusion.31 = f32[2048,512]{1,0:T(8,128)} fusion(bf16[2048,512]{1,0:T(8,128)(2,1)S(1)} %fusion.4, bf16[512,512]{1,0:T(8,128)(2,1)S(1)} %copy-done.8), kind=kOutput, calls=%fused_computation.91 | convolution fusion | flops 1073741824 | bytes 6815744 | tf_op jit(solution)/shard_map/dot_general | solution.py:174
  147.5 4.1 %collective-permute-start.20 = (bf16[4,4,32,512]{3,2,1,0:T(8,128)(2,1)S(1)}, bf16[4,4,32,512]{3,2,1,0:T(8,128)(2,1)S(1)}, u32[]{:S(2)}, u32[]{:S(2)}) collective-permute-start(bf16[4,4,32,512]{3,2,1,0:T(8,128)(2,1)S(1)} %bitcast_dynamic-update-slice_fusion), channel_id=1, source_target_pairs={{0,4},{4,0},{8,12},{12,8},{16,20},{20,16},{24,28},{28,24},{1,5},{5... | collective-permute-start | bytes 1572872 | tf_op jit(solution)/shard_map/ppermute | solution.py:15
  151.6 1.5 collective-permute-done.20
  153.2 1.6 %convert_multiply_fusion = (f32[2,4,4,16,512]{4,3,2,1,0:T(8,128)}, f32[2,4,4,16,512]{4,3,2,1,0:T(8,128)}) fusion(bf16[1,4,4,16,512]{4,3,2,1,0:T(8,128)(2,1)S(1)} %get-tuple-element.34, bf16[1,4,4,16,512]{4,3,2,1,0:T(8,128)(2,1)S(1)} %get-tuple-element.32, bf16[1,4,4,16,512]{4,3,2,1,0:T(8,128)(2,1)S(1)} %get-tuple-element.33, ...), kind=kLoop, calls=%fused_computation.14 | loop fusion | flops 1572864 | bytes 3145728 | tf_op jit(solution)/shard_map/mul | solution.py:187
  (89 shorter events, 17.2 us)
Async XLA Ops:
  0.6 20.8 %copy-start = (bf16[2048,512]{1,0:T(8,128)(2,1)S(1)}, bf16[2048,512]{1,0:T(8,128)(2,1)}, u32[]{:S(2)}) copy-start(bf16[2048,512]{1,0:T(8,128)(2,1)} %param.9) | copy-start | bytes 6291460
  0.6 13.4 %collective-permute-start = (bf16[8,512]{1,0:T(8,128)(2,1)}, bf16[8,512]{1,0:T(8,128)(2,1)S(1)}, u32[]{:S(2)}, u32[]{:S(2)}) collective-permute-start(bf16[8,512]{1,0:T(8,128)(2,1)} %param.15), channel_id=1, source_target_pairs={{0,1},{1,0},{2,3},{3,2},{4,5},{5,4},{6,7},{7,6},{8,9},{9,8},{10,11... | collective-permute-start | bytes 24584 | tf_op jit(solution)/shard_map/ppermute | solution.py:20
  2.8 11.2 %collective-permute-start.1 = (bf16[8,512]{1,0:T(8,128)(2,1)}, bf16[8,512]{1,0:T(8,128)(2,1)S(1)}, u32[]{:S(2)}, u32[]{:S(2)}) collective-permute-start(bf16[8,512]{1,0:T(8,128)(2,1)} %param.15), channel_id=1, source_target_pairs={{0,2},{1,3},{2,0},{3,1},{4,6},{5,7},{6,4},{7,5},{8,10},{9,11},{10,... | collective-permute-start | bytes 24584 | tf_op jit(solution)/shard_map/ppermute | solution.py:20
  5.1 8.9 %collective-permute-start.2 = (bf16[8,512]{1,0:T(8,128)(2,1)}, bf16[8,512]{1,0:T(8,128)(2,1)S(1)}, u32[]{:S(2)}, u32[]{:S(2)}) collective-permute-start(bf16[8,512]{1,0:T(8,128)(2,1)} %param.15), channel_id=1, source_target_pairs={{0,3},{1,2},{2,1},{3,0},{4,7},{5,6},{6,5},{7,4},{8,11},{9,10},{10,... | collective-permute-start | bytes 24584 | tf_op jit(solution)/shard_map/ppermute | solution.py:20
  7.4 6.6 %copy-start.10 = (bf16[8,512]{1,0:T(8,128)(2,1)S(1)}, bf16[8,512]{1,0:T(8,128)(2,1)}, u32[]{:S(2)}) copy-start(bf16[8,512]{1,0:T(8,128)(2,1)} %param.15) | copy-start | bytes 24580
  14.1 7.2 %copy-start.12 = (s32[1,32]{1,0:T(1,128)S(1)}, s32[1,32]{1,0:T(1,128)}, u32[]{:S(2)}) copy-start(s32[1,32]{1,0:T(1,128)} %param.11) | copy-start | bytes 388
  14.1 7.3 %copy-start.8 = (bf16[512,512]{1,0:T(8,128)(2,1)S(1)}, bf16[512,512]{1,0:T(8,128)(2,1)}, u32[]{:S(2)}) copy-start(bf16[512,512]{1,0:T(8,128)(2,1)} %param.16) | copy-start | bytes 1572868
  14.1 55.4 %all-to-all-start = ((bf16[32,64,512]{2,1,0:T(8,128)(2,1)}), bf16[32,64,512]{2,1,0:T(8,128)(2,1)}, u32[]{:S(2)}, u32[]{:S(2)}) async-start(bf16[32,64,512]{2,1,0:T(8,128)(2,1)} %bitcast.106), calls=%async_computation | async-start | bytes 4194304 | tf_op jit(solution)/shard_map/all_to_all | solution.py:113
  21.5 1.8 %copy-start.13 = (bf16[2048,512]{1,0:T(8,128)(2,1)S(1)}, bf16[2048,512]{1,0:T(8,128)(2,1)}, u32[]{:S(2)}) copy-start(bf16[2048,512]{1,0:T(8,128)(2,1)} %param.10) | copy-start | bytes 6291460
  23.2 16.4 %copy-start.11 = (s32[2048]{0:T(1024)S(1)}, s32[2048]{0:T(1024)}, u32[]{:S(2)}) copy-start(s32[2048]{0:T(1024)} %param.13) | copy-start | bytes 24580
  27.0 8.5 %collective-permute-start.3 = (bf16[4,8,512]{2,1,0:T(8,128)(2,1)S(1)}, bf16[4,8,512]{2,1,0:T(8,128)(2,1)S(1)}, u32[]{:S(2)}, u32[]{:S(2)}) collective-permute-start(bf16[4,8,512]{2,1,0:T(8,128)(2,1)S(1)} %bitcast_dynamic-update-slice_fusion.12), channel_id=1, source_target_pairs={{0,8},{4,12},{8,0},{12,4},{16,24},{20,28},{24,16},{28,20},{1,9},{5... | collective-permute-start | bytes 98312 | tf_op jit(solution)/shard_map/ppermute | solution.py:15
  28.3 7.1 %collective-permute-start.4 = (bf16[4,8,512]{2,1,0:T(8,128)(2,1)S(1)}, bf16[4,8,512]{2,1,0:T(8,128)(2,1)S(1)}, u32[]{:S(2)}, u32[]{:S(2)}) collective-permute-start(bf16[4,8,512]{2,1,0:T(8,128)(2,1)S(1)} %bitcast_dynamic-update-slice_fusion.12), channel_id=1, source_target_pairs={{0,16},{4,20},{8,24},{12,28},{16,0},{20,4},{24,8},{28,12},{1,17},{... | collective-permute-start | bytes 98312 | tf_op jit(solution)/shard_map/ppermute | solution.py:15
  29.5 8.6 %collective-permute-start.5 = (bf16[4,8,512]{2,1,0:T(8,128)(2,1)S(1)}, bf16[4,8,512]{2,1,0:T(8,128)(2,1)S(1)}, u32[]{:S(2)}, u32[]{:S(2)}) collective-permute-start(bf16[4,8,512]{2,1,0:T(8,128)(2,1)S(1)} %bitcast_dynamic-update-slice_fusion.12), channel_id=1, source_target_pairs={{0,24},{4,28},{8,16},{12,20},{16,8},{20,12},{24,0},{28,4},{1,25},{... | collective-permute-start | bytes 98312 | tf_op jit(solution)/shard_map/ppermute | solution.py:15
  38.1 2.5 %collective-permute-start.6 = (bf16[4,4,8,512]{3,2,1,0:T(8,128)(2,1)S(1)}, bf16[4,4,8,512]{3,2,1,0:T(8,128)(2,1)S(1)}, u32[]{:S(2)}, u32[]{:S(2)}) collective-permute-start(bf16[4,4,8,512]{3,2,1,0:T(8,128)(2,1)S(1)} %bitcast_dynamic-update-slice_fusion.8), channel_id=1, source_target_pairs={{0,4},{4,0},{8,12},{12,8},{16,20},{20,16},{24,28},{28,24},{1,5},{5... | collective-permute-start | bytes 393224 | tf_op jit(solution)/shard_map/ppermute | solution.py:15
  75.2 54.0 %all-to-all-start.1 = ((bf16[32,64,512]{2,1,0:T(8,128)(2,1)}), bf16[32,64,512]{2,1,0:T(8,128)(2,1)}, u32[]{:S(2)}, u32[]{:S(2)}) async-start(bf16[32,64,512]{2,1,0:T(8,128)(2,1)} %bitcast.110), calls=%async_computation.1 | async-start | bytes 4194304 | tf_op jit(solution)/shard_map/all_to_all | solution.py:136
  78.7 2.5 %copy-start.7 = (bf16[2048,512]{1,0:T(8,128)(2,1)S(1)}, bf16[2048,512]{1,0:T(8,128)(2,1)}, u32[]{:S(2)}) copy-start(bf16[2048,512]{1,0:T(8,128)(2,1)} %fusion.3) | copy-start | bytes 6291460
  81.1 1.6 %copy-start.14 = (bf16[2048,512]{1,0:T(8,128)(2,1)S(1)}, bf16[2048,512]{1,0:T(8,128)(2,1)}, u32[]{:S(2)}) copy-start(bf16[2048,512]{1,0:T(8,128)(2,1)} %param.10) | copy-start | bytes 6291460
  87.0 3.5 %collective-permute-start.7 = (f32[4,4,40,512]{3,2,1,0:T(8,128)}, f32[4,4,40,512]{3,2,1,0:T(8,128)}, u32[]{:S(2)}, u32[]{:S(2)}) collective-permute-start(f32[4,4,40,512]{3,2,1,0:T(8,128)} %dynamic-slice_bitcast_fusion), channel_id=1, source_target_pairs={{0,4},{4,0},{8,12},{12,8},{16,20},{20,16},{24,28},{28,24},{1,5},{5... | collective-permute-start | bytes 3932168 | tf_op jit(solution)/shard_map/ppermute | solution.py:15
  92.6 40.4 %copy-start.5 = (s32[2048]{0:T(1024)S(1)}, s32[2048]{0:T(1024)}, u32[]{:S(2)}) copy-start(s32[2048]{0:T(1024)} %param.12) | copy-start | bytes 24580
  92.6 10.2 %collective-permute-start.10 = (bf16[4,40,512]{2,1,0:T(8,128)(2,1)S(1)}, bf16[4,40,512]{2,1,0:T(8,128)(2,1)S(1)}, u32[]{:S(2)}, u32[]{:S(2)}) collective-permute-start(bf16[4,40,512]{2,1,0:T(8,128)(2,1)S(1)} %get-tuple-element.37), channel_id=1, source_target_pairs={{0,24},{4,28},{8,16},{12,20},{16,8},{20,12},{24,0},{28,4},{1,25},{... | collective-permute-start | bytes 491528 | tf_op jit(solution)/shard_map/ppermute | solution.py:15
  94.9 13.3 %collective-permute-start.8 = (bf16[4,40,512]{2,1,0:T(8,128)(2,1)S(1)}, bf16[4,40,512]{2,1,0:T(8,128)(2,1)S(1)}, u32[]{:S(2)}, u32[]{:S(2)}) collective-permute-start(bf16[4,40,512]{2,1,0:T(8,128)(2,1)S(1)} %get-tuple-element.36), channel_id=1, source_target_pairs={{0,8},{4,12},{8,0},{12,4},{16,24},{20,28},{24,16},{28,20},{1,9},{5... | collective-permute-start | bytes 491528 | tf_op jit(solution)/shard_map/ppermute | solution.py:15
  95.1 13.0 %collective-permute-start.9 = (bf16[4,40,512]{2,1,0:T(8,128)(2,1)S(1)}, bf16[4,40,512]{2,1,0:T(8,128)(2,1)S(1)}, u32[]{:S(2)}, u32[]{:S(2)}) collective-permute-start(bf16[4,40,512]{2,1,0:T(8,128)(2,1)S(1)} %get-tuple-element.38), channel_id=1, source_target_pairs={{0,16},{4,20},{8,24},{12,28},{16,0},{20,4},{24,8},{28,12},{1,17},{... | collective-permute-start | bytes 491528 | tf_op jit(solution)/shard_map/ppermute | solution.py:15
  108.2 7.1 %collective-permute-start.11 = (bf16[40,512]{1,0:T(8,128)(2,1)S(1)}, bf16[40,512]{1,0:T(8,128)(2,1)S(1)}, u32[]{:S(2)}, u32[]{:S(2)}) collective-permute-start(bf16[40,512]{1,0:T(8,128)(2,1)S(1)} %get-tuple-element.41), channel_id=1, source_target_pairs={{0,1},{1,0},{2,3},{3,2},{4,5},{5,4},{6,7},{7,6},{8,9},{9,8},{10,11... | collective-permute-start | bytes 122888 | tf_op jit(solution)/shard_map/ppermute | solution.py:20
  108.6 20.6 %collective-permute-start.12 = (bf16[40,512]{1,0:T(8,128)(2,1)S(1)}, bf16[40,512]{1,0:T(8,128)(2,1)S(1)}, u32[]{:S(2)}, u32[]{:S(2)}) collective-permute-start(bf16[40,512]{1,0:T(8,128)(2,1)S(1)} %get-tuple-element.43), channel_id=1, source_target_pairs={{0,2},{1,3},{2,0},{3,1},{4,6},{5,7},{6,4},{7,5},{8,10},{9,11},{10,... | collective-permute-start | bytes 122888 | tf_op jit(solution)/shard_map/ppermute | solution.py:20
  114.3 14.9 %collective-permute-start.13 = (bf16[40,512]{1,0:T(8,128)(2,1)S(1)}, bf16[40,512]{1,0:T(8,128)(2,1)S(1)}, u32[]{:S(2)}, u32[]{:S(2)}) collective-permute-start(bf16[40,512]{1,0:T(8,128)(2,1)S(1)} %get-tuple-element.42), channel_id=1, source_target_pairs={{0,3},{1,2},{2,1},{3,0},{4,7},{5,6},{6,5},{7,4},{8,11},{9,10},{10,... | collective-permute-start | bytes 122888 | tf_op jit(solution)/shard_map/ppermute | solution.py:20
  129.3 11.1 %collective-permute-start.14 = (bf16[32,512]{1,0:T(8,128)(2,1)S(1)}, bf16[32,512]{1,0:T(8,128)(2,1)S(1)}, u32[]{:S(2)}, u32[]{:S(2)}) collective-permute-start(bf16[32,512]{1,0:T(8,128)(2,1)S(1)} %get-tuple-element.27), channel_id=1, source_target_pairs={{0,1},{1,0},{2,3},{3,2},{4,5},{5,4},{6,7},{7,6},{8,9},{9,8},{10,11... | collective-permute-start | bytes 98312 | tf_op jit(solution)/shard_map/ppermute | solution.py:20
  130.8 9.6 %collective-permute-start.15 = (bf16[32,512]{1,0:T(8,128)(2,1)S(1)}, bf16[32,512]{1,0:T(8,128)(2,1)S(1)}, u32[]{:S(2)}, u32[]{:S(2)}) collective-permute-start(bf16[32,512]{1,0:T(8,128)(2,1)S(1)} %get-tuple-element.27), channel_id=1, source_target_pairs={{0,2},{1,3},{2,0},{3,1},{4,6},{5,7},{6,4},{7,5},{8,10},{9,11},{10,... | collective-permute-start | bytes 98312 | tf_op jit(solution)/shard_map/ppermute | solution.py:20
  130.8 9.6 %collective-permute-start.16 = (bf16[32,512]{1,0:T(8,128)(2,1)S(1)}, bf16[32,512]{1,0:T(8,128)(2,1)S(1)}, u32[]{:S(2)}, u32[]{:S(2)}) collective-permute-start(bf16[32,512]{1,0:T(8,128)(2,1)S(1)} %get-tuple-element.27), channel_id=1, source_target_pairs={{0,3},{1,2},{2,1},{3,0},{4,7},{5,6},{6,5},{7,4},{8,11},{9,10},{10,... | collective-permute-start | bytes 98312 | tf_op jit(solution)/shard_map/ppermute | solution.py:20
  140.4 6.3 %collective-permute-start.17 = (bf16[4,32,512]{2,1,0:T(8,128)(2,1)S(1)}, bf16[4,32,512]{2,1,0:T(8,128)(2,1)S(1)}, u32[]{:S(2)}, u32[]{:S(2)}) collective-permute-start(bf16[4,32,512]{2,1,0:T(8,128)(2,1)S(1)} %bitcast_dynamic-update-slice_fusion.4), channel_id=1, source_target_pairs={{0,8},{4,12},{8,0},{12,4},{16,24},{20,28},{24,16},{28,20},{1,9},{5... | collective-permute-start | bytes 393224 | tf_op jit(solution)/shard_map/ppermute | solution.py:15
  141.8 5.0 %collective-permute-start.18 = (bf16[4,32,512]{2,1,0:T(8,128)(2,1)S(1)}, bf16[4,32,512]{2,1,0:T(8,128)(2,1)S(1)}, u32[]{:S(2)}, u32[]{:S(2)}) collective-permute-start(bf16[4,32,512]{2,1,0:T(8,128)(2,1)S(1)} %bitcast_dynamic-update-slice_fusion.4), channel_id=1, source_target_pairs={{0,16},{4,20},{8,24},{12,28},{16,0},{20,4},{24,8},{28,12},{1,17},{... | collective-permute-start | bytes 393224 | tf_op jit(solution)/shard_map/ppermute | solution.py:15
  142.6 4.9 %collective-permute-start.19 = (bf16[4,32,512]{2,1,0:T(8,128)(2,1)S(1)}, bf16[4,32,512]{2,1,0:T(8,128)(2,1)S(1)}, u32[]{:S(2)}, u32[]{:S(2)}) collective-permute-start(bf16[4,32,512]{2,1,0:T(8,128)(2,1)S(1)} %bitcast_dynamic-update-slice_fusion.4), channel_id=1, source_target_pairs={{0,24},{4,28},{8,16},{12,20},{16,8},{20,12},{24,0},{28,4},{1,25},{... | collective-permute-start | bytes 393224 | tf_op jit(solution)/shard_map/ppermute | solution.py:15
  147.5 5.6 %collective-permute-start.20 = (bf16[4,4,32,512]{3,2,1,0:T(8,128)(2,1)S(1)}, bf16[4,4,32,512]{3,2,1,0:T(8,128)(2,1)S(1)}, u32[]{:S(2)}, u32[]{:S(2)}) collective-permute-start(bf16[4,4,32,512]{3,2,1,0:T(8,128)(2,1)S(1)} %bitcast_dynamic-update-slice_fusion), channel_id=1, source_target_pairs={{0,4},{4,0},{8,12},{12,8},{16,20},{20,16},{24,28},{28,24},{1,5},{5... | collective-permute-start | bytes 1572872 | tf_op jit(solution)/shard_map/ppermute | solution.py:15
  (6 other events, 7.8 us)

commit v3 on v2

v3 whole, which is shorter than its diff:
```python
import functools
import math

import jax
import jax.numpy as jnp
from jax import lax
from jax.experimental import pallas as pl
from jax.experimental.pallas import tpu as pltpu
from jax.sharding import PartitionSpec as P

AXES = ("rows", "grp")


def shift_rows(value, mask):
    size = lax.axis_size("rows")
    return lax.ppermute(value, "rows", [(i, i ^ mask) for i in range(size)])


def shift_grp(value, mask):
    size = lax.axis_size("grp")
    return lax.ppermute(value, "grp", [(i, i ^ mask) for i in range(size)])


def pick_kernel(key_ref, table_ref, out_ref):
    tile, length = key_ref.shape[1], table_ref.shape[0]
    keys = jnp.transpose(jnp.broadcast_to(key_ref[...], (128, tile)))
    lane = lax.broadcasted_iota(jnp.int32, (tile, 128), 1)
    one, zero = jnp.bfloat16(1), jnp.bfloat16(0)
    hot = jnp.concatenate(
        [jnp.where(keys == lane + at, one, zero) for at in range(0, length, 128)], axis=1
    )
    out_ref[...] = jnp.dot(hot, table_ref[...], preferred_element_type=jnp.float32).astype(
        jnp.bfloat16
    )


def pick(table, keys, space, limit, tile=512):
    length, width = table.shape
    count = keys.shape[0]
    tile = min(tile, count)
    return pl.pallas_call(
        pick_kernel,
        grid=(count // tile,),
        out_shape=space((count, width), jnp.bfloat16),
        in_specs=[
            pl.BlockSpec((1, tile), lambda i: (0, i)),
            pl.BlockSpec((length, width), lambda i: (0, 0)),
        ],
        out_specs=pl.BlockSpec((tile, width), lambda i: (i, 0)),
        compiler_params=pltpu.CompilerParams(vmem_limit_bytes=limit << 20),
        cost_estimate=pl.CostEstimate(
            flops=2 * count * length * width,
            bytes_accessed=2 * (length + count) * width,
            transcendentals=0,
        ),
        name="pick_rows",
    )(keys.reshape(1, count), table)


def gate_kernel(count_ref, hc_ref, hp_ref, wc_ref, wp_ref, out_ref, *, capacity):
    blocks = out_ref.shape[0] // capacity
    preact = jnp.dot(hc_ref[...], wc_ref[...], preferred_element_type=jnp.float32) + jnp.dot(
        hp_ref[...], wp_ref[...], preferred_element_type=jnp.float32
    )
    squashed = jax.nn.sigmoid(preact)
    slot = lax.broadcasted_iota(jnp.int32, (capacity, 1), 0)
    first = pl.program_id(0) * blocks
    live = jnp.concatenate([slot < count_ref[0, first + k] for k in range(blocks)])
    out_ref[...] = jnp.where(live, squashed * (1.0 + preact * (1.0 - squashed)), 0.0)


def slot_gate(cust_count, hc_edge, hp_edge, w_cust, w_prod, tile=512):
    count, width = hc_edge.shape
    tile = min(tile, count)
    slots = pl.BlockSpec((tile, width), lambda i, c: (i, 0))
    whole = pl.BlockSpec((width, width), lambda i, c: (0, 0))
    return pl.pallas_call(
        functools.partial(gate_kernel, capacity=count // cust_count.shape[1]),
        grid_spec=pltpu.PrefetchScalarGridSpec(
            num_scalar_prefetch=1,
            grid=(count // tile,),
            in_specs=[slots, slots, whole, whole],
            out_specs=slots,
        ),
        out_shape=pltpu.VMEM((count, width), jnp.float32),
        compiler_params=pltpu.CompilerParams(vmem_limit_bytes=32 << 20),
        cost_estimate=pl.CostEstimate(
            flops=4 * count * width * width,
            bytes_accessed=8 * count * width,
            transcendentals=count * width,
        ),
        name="slot_gate",
    )(cust_count, hc_edge, hp_edge, w_cust, w_prod)


def terms_kernel(half_ref, at_ref, hc_ref, hp_ref, delta_ref, out_ref):
    delta = delta_ref[...]
    columns = hc_ref.shape[1]
    products = out_ref.shape[0] - 2 * columns
    wanted = half_ref[0] * products + lax.broadcasted_iota(jnp.int32, (products, 1), 0)
    hot = jnp.where(at_ref[...] == wanted, jnp.bfloat16(1), jnp.bfloat16(0))
    contract = (((0,), (0,)), ((), ()))
    parts = (
        jnp.dot(hot, delta, preferred_element_type=jnp.float32),
        lax.dot_general(hc_ref[...], delta, contract, preferred_element_type=jnp.float32),
        lax.dot_general(hp_ref[...], delta, contract, preferred_element_type=jnp.float32),
    )
    starts = (0, products, products + columns)

    @pl.when(pl.program_id(0) == 0)
    def _():
        for at, part in zip(starts, parts):
            out_ref[at : at + part.shape[0], :] = part

    @pl.when(pl.program_id(0) > 0)
    def _():
        for at, part in zip(starts, parts):
            out_ref[at : at + part.shape[0], :] += part


def half_terms(half, prod_at, hc_edge, hp_edge, delta, products, tile=2048):
    count, width = delta.shape
    tile = min(tile, count)
    columns = width // 2
    rows = products // 2 + 2 * columns
    edge = pl.BlockSpec((tile, columns), lambda i, h: (i, h[0]))
    return pl.pallas_call(
        terms_kernel,
        grid_spec=pltpu.PrefetchScalarGridSpec(
            num_scalar_prefetch=1,
            grid=(count // tile,),
            in_specs=[
                pl.BlockSpec((1, tile), lambda i, h: (0, i)),
                edge,
                edge,
                pl.BlockSpec((tile, width), lambda i, h: (i, 0)),
            ],
            out_specs=pl.BlockSpec((rows, width), lambda i, h: (0, 0)),
        ),
        out_shape=jax.ShapeDtypeStruct((rows, width), jnp.float32),
        compiler_params=pltpu.CompilerParams(vmem_limit_bytes=32 << 20),
        cost_estimate=pl.CostEstimate(
            flops=2 * count * rows * width, bytes_accessed=4 * count * width, transcendentals=0
        ),
        name="half_terms",
    )(half.reshape(1), prod_at.reshape(1, count), hc_edge, hp_edge, delta)


def owner_sum_kernel(key_ref, rows_ref, *refs):
    out_ref = refs[-1]
    tile = out_ref.shape[0]
    wanted = pl.program_id(0) * tile + lax.broadcasted_iota(jnp.int32, (tile, 1), 0)
    hot = jnp.where(key_ref[...] == wanted, jnp.bfloat16(1), jnp.bfloat16(0))
    out_ref[...] = jnp.dot(hot, rows_ref[...], preferred_element_type=jnp.float32)


def owner_sum(keys, rows, owned, width, at, earlier=None, tile=512):
    count, columns = rows.shape
    tile = min(tile, owned)
    in_specs = [
        pl.BlockSpec((1, count), lambda i: (0, 0)),
        pl.BlockSpec((count, columns), lambda i: (0, 0)),
    ]
    operands = [keys.reshape(1, count), rows]
    aliases = {}
    if earlier is not None:
        in_specs.append(pl.BlockSpec(memory_space=pl.ANY))
        operands.append(earlier)
        aliases = {2: 0}
    return pl.pallas_call(
        owner_sum_kernel,
        grid=(owned // tile,),
        out_shape=jax.ShapeDtypeStruct((owned, width), jnp.float32),
        in_specs=in_specs,
        out_specs=pl.BlockSpec((tile, columns), lambda i: (i, at // columns)),
        input_output_aliases=aliases,
        compiler_params=pltpu.CompilerParams(vmem_limit_bytes=32 << 20),
        cost_estimate=pl.CostEstimate(
            flops=0 if earlier is None else 2 * owned * columns * count,
            bytes_accessed=0 if earlier is None else 2 * count * columns + 4 * owned * columns,
            transcendentals=0,
        ),
        name="owner_sum",
    )(*operands)


def delta_kernel(got_ref, product_ref, gate_ref, weight_ref, delta_ref, *out_refs):
    upstream = got_ref[...].astype(jnp.float32) + product_ref[...].astype(jnp.float32)
    delta = (upstream * gate_ref[...]).astype(jnp.bfloat16)
    delta_ref[...] = delta
    at = 0
    for out_ref in out_refs:
        part = weight_ref[at : at + out_ref.shape[1], :]
        at += out_ref.shape[1]
        out_ref[...] = lax.dot_general(
            delta, part, (((1,), (1,)), ((), ())), preferred_element_type=jnp.float32
        ).astype(jnp.bfloat16)


def delta_and_rows(got, product_rows, gate, weight, cuts, tile=1024):
    count, width = got.shape
    tile = min(tile, count)
    slots = lambda columns: pl.BlockSpec((tile, columns), lambda i: (i, 0))
    return pl.pallas_call(
        delta_kernel,
        grid=(count // tile,),
        in_specs=[
            slots(width),
            slots(width),
            slots(width),
            pl.BlockSpec((width, width), lambda i: (0, 0)),
        ],
        out_specs=[slots(width)] + [slots(columns) for columns in cuts],
        out_shape=[jax.ShapeDtypeStruct((count, width), jnp.bfloat16)]
        + [pltpu.HBM((count, columns), jnp.bfloat16) for columns in cuts],
        compiler_params=pltpu.CompilerParams(vmem_limit_bytes=56 << 20),
        cost_estimate=pl.CostEstimate(
            flops=2 * count * width * width, bytes_accessed=12 * count * width, transcendentals=0
        ),
        name="delta_and_rows",
    )(got, product_rows, gate, weight)


def place():
    row = lax.axis_index("rows")
    return row % 2, row // 2, lax.axis_index("grp")


def spread(mine, shift, size, step, here):
    blocks = [mine] + [shift(mine, step * k) for k in range(1, size)]
    stacked = jnp.zeros((size,) + mine.shape, mine.dtype)
    for k, block in enumerate(blocks):
        stacked = lax.dynamic_update_index_in_dim(stacked, block, here ^ k, 0)
    return stacked


def gather_grp(mine):
    return spread(mine, shift_grp, lax.axis_size("grp"), 1, lax.axis_index("grp"))


def gather_rows(own):
    core, plane, grp = place()
    own = spread(own, shift_rows, lax.axis_size("rows") // 2, 2, plane)
    other = shift_rows(own, 1)
    first = core == 0
    return jnp.stack([jnp.where(first, own, other), jnp.where(first, other, own)])


def fold(terms, shift, size, step, here):
    total = lax.dynamic_index_in_dim(terms, here, 0, False)
    leaving = terms.astype(jnp.bfloat16)
    for k in range(1, size):
        sent = lax.dynamic_index_in_dim(leaving, here ^ k, 0, False)
        total = total + shift(sent, step * k).astype(jnp.float32)
    return total


def body(hc_edge, hp_edge, cust_count, recv_key, prod_key, cust_grad, prod_grad, w_cust, w_prod):
    devices = lax.axis_size(AXES)
    grps = lax.axis_size("grp")
    planes = lax.axis_size("rows") // 2
    slot_count, width = hc_edge.shape
    capacity = slot_count // devices
    product_count = prod_grad.shape[0]
    grid = (2, planes, grps)

    products = gather_grp(prod_grad)
    owned_rows = pick(cust_grad, recv_key, pltpu.HBM, 60)
    owned_rows, products = lax.optimization_barrier((owned_rows, products))
    fetched = lax.all_to_all(
        owned_rows.reshape(devices, capacity, width), AXES, split_axis=0, concat_axis=0, tiled=True
    ).reshape(slot_count, width)

    owner, low = prod_key // product_count, prod_key % product_count
    row, grp = owner // grps, owner % grps
    prod_at = (((row % 2) * planes + row // 2) * grps + grp) * product_count + low
    product_table = gather_rows(products).reshape(devices * product_count, width)
    product_rows = pick(product_table, prod_at, jax.ShapeDtypeStruct, 16)

    gate = slot_gate(cust_count, hc_edge, hp_edge, w_cust, w_prod)
    cut = width // 2
    delta, first, second = delta_and_rows(
        fetched, product_rows, gate, w_cust, (cut, width - cut)
    )

    def give_back(rows):
        return lax.all_to_all(
            rows.reshape(devices, capacity, -1), AXES, split_axis=0, concat_axis=0, tiled=True
        ).reshape(slot_count, -1)

    returned = give_back(first)

    core, plane, _ = place()
    products = devices * product_count
    sent = half_terms(1 - core, prod_at, hc_edge, hp_edge, delta, products)
    kept = half_terms(core, prod_at, hc_edge, hp_edge, delta, products)
    kept = kept + shift_rows(sent, 1)
    cuts = (0, products // 2, products // 2 + width // 2, products // 2 + width)
    terms = jnp.concatenate(
        [kept[a:b].reshape(planes, grps, -1, width) for a, b in zip(cuts, cuts[1:])], axis=2
    )
    leaving = terms.astype(jnp.bfloat16)
    got = [
        shift_rows(lax.dynamic_index_in_dim(leaving, plane ^ k, 0, False), 2 * k)
        for k in range(1, planes)
    ]
    got, returned = lax.optimization_barrier((got, returned))
    mine = lax.dynamic_index_in_dim(terms, plane, 0, False)
    for block in got:
        mine = mine + block.astype(jnp.float32)
    mine = fold(mine, shift_grp, grps, 1, lax.axis_index("grp"))
    mine, second = lax.optimization_barrier((mine, second))
    returned_second = give_back(second)
    grad_scale = 1.0 / math.sqrt(slot_count * devices)
    share = width // devices
    owned = cust_grad.shape[0]
    own = gather_grp(mine[product_count:].astype(jnp.bfloat16))
    own, mine, returned = lax.optimization_barrier((own, mine, returned))
    prod_table_grad = lax.dot_general(
        mine[:product_count],
        w_prod.astype(jnp.float32),
        (((1,), (1,)), ((), ())),
        precision=lax.Precision.HIGHEST,
        preferred_element_type=jnp.float32,
    ) * math.sqrt(product_count / slot_count)
    table = owner_sum(recv_key, returned, owned, width, 0)
    own = spread(own, shift_rows, planes, 2, plane)
    own, table, prod_table_grad = lax.optimization_barrier((own, table, prod_table_grad))
    other = shift_rows(own, 1)
    cust_table_grad = owner_sum(recv_key, returned_second, owned, width, cut, table)

    def whole(share_at):
        pick_share = slice(share_at, share_at + share)
        mine_part, other_part = own[:, :, pick_share], other[:, :, pick_share]
        first = lax.axis_index("rows") % 2 == 0
        both = [jnp.where(first, mine_part, other_part), jnp.where(first, other_part, mine_part)]
        return jnp.stack(both).astype(jnp.float32).reshape(width, width) * grad_scale

    return cust_table_grad, prod_table_grad, whole(0), whole(share)


def solution(mesh):
    rows = P(AXES, None)
    placed = (rows, rows, rows, P(AXES), P(AXES), rows, rows, P(), P())
    return jax.shard_map(
        body,
        mesh=mesh,
        in_specs=placed,
        out_specs=(rows, rows, P(), P()),
        check_vma=False,
    )
```

time: 156 us -> 150 us (0.962)
  Pallas kernels: 6.64 us -> 29.3 us
  matrix products: 20.8 us -> 1.13 us
  other arithmetic: 9.97 us -> 2.36 us
    pallas_call x2 -> x8, Pallas kernels: 6.64 us -> 29.3 us  [the longest x2 9.09 us: pick(): pl.pallas_call(pick_kernel, grid=(count // tile,), out_shape=space((count...]
    dot_general x7 -> x0, matrix products: 19.7 us -> none  [the longest x1 6.27 us: body(): jnp.dot(one_hot, returned, preferred_element_type=jnp.float32)]
    ppermute x9, waiting for transfers between devices: 13.8 us -> 2.13 us  [shift_grp(): return lax.ppermute(value, 'grp', [(i, i ^ mask) for i in range(size)])]
    all_to_all x1 -> x2, waiting for transfers between devices: 0.01 us -> 9.57 us  [give_back(): lax.all_to_all(rows.reshape(devices, capacity, -1), AXES, split_axis=0, c...]
    ppermute x12, waiting for transfers between devices: 27.2 us -> 36.6 us  [shift_rows(): return lax.ppermute(value, 'rows', [(i, i ^ mask) for i in range(size)])]
    all_to_all x1, waiting for transfers between devices: 26.1 us -> 19.4 us  [body(): lax.all_to_all(owned_rows.reshape(devices, capacity, width), AXES, split_...]
    all_to_all x1 -> x2, starting transfers between devices: 3.42 us -> 9.59 us  [give_back(): lax.all_to_all(rows.reshape(devices, capacity, -1), AXES, split_axis=0, c...]
    convert_element_type x1, other arithmetic: 5.65 us -> 0.08 us  [body(): leaving = terms.astype(jnp.bfloat16)]
  transfers between devices with their start and end apart: 23 -> 24, of which waited for: 10 -> 15; matrix products, arithmetic and copies ran while one was open for 16% -> 2% of each run, Pallas kernels for 4% -> 13%
where the time goes in v3:
time: 150 us
  waiting for transfers between devices  67.6 us (45%)
  starting transfers between devices  39.6 us (26%)
  Pallas kernels  29.3 us (20%)
  local copies, waits for them, and re-layouts  8.52 us (6%)
  other arithmetic  2.36 us (2%)
    ppermute x12, waiting for transfers between devices, shift_rows(): return lax.ppermute(value, 'rows', [(i, i ^ mask) for i in range(size)])  36.6 us
    all_to_all x1, waiting for transfers between devices, body(): lax.all_to_all(owned_rows.reshape(devices, capacity, width), AXES, split_...  19.4 us
    ppermute x9, starting transfers between devices, shift_grp(): return lax.ppermute(value, 'grp', [(i, i ^ mask) for i in range(size)])  11.7 us
    ppermute x12, starting transfers between devices, shift_rows(): return lax.ppermute(value, 'rows', [(i, i ^ mask) for i in range(size)])  11.1 us
    all_to_all x2, starting transfers between devices, give_back(): lax.all_to_all(rows.reshape(devices, capacity, -1), AXES, split_axis=0, c...  9.59 us
    all_to_all x2, waiting for transfers between devices, give_back(): lax.all_to_all(rows.reshape(devices, capacity, -1), AXES, split_axis=0, c...  9.57 us
    pallas_call x2, Pallas kernels, pick(): pl.pallas_call(pick_kernel, grid=(count // tile,), out_shape=space((count...  9.09 us
    unnamed x26, local copies, waits for them, and re-layouts  8.15 us
  transfers between devices with their start and end apart: 24, of which 15 were waited for; matrix products, arithmetic and copies ran while one was open for 2% of the time, Pallas kernels for 13%

profile of v3, /device:TPU:1, one launch (start us, length us, event | category | flops | bytes accessed | tf_op | source)
XLA Modules:
  0.0 149.6 jit_solution(9714016062181871017)
XLA Ops:
  0.6 2.2 %collective-permute-start = (bf16[8,512]{1,0:T(8,128)(2,1)}, bf16[8,512]{1,0:T(8,128)(2,1)S(1)}, u32[]{:S(2)}, u32[]{:S(2)}) collective-permute-start(bf16[8,512]{1,0:T(8,128)(2,1)} %param.15), channel_id=1, source_target_pairs={{0,1},{1,0},{2,3},{3,2},{4,5},{5,4},{6,7},{7,6},{8,9},{9,8},{10,11... | collective-permute-start | bytes 24584 | tf_op jit(solution)/shard_map/ppermute | solution.py:21
  2.8 2.3 %collective-permute-start.1 = (bf16[8,512]{1,0:T(8,128)(2,1)}, bf16[8,512]{1,0:T(8,128)(2,1)S(1)}, u32[]{:S(2)}, u32[]{:S(2)}) collective-permute-start(bf16[8,512]{1,0:T(8,128)(2,1)} %param.15), channel_id=1, source_target_pairs={{0,2},{1,3},{2,0},{3,1},{4,6},{5,7},{6,4},{7,5},{8,10},{9,11},{10,... | collective-permute-start | bytes 24584 | tf_op jit(solution)/shard_map/ppermute | solution.py:21
  5.1 7.6 %pick_rows.2 = bf16[2048,512]{1,0:T(8,128)(2,1)} custom-call(s32[1,2048]{1,0:T(1,128)} %bitcast.92, bf16[2048,512]{1,0:T(8,128)(2,1)} %table_ref.1), custom_call_target="tpu_custom_call" | custom-call | flops 4294967296 | bytes 4194304 | tf_op jit(solution)/shard_map/pick_rows/pallas_call | solution.py:41
  13.0 7.1 %all-to-all-start = ((bf16[32,64,512]{2,1,0:T(8,128)(2,1)}), bf16[32,64,512]{2,1,0:T(8,128)(2,1)}, u32[]{:S(2)}, u32[]{:S(2)}) async-start(bf16[32,64,512]{2,1,0:T(8,128)(2,1)} %bitcast.101), calls=%async_computation | async-start | bytes 4194304 | tf_op jit(solution)/shard_map/all_to_all | solution.py:270
  22.9 11.4 %collective-permute-done.3 = bf16[4,8,512]{2,1,0:T(8,128)(2,1)S(1)} collective-permute-done((bf16[4,8,512]{2,1,0:T(8,128)(2,1)S(1)}, bf16[4,8,512]{2,1,0:T(8,128)(2,1)S(1)}, u32[]{:S(2)}, u32[]{:S(2)}) %collective-permute-start.3) | collective-permute-done | bytes 32800 | tf_op jit(solution)/shard_map/ppermute | solution.py:16
  34.4 2.6 %collective-permute-done.5 = bf16[4,8,512]{2,1,0:T(8,128)(2,1)S(1)} collective-permute-done((bf16[4,8,512]{2,1,0:T(8,128)(2,1)S(1)}, bf16[4,8,512]{2,1,0:T(8,128)(2,1)S(1)}, u32[]{:S(2)}, u32[]{:S(2)}) %collective-permute-start.5) | collective-permute-done | bytes 32800 | tf_op jit(solution)/shard_map/ppermute | solution.py:16
  37.0 1.5 collective-permute-start.6
  38.5 1.6 %copy-done.1 = bf16[2048,512]{1,0:T(8,128)(2,1)S(1)} copy-done((bf16[2048,512]{1,0:T(8,128)(2,1)S(1)}, bf16[2048,512]{1,0:T(8,128)(2,1)}, u32[]{:S(2)}) %copy-start.1) | copy-done | bytes 2097176
  40.1 4.0 %slot_gate.1.gate_ref = f32[2048,512]{1,0:T(8,128)S(1)} custom-call(s32[1,32]{1,0:T(1,128)S(1)} %copy-done.10, bf16[2048,512]{1,0:T(8,128)(2,1)S(1)} %copy-done, bf16[2048,512]{1,0:T(8,128)(2,1)S(1)} %copy-done.1, bf16[512,512]{1,0:T(8,128)(2,1)S(1)} %copy-done.6, bf16[512,512]{1,0:T(8,128)(2,1)S(1)} %copy-done.7), custom_call_target="tpu_custom_call" | custom-call | flops 2147483648 | bytes 8388608 | tf_op jit(solution)/shard_map/slot_gate/pallas_call | solution.py:77
  44.2 2.0 %copy-done.3 = f32[2048,512]{1,0:T(8,128)} copy-done((f32[2048,512]{1,0:T(8,128)}, f32[2048,512]{1,0:T(8,128)S(1)}, u32[]{:S(2)}) %copy-start.3) | copy-done | bytes 4194328
  49.0 19.4 %all-to-all-done = bf16[32,64,512]{2,1,0:T(8,128)(2,1)} async-done(((bf16[32,64,512]{2,1,0:T(8,128)(2,1)}), bf16[32,64,512]{2,1,0:T(8,128)(2,1)}, u32[]{:S(2)}, u32[]{:S(2)}) %all-to-all-start) | async-done | bytes 2097184 | tf_op jit(solution)/shard_map/all_to_all | solution.py:270
  68.4 5.6 %delta_and_rows.1 = (bf16[2048,512]{1,0:T(8,128)(2,1)}, bf16[2048,256]{1,0:T(8,128)(2,1)}, bf16[2048,256]{1,0:T(8,128)(2,1)}) custom-call(bf16[2048,512]{1,0:T(8,128)(2,1)} %bitcast.8.got_ref, bf16[2048,512]{1,0:T(8,128)(2,1)} %copy-done.5, f32[2048,512]{1,0:T(8,128)} %copy-done.3, bf16[512,512]{1,0:T(8,128)(2,1)} %weight_ref.1), custom_call_target="tpu_custom_call" | custom-call | flops 1073741824 | bytes 12582912 | tf_op jit(solution)/shard_map/delta_and_rows/pallas_call | solution.py:204
  74.0 3.3 %all-to-all-start.1 = ((bf16[32,64,256]{2,1,0:T(8,128)(2,1)}), bf16[32,64,256]{2,1,0:T(8,128)(2,1)S(1)}, u32[]{:S(2)}, u32[]{:S(2)}) async-start(bf16[32,64,256]{2,1,0:T(8,128)(2,1)} %bitcast.105), calls=%async_computation.1 | async-start | bytes 2097152 | tf_op jit(solution)/shard_map/all_to_all | solution.py:287
  77.4 1.6 %copy-done.2 = bf16[2048,512]{1,0:T(8,128)(2,1)S(1)} copy-done((bf16[2048,512]{1,0:T(8,128)(2,1)S(1)}, bf16[2048,512]{1,0:T(8,128)(2,1)}, u32[]{:S(2)}) %copy-start.2) | copy-done | bytes 2097176
  78.9 1.6 %copy-done.4 = bf16[2048,512]{1,0:T(8,128)(2,1)S(1)} copy-done((bf16[2048,512]{1,0:T(8,128)(2,1)S(1)}, bf16[2048,512]{1,0:T(8,128)(2,1)}, u32[]{:S(2)}) %copy-start.4) | copy-done | bytes 2097176
  80.5 1.5 %half_terms.3 = f32[640,512]{1,0:T(8,128)S(1)} custom-call(s32[1]{0:T(128)} %bitcast.16.half_ref, s32[1,2048]{1,0:T(1,128)S(1)} %bitcast.90, bf16[2048,512]{1,0:T(8,128)(2,1)S(1)} %copy-done, bf16[2048,512]{1,0:T(8,128)(2,1)S(1)} %copy-done.2, bf16[2048,512]{1,0:T(8,128)(2,1)S(1)} %copy-done.4), custom_call_target="tpu_custom_call" | custom-call | flops 1342177280 | bytes 4194304 | tf_op jit(solution)/shard_map/half_terms/pallas_call | solution.py:127
  82.4 1.5 %half_terms.2 = f32[640,512]{1,0:T(8,128)S(1)} custom-call(s32[1]{0:T(128)} %bitcast.1.half_ref, s32[1,2048]{1,0:T(1,128)S(1)} %bitcast.91, bf16[2048,512]{1,0:T(8,128)(2,1)S(1)} %copy-done, bf16[2048,512]{1,0:T(8,128)(2,1)S(1)} %copy-done.2, bf16[2048,512]{1,0:T(8,128)(2,1)S(1)} %copy-done.4), custom_call_target="tpu_custom_call" | custom-call | flops 1342177280 | bytes 4194304 | tf_op jit(solution)/shard_map/half_terms/pallas_call | solution.py:127
  85.7 2.4 %collective-permute-start.10 = (bf16[4,40,512]{2,1,0:T(8,128)(2,1)S(1)}, bf16[4,40,512]{2,1,0:T(8,128)(2,1)S(1)}, u32[]{:S(2)}, u32[]{:S(2)}) collective-permute-start(bf16[4,40,512]{2,1,0:T(8,128)(2,1)S(1)} %get-tuple-element.48), channel_id=1, source_target_pairs={{0,24},{4,28},{8,16},{12,20},{16,8},{20,12},{24,0},{28,4},{1,25},{... | collective-permute-start | bytes 491528 | tf_op jit(solution)/shard_map/ppermute | solution.py:16
  88.5 6.4 %collective-permute-done.10 = bf16[4,40,512]{2,1,0:T(8,128)(2,1)S(1)} collective-permute-done((bf16[4,40,512]{2,1,0:T(8,128)(2,1)S(1)}, bf16[4,40,512]{2,1,0:T(8,128)(2,1)S(1)}, u32[]{:S(2)}, u32[]{:S(2)}) %collective-permute-start.10) | collective-permute-done | bytes 163872 | tf_op jit(solution)/shard_map/ppermute | solution.py:16
  94.9 3.6 %collective-permute-done.8 = bf16[4,40,512]{2,1,0:T(8,128)(2,1)S(1)} collective-permute-done((bf16[4,40,512]{2,1,0:T(8,128)(2,1)S(1)}, bf16[4,40,512]{2,1,0:T(8,128)(2,1)S(1)}, u32[]{:S(2)}, u32[]{:S(2)}) %collective-permute-start.8) | collective-permute-done | bytes 163872 | tf_op jit(solution)/shard_map/ppermute | solution.py:16
  99.1 4.6 %all-to-all-done.1 = bf16[32,64,256]{2,1,0:T(8,128)(2,1)S(1)} async-done(((bf16[32,64,256]{2,1,0:T(8,128)(2,1)}), bf16[32,64,256]{2,1,0:T(8,128)(2,1)S(1)}, u32[]{:S(2)}, u32[]{:S(2)}) %all-to-all-start.1) | async-done | bytes 1048608 | tf_op jit(solution)/shard_map/all_to_all | solution.py:287
  104.7 2.7 %collective-permute-start.13 = (bf16[40,512]{1,0:T(8,128)(2,1)S(1)}, bf16[40,512]{1,0:T(8,128)(2,1)S(1)}, u32[]{:S(2)}, u32[]{:S(2)}) collective-permute-start(bf16[40,512]{1,0:T(8,128)(2,1)S(1)} %get-tuple-element.54), channel_id=1, source_target_pairs={{0,3},{1,2},{2,1},{3,0},{4,7},{5,6},{6,5},{7,4},{8,11},{9,10},{10,... | collective-permute-start | bytes 122888 | tf_op jit(solution)/shard_map/ppermute | solution.py:21
  107.7 1.8 %collective-permute-done.13 = bf16[40,512]{1,0:T(8,128)(2,1)S(1)} collective-permute-done((bf16[40,512]{1,0:T(8,128)(2,1)S(1)}, bf16[40,512]{1,0:T(8,128)(2,1)S(1)}, u32[]{:S(2)}, u32[]{:S(2)}) %collective-permute-start.13) | collective-permute-done | bytes 40992 | tf_op jit(solution)/shard_map/ppermute | solution.py:21
  110.5 2.0 %collective-permute-start.15 = (bf16[32,512]{1,0:T(8,128)(2,1)S(1)}, bf16[32,512]{1,0:T(8,128)(2,1)S(1)}, u32[]{:S(2)}, u32[]{:S(2)}) collective-permute-start(bf16[32,512]{1,0:T(8,128)(2,1)S(1)} %get-tuple-element.39), channel_id=1, source_target_pairs={{0,2},{1,3},{2,0},{3,1},{4,6},{5,7},{6,4},{7,5},{8,10},{9,11},{10,... | collective-permute-start | bytes 98312 | tf_op jit(solution)/shard_map/ppermute | solution.py:21
  113.2 6.3 %all-to-all-start.2 = ((bf16[32,64,256]{2,1,0:T(8,128)(2,1)}), bf16[32,64,256]{2,1,0:T(8,128)(2,1)S(1)}, u32[]{:S(2)}, u32[]{:S(2)}) async-start(bf16[32,64,256]{2,1,0:T(8,128)(2,1)} %bitcast.104), calls=%async_computation.2 | async-start | bytes 2097152 | tf_op jit(solution)/shard_map/all_to_all | solution.py:287
  122.3 3.7 %owner_sum.2.refs_0_ = f32[2048,512]{1,0:T(8,128)} custom-call(s32[1,2048]{1,0:T(1,128)S(1)} %bitcast.93, bf16[2048,256]{1,0:T(8,128)(2,1)S(1)} %bitcast.86), custom_call_target="tpu_custom_call" | custom-call | tf_op jit(solution)/shard_map/owner_sum/pallas_call | solution.py:170
  127.3 4.6 %collective-permute-done.17 = bf16[4,32,512]{2,1,0:T(8,128)(2,1)S(1)} collective-permute-done((bf16[4,32,512]{2,1,0:T(8,128)(2,1)S(1)}, bf16[4,32,512]{2,1,0:T(8,128)(2,1)S(1)}, u32[]{:S(2)}, u32[]{:S(2)}) %collective-permute-start.17) | collective-permute-done | bytes 131104 | tf_op jit(solution)/shard_map/ppermute | solution.py:16
  133.1 3.4 %collective-permute-done.19 = bf16[4,32,512]{2,1,0:T(8,128)(2,1)S(1)} collective-permute-done((bf16[4,32,512]{2,1,0:T(8,128)(2,1)S(1)}, bf16[4,32,512]{2,1,0:T(8,128)(2,1)S(1)}, u32[]{:S(2)}, u32[]{:S(2)}) %collective-permute-start.19) | collective-permute-done | bytes 131104 | tf_op jit(solution)/shard_map/ppermute | solution.py:16
  137.7 1.5 %collective-permute-done.20 = bf16[4,4,32,512]{3,2,1,0:T(8,128)(2,1)S(1)} collective-permute-done((bf16[4,4,32,512]{3,2,1,0:T(8,128)(2,1)S(1)}, bf16[4,4,32,512]{3,2,1,0:T(8,128)(2,1)S(1)}, u32[]{:S(2)}, u32[]{:S(2)}) %collective-permute-start.20) | collective-permute-done | bytes 524320 | tf_op jit(solution)/shard_map/ppermute | solution.py:16
  139.3 1.6 %convert_multiply_fusion = (f32[2,4,4,16,512]{4,3,2,1,0:T(8,128)}, f32[2,4,4,16,512]{4,3,2,1,0:T(8,128)}) fusion(bf16[1,4,4,16,512]{4,3,2,1,0:T(8,128)(2,1)S(1)} %get-tuple-element.46, bf16[1,4,4,16,512]{4,3,2,1,0:T(8,128)(2,1)S(1)} %get-tuple-element.44, bf16[1,4,4,16,512]{4,3,2,1,0:T(8,128)(2,1)S(1)} %get-tuple-element.45, ...), kind=kLoop, calls=%fused_computation.2 | loop fusion | flops 1572864 | bytes 3145728 | tf_op jit(solution)/shard_map/mul | solution.py:337
  140.9 5.0 %all-to-all-done.2 = bf16[32,64,256]{2,1,0:T(8,128)(2,1)S(1)} async-done(((bf16[32,64,256]{2,1,0:T(8,128)(2,1)}), bf16[32,64,256]{2,1,0:T(8,128)(2,1)S(1)}, u32[]{:S(2)}, u32[]{:S(2)}) %all-to-all-start.2) | async-done | bytes 1048608 | tf_op jit(solution)/shard_map/all_to_all | solution.py:287
  145.9 3.7 %owner_sum.3 = f32[2048,512]{1,0:T(8,128)} custom-call(s32[1,2048]{1,0:T(1,128)S(1)} %bitcast.94, bf16[2048,256]{1,0:T(8,128)(2,1)S(1)} %bitcast.87, f32[2048,512]{1,0:T(8,128)} %owner_sum.2.refs_0_), custom_call_target="tpu_custom_call", output_to_operand_aliasing={{}: (2, {})} | custom-call | flops 2147483648 | bytes 3145728 | tf_op jit(solution)/shard_map/owner_sum/pallas_call | solution.py:170
  (85 shorter events, 18.2 us)
Async XLA Ops:
  0.6 12.2 %collective-permute-start = (bf16[8,512]{1,0:T(8,128)(2,1)}, bf16[8,512]{1,0:T(8,128)(2,1)S(1)}, u32[]{:S(2)}, u32[]{:S(2)}) collective-permute-start(bf16[8,512]{1,0:T(8,128)(2,1)} %param.15), channel_id=1, source_target_pairs={{0,1},{1,0},{2,3},{3,2},{4,5},{5,4},{6,7},{7,6},{8,9},{9,8},{10,11... | collective-permute-start | bytes 24584 | tf_op jit(solution)/shard_map/ppermute | solution.py:21
  2.8 10.0 %collective-permute-start.1 = (bf16[8,512]{1,0:T(8,128)(2,1)}, bf16[8,512]{1,0:T(8,128)(2,1)S(1)}, u32[]{:S(2)}, u32[]{:S(2)}) collective-permute-start(bf16[8,512]{1,0:T(8,128)(2,1)} %param.15), channel_id=1, source_target_pairs={{0,2},{1,3},{2,0},{3,1},{4,6},{5,7},{6,4},{7,5},{8,10},{9,11},{10,... | collective-permute-start | bytes 24584 | tf_op jit(solution)/shard_map/ppermute | solution.py:21
  5.1 7.8 %collective-permute-start.2 = (bf16[8,512]{1,0:T(8,128)(2,1)}, bf16[8,512]{1,0:T(8,128)(2,1)S(1)}, u32[]{:S(2)}, u32[]{:S(2)}) collective-permute-start(bf16[8,512]{1,0:T(8,128)(2,1)} %param.15), channel_id=1, source_target_pairs={{0,3},{1,2},{2,1},{3,0},{4,7},{5,6},{6,5},{7,4},{8,11},{9,10},{10,... | collective-permute-start | bytes 24584 | tf_op jit(solution)/shard_map/ppermute | solution.py:21
  5.1 7.7 %copy-start.11 = (bf16[8,512]{1,0:T(8,128)(2,1)S(1)}, bf16[8,512]{1,0:T(8,128)(2,1)}, u32[]{:S(2)}) copy-start(bf16[8,512]{1,0:T(8,128)(2,1)} %param.15) | copy-start | bytes 24580
  12.9 7.2 %copy-start.12 = (s32[2048]{0:T(1024)S(1)}, s32[2048]{0:T(1024)}, u32[]{:S(2)}) copy-start(s32[2048]{0:T(1024)} %param.13) | copy-start | bytes 24580
  12.9 25.6 %copy-start = (bf16[2048,512]{1,0:T(8,128)(2,1)S(1)}, bf16[2048,512]{1,0:T(8,128)(2,1)}, u32[]{:S(2)}) copy-start(bf16[2048,512]{1,0:T(8,128)(2,1)} %hc_ref.5) | copy-start | bytes 6291460
  12.9 25.6 %copy-start.6 = (bf16[512,512]{1,0:T(8,128)(2,1)S(1)}, bf16[512,512]{1,0:T(8,128)(2,1)}, u32[]{:S(2)}) copy-start(bf16[512,512]{1,0:T(8,128)(2,1)} %weight_ref.1) | copy-start | bytes 1572868
  12.9 25.6 %copy-start.7 = (bf16[512,512]{1,0:T(8,128)(2,1)S(1)}, bf16[512,512]{1,0:T(8,128)(2,1)}, u32[]{:S(2)}) copy-start(bf16[512,512]{1,0:T(8,128)(2,1)} %wp_ref.1) | copy-start | bytes 1572868
  13.0 25.5 %copy-start.10 = (s32[1,32]{1,0:T(1,128)S(1)}, s32[1,32]{1,0:T(1,128)}, u32[]{:S(2)}) copy-start(s32[1,32]{1,0:T(1,128)} %count_ref.1) | copy-start | bytes 388
  13.0 55.4 %all-to-all-start = ((bf16[32,64,512]{2,1,0:T(8,128)(2,1)}), bf16[32,64,512]{2,1,0:T(8,128)(2,1)}, u32[]{:S(2)}, u32[]{:S(2)}) async-start(bf16[32,64,512]{2,1,0:T(8,128)(2,1)} %bitcast.101), calls=%async_computation | async-start | bytes 4194304 | tf_op jit(solution)/shard_map/all_to_all | solution.py:270
  20.2 14.1 %collective-permute-start.3 = (bf16[4,8,512]{2,1,0:T(8,128)(2,1)S(1)}, bf16[4,8,512]{2,1,0:T(8,128)(2,1)S(1)}, u32[]{:S(2)}, u32[]{:S(2)}) collective-permute-start(bf16[4,8,512]{2,1,0:T(8,128)(2,1)S(1)} %bitcast_dynamic-update-slice_fusion.12), channel_id=1, source_target_pairs={{0,8},{4,12},{8,0},{12,4},{16,24},{20,28},{24,16},{28,20},{1,9},{5... | collective-permute-start | bytes 98312 | tf_op jit(solution)/shard_map/ppermute | solution.py:16
  21.6 12.7 %collective-permute-start.4 = (bf16[4,8,512]{2,1,0:T(8,128)(2,1)S(1)}, bf16[4,8,512]{2,1,0:T(8,128)(2,1)S(1)}, u32[]{:S(2)}, u32[]{:S(2)}) collective-permute-start(bf16[4,8,512]{2,1,0:T(8,128)(2,1)S(1)} %bitcast_dynamic-update-slice_fusion.12), channel_id=1, source_target_pairs={{0,16},{4,20},{8,24},{12,28},{16,0},{20,4},{24,8},{28,12},{1,17},{... | collective-permute-start | bytes 98312 | tf_op jit(solution)/shard_map/ppermute | solution.py:16
  22.8 14.2 %collective-permute-start.5 = (bf16[4,8,512]{2,1,0:T(8,128)(2,1)S(1)}, bf16[4,8,512]{2,1,0:T(8,128)(2,1)S(1)}, u32[]{:S(2)}, u32[]{:S(2)}) collective-permute-start(bf16[4,8,512]{2,1,0:T(8,128)(2,1)S(1)} %bitcast_dynamic-update-slice_fusion.12), channel_id=1, source_target_pairs={{0,24},{4,28},{8,16},{12,20},{16,8},{20,12},{24,0},{28,4},{1,25},{... | collective-permute-start | bytes 98312 | tf_op jit(solution)/shard_map/ppermute | solution.py:16
  37.0 9.2 %collective-permute-start.6 = (bf16[4,4,8,512]{3,2,1,0:T(8,128)(2,1)S(1)}, bf16[4,4,8,512]{3,2,1,0:T(8,128)(2,1)S(1)}, u32[]{:S(2)}, u32[]{:S(2)}) collective-permute-start(bf16[4,4,8,512]{3,2,1,0:T(8,128)(2,1)S(1)} %bitcast_dynamic-update-slice_fusion.8), channel_id=1, source_target_pairs={{0,4},{4,0},{8,12},{12,8},{16,20},{20,16},{24,28},{28,24},{1,5},{5... | collective-permute-start | bytes 393224 | tf_op jit(solution)/shard_map/ppermute | solution.py:16
  74.0 29.7 %all-to-all-start.1 = ((bf16[32,64,256]{2,1,0:T(8,128)(2,1)}), bf16[32,64,256]{2,1,0:T(8,128)(2,1)S(1)}, u32[]{:S(2)}, u32[]{:S(2)}) async-start(bf16[32,64,256]{2,1,0:T(8,128)(2,1)} %bitcast.105), calls=%async_computation.1 | async-start | bytes 2097152 | tf_op jit(solution)/shard_map/all_to_all | solution.py:287
  82.1 3.1 %collective-permute-start.7 = (f32[640,512]{1,0:T(8,128)S(1)}, f32[640,512]{1,0:T(8,128)S(1)}, u32[]{:S(2)}, u32[]{:S(2)}) collective-permute-start(f32[640,512]{1,0:T(8,128)S(1)} %half_terms.3), channel_id=1, source_target_pairs={{0,4},{4,0},{8,12},{12,8},{16,20},{20,16},{24,28},{28,24},{1,5},{5... | collective-permute-start | bytes 3932168 | tf_op jit(solution)/shard_map/ppermute | solution.py:16
  85.7 9.3 %collective-permute-start.10 = (bf16[4,40,512]{2,1,0:T(8,128)(2,1)S(1)}, bf16[4,40,512]{2,1,0:T(8,128)(2,1)S(1)}, u32[]{:S(2)}, u32[]{:S(2)}) collective-permute-start(bf16[4,40,512]{2,1,0:T(8,128)(2,1)S(1)} %get-tuple-element.48), channel_id=1, source_target_pairs={{0,24},{4,28},{8,16},{12,20},{16,8},{20,12},{24,0},{28,4},{1,25},{... | collective-permute-start | bytes 491528 | tf_op jit(solution)/shard_map/ppermute | solution.py:16
  88.0 10.5 %collective-permute-start.8 = (bf16[4,40,512]{2,1,0:T(8,128)(2,1)S(1)}, bf16[4,40,512]{2,1,0:T(8,128)(2,1)S(1)}, u32[]{:S(2)}, u32[]{:S(2)}) collective-permute-start(bf16[4,40,512]{2,1,0:T(8,128)(2,1)S(1)} %get-tuple-element.50), channel_id=1, source_target_pairs={{0,8},{4,12},{8,0},{12,4},{16,24},{20,28},{24,16},{28,20},{1,9},{5... | collective-permute-start | bytes 491528 | tf_op jit(solution)/shard_map/ppermute | solution.py:16
  88.3 10.8 %collective-permute-start.9 = (bf16[4,40,512]{2,1,0:T(8,128)(2,1)S(1)}, bf16[4,40,512]{2,1,0:T(8,128)(2,1)S(1)}, u32[]{:S(2)}, u32[]{:S(2)}) collective-permute-start(bf16[4,40,512]{2,1,0:T(8,128)(2,1)S(1)} %get-tuple-element.49), channel_id=1, source_target_pairs={{0,16},{4,20},{8,24},{12,28},{16,0},{20,4},{24,8},{28,12},{1,17},{... | collective-permute-start | bytes 491528 | tf_op jit(solution)/shard_map/ppermute | solution.py:16
  103.8 3.6 %collective-permute-start.11 = (bf16[40,512]{1,0:T(8,128)(2,1)S(1)}, bf16[40,512]{1,0:T(8,128)(2,1)S(1)}, u32[]{:S(2)}, u32[]{:S(2)}) collective-permute-start(bf16[40,512]{1,0:T(8,128)(2,1)S(1)} %get-tuple-element.53), channel_id=1, source_target_pairs={{0,1},{1,0},{2,3},{3,2},{4,5},{5,4},{6,7},{7,6},{8,9},{9,8},{10,11... | collective-permute-start | bytes 122888 | tf_op jit(solution)/shard_map/ppermute | solution.py:21
  103.9 3.8 %collective-permute-start.12 = (bf16[40,512]{1,0:T(8,128)(2,1)S(1)}, bf16[40,512]{1,0:T(8,128)(2,1)S(1)}, u32[]{:S(2)}, u32[]{:S(2)}) collective-permute-start(bf16[40,512]{1,0:T(8,128)(2,1)S(1)} %get-tuple-element.55), channel_id=1, source_target_pairs={{0,2},{1,3},{2,0},{3,1},{4,6},{5,7},{6,4},{7,5},{8,10},{9,11},{10,... | collective-permute-start | bytes 122888 | tf_op jit(solution)/shard_map/ppermute | solution.py:21
  104.7 4.8 %collective-permute-start.13 = (bf16[40,512]{1,0:T(8,128)(2,1)S(1)}, bf16[40,512]{1,0:T(8,128)(2,1)S(1)}, u32[]{:S(2)}, u32[]{:S(2)}) collective-permute-start(bf16[40,512]{1,0:T(8,128)(2,1)S(1)} %get-tuple-element.54), channel_id=1, source_target_pairs={{0,3},{1,2},{2,1},{3,0},{4,7},{5,6},{6,5},{7,4},{8,11},{9,10},{10,... | collective-permute-start | bytes 122888 | tf_op jit(solution)/shard_map/ppermute | solution.py:21
  109.6 12.7 %copy-start.9 = (s32[2048]{0:T(1024)S(1)}, s32[2048]{0:T(1024)}, u32[]{:S(2)}) copy-start(s32[2048]{0:T(1024)} %param.12) | copy-start | bytes 24580
  109.6 9.9 %collective-permute-start.14 = (bf16[32,512]{1,0:T(8,128)(2,1)S(1)}, bf16[32,512]{1,0:T(8,128)(2,1)S(1)}, u32[]{:S(2)}, u32[]{:S(2)}) collective-permute-start(bf16[32,512]{1,0:T(8,128)(2,1)S(1)} %get-tuple-element.39), channel_id=1, source_target_pairs={{0,1},{1,0},{2,3},{3,2},{4,5},{5,4},{6,7},{7,6},{8,9},{9,8},{10,11... | collective-permute-start | bytes 98312 | tf_op jit(solution)/shard_map/ppermute | solution.py:21
  110.5 9.0 %collective-permute-start.15 = (bf16[32,512]{1,0:T(8,128)(2,1)S(1)}, bf16[32,512]{1,0:T(8,128)(2,1)S(1)}, u32[]{:S(2)}, u32[]{:S(2)}) collective-permute-start(bf16[32,512]{1,0:T(8,128)(2,1)S(1)} %get-tuple-element.39), channel_id=1, source_target_pairs={{0,2},{1,3},{2,0},{3,1},{4,6},{5,7},{6,4},{7,5},{8,10},{9,11},{10,... | collective-permute-start | bytes 98312 | tf_op jit(solution)/shard_map/ppermute | solution.py:21
  112.5 7.1 %collective-permute-start.16 = (bf16[32,512]{1,0:T(8,128)(2,1)S(1)}, bf16[32,512]{1,0:T(8,128)(2,1)S(1)}, u32[]{:S(2)}, u32[]{:S(2)}) collective-permute-start(bf16[32,512]{1,0:T(8,128)(2,1)S(1)} %get-tuple-element.39), channel_id=1, source_target_pairs={{0,3},{1,2},{2,1},{3,0},{4,7},{5,6},{6,5},{7,4},{8,11},{9,10},{10,... | collective-permute-start | bytes 98312 | tf_op jit(solution)/shard_map/ppermute | solution.py:21
  113.2 32.6 %all-to-all-start.2 = ((bf16[32,64,256]{2,1,0:T(8,128)(2,1)}), bf16[32,64,256]{2,1,0:T(8,128)(2,1)S(1)}, u32[]{:S(2)}, u32[]{:S(2)}) async-start(bf16[32,64,256]{2,1,0:T(8,128)(2,1)} %bitcast.104), calls=%async_computation.2 | async-start | bytes 2097152 | tf_op jit(solution)/shard_map/all_to_all | solution.py:287
  119.6 6.5 %copy-start.8 = (bf16[512,512]{1,0:T(8,128)(2,1)S(1)}, bf16[512,512]{1,0:T(8,128)(2,1)}, u32[]{:S(2)}) copy-start(bf16[512,512]{1,0:T(8,128)(2,1)} %wp_ref.1) | copy-start | bytes 1572868
  119.6 12.2 %collective-permute-start.17 = (bf16[4,32,512]{2,1,0:T(8,128)(2,1)S(1)}, bf16[4,32,512]{2,1,0:T(8,128)(2,1)S(1)}, u32[]{:S(2)}, u32[]{:S(2)}) collective-permute-start(bf16[4,32,512]{2,1,0:T(8,128)(2,1)S(1)} %bitcast_dynamic-update-slice_fusion.4), channel_id=1, source_target_pairs={{0,8},{4,12},{8,0},{12,4},{16,24},{20,28},{24,16},{28,20},{1,9},{5... | collective-permute-start | bytes 393224 | tf_op jit(solution)/shard_map/ppermute | solution.py:16
  121.1 12.0 %collective-permute-start.18 = (bf16[4,32,512]{2,1,0:T(8,128)(2,1)S(1)}, bf16[4,32,512]{2,1,0:T(8,128)(2,1)S(1)}, u32[]{:S(2)}, u32[]{:S(2)}) collective-permute-start(bf16[4,32,512]{2,1,0:T(8,128)(2,1)S(1)} %bitcast_dynamic-update-slice_fusion.4), channel_id=1, source_target_pairs={{0,16},{4,20},{8,24},{12,28},{16,0},{20,4},{24,8},{28,12},{1,17},{... | collective-permute-start | bytes 393224 | tf_op jit(solution)/shard_map/ppermute | solution.py:16
  122.2 14.2 %collective-permute-start.19 = (bf16[4,32,512]{2,1,0:T(8,128)(2,1)S(1)}, bf16[4,32,512]{2,1,0:T(8,128)(2,1)S(1)}, u32[]{:S(2)}, u32[]{:S(2)}) collective-permute-start(bf16[4,32,512]{2,1,0:T(8,128)(2,1)S(1)} %bitcast_dynamic-update-slice_fusion.4), channel_id=1, source_target_pairs={{0,24},{4,28},{8,16},{12,20},{16,8},{20,12},{24,0},{28,4},{1,25},{... | collective-permute-start | bytes 393224 | tf_op jit(solution)/shard_map/ppermute | solution.py:16
  136.5 2.7 %collective-permute-start.20 = (bf16[4,4,32,512]{3,2,1,0:T(8,128)(2,1)S(1)}, bf16[4,4,32,512]{3,2,1,0:T(8,128)(2,1)S(1)}, u32[]{:S(2)}, u32[]{:S(2)}) collective-permute-start(bf16[4,4,32,512]{3,2,1,0:T(8,128)(2,1)S(1)} %bitcast_dynamic-update-slice_fusion), channel_id=1, source_target_pairs={{0,4},{4,0},{8,12},{12,8},{16,20},{20,16},{24,28},{28,24},{1,5},{5... | collective-permute-start | bytes 1572872 | tf_op jit(solution)/shard_map/ppermute | solution.py:16
  (5 other events, 8.1 us)

commit v4 on v3

--- a/solution.py
+++ b/solution.py
@@ -34,7 +34,7 @@
     )
 
 
-def pick(table, keys, space, limit, tile=512):
+def pick(table, keys, space, limit, tile=1024):
     length, width = table.shape
     count = keys.shape[0]
     tile = min(tile, count)
@@ -154,7 +154,7 @@
     out_ref[...] = jnp.dot(hot, rows_ref[...], preferred_element_type=jnp.float32)
 
 
-def owner_sum(keys, rows, owned, width, at, earlier=None, tile=512):
+def owner_sum(keys, rows, owned, width, at, earlier=None, tile=1024):
     count, columns = rows.shape
     tile = min(tile, owned)
     in_specs = [
@@ -278,7 +278,7 @@
     product_rows = pick(product_table, prod_at, jax.ShapeDtypeStruct, 16)
 
     gate = slot_gate(cust_count, hc_edge, hp_edge, w_cust, w_prod)
-    cut = width // 2
+    cut = width * 3 // 4
     delta, first, second = delta_and_rows(
         fetched, product_rows, gate, w_cust, (cut, width - cut)
     )
@@ -304,12 +304,11 @@
         shift_rows(lax.dynamic_index_in_dim(leaving, plane ^ k, 0, False), 2 * k)
         for k in range(1, planes)
     ]
-    got, returned = lax.optimization_barrier((got, returned))
     mine = lax.dynamic_index_in_dim(terms, plane, 0, False)
     for block in got:
         mine = mine + block.astype(jnp.float32)
     mine = fold(mine, shift_grp, grps, 1, lax.axis_index("grp"))
-    mine, second = lax.optimization_barrier((mine, second))
+    mine, returned, second = lax.optimization_barrier((mine, returned, second))
     returned_second = give_back(second)
     grad_scale = 1.0 / math.sqrt(slot_count * devices)
     share = width // devices
@@ -328,6 +327,7 @@
     own, table, prod_table_grad = lax.optimization_barrier((own, table, prod_table_grad))
     other = shift_rows(own, 1)
     cust_table_grad = owner_sum(recv_key, returned_second, owned, width, cut, table)
+    other, cust_table_grad = lax.optimization_barrier((other, cust_table_grad))
 
     def whole(share_at):
         pick_share = slice(share_at, share_at + share)

time: 150 us -> 147 us (0.980)
  waiting for transfers between devices: 67.6 us -> 59.8 us
  Pallas kernels: 29.3 us -> 31.8 us
  starting transfers between devices: 39.6 us -> 41.5 us
    all_to_all x2, waiting for transfers between devices: 9.57 us -> 0.31 us  [give_back(): lax.all_to_all(rows.reshape(devices, capacity, -1), AXES, split_axis=0, c...]
    ppermute x9, waiting for transfers between devices: 2.13 us -> 10.2 us  [shift_grp(): return lax.ppermute(value, 'grp', [(i, i ^ mask) for i in range(size)])]
    ppermute x12, waiting for transfers between devices: 36.6 us -> 29.5 us  [shift_rows(): return lax.ppermute(value, 'rows', [(i, i ^ mask) for i in range(size)])]
    pallas_call x2, Pallas kernels: 7.48 us -> 10.5 us  [owner_sum(): pl.pallas_call(owner_sum_kernel, grid=(owned // tile,), out_shape=jax.Sha...]
    ppermute x9, starting transfers between devices: 11.7 us -> 14.1 us  [shift_grp(): return lax.ppermute(value, 'grp', [(i, i ^ mask) for i in range(size)])]
    unnamed x26 -> x24, local copies, waits for them, and re-layouts: 8.15 us -> 8.15 us
  transfers between devices with their start and end apart: 24 -> 24, of which waited for: 15 -> 10; matrix products, arithmetic and copies ran while one was open for 2% -> 1% of each run, Pallas kernels for 13% -> 18%
where the time goes in v4:
time: 147 us; the launch traced here: 146 us
  waiting for transfers between devices  59.8 us (41%)
  starting transfers between devices  41.5 us (28%)
  Pallas kernels  31.8 us (22%)
  local copies, waits for them, and re-layouts  8.53 us (6%)
  other arithmetic  2.36 us (2%)
    ppermute x12, waiting for transfers between devices, shift_rows(): return lax.ppermute(value, 'rows', [(i, i ^ mask) for i in range(size)])  29.5 us
    all_to_all x1, waiting for transfers between devices, body(): lax.all_to_all(owned_rows.reshape(devices, capacity, width), AXES, split_...  19.8 us
    ppermute x9, starting transfers between devices, shift_grp(): return lax.ppermute(value, 'grp', [(i, i ^ mask) for i in range(size)])  14.1 us
    ppermute x12, starting transfers between devices, shift_rows(): return lax.ppermute(value, 'rows', [(i, i ^ mask) for i in range(size)])  11.3 us
    pallas_call x2, Pallas kernels, owner_sum(): pl.pallas_call(owner_sum_kernel, grid=(owned // tile,), out_shape=jax.Sha...  10.5 us
    ppermute x9, waiting for transfers between devices, shift_grp(): return lax.ppermute(value, 'grp', [(i, i ^ mask) for i in range(size)])  10.2 us
    all_to_all x2, starting transfers between devices, give_back(): lax.all_to_all(rows.reshape(devices, capacity, -1), AXES, split_axis=0, c...  9.03 us
    pallas_call x2, Pallas kernels, pick(): pl.pallas_call(pick_kernel, grid=(count // tile,), out_shape=space((count...  8.35 us
  transfers between devices with their start and end apart: 24, of which 10 were waited for; matrix products, arithmetic and copies ran while one was open for 1% of the time, Pallas kernels for 18%

profile of v4, /device:TPU:1, one launch (start us, length us, event | category | flops | bytes accessed | tf_op | source)
XLA Modules:
  0.0 146.3 jit_solution(3684737627948285832)
XLA Ops:
  0.6 2.2 %collective-permute-start = (bf16[8,512]{1,0:T(8,128)(2,1)}, bf16[8,512]{1,0:T(8,128)(2,1)S(1)}, u32[]{:S(2)}, u32[]{:S(2)}) collective-permute-start(bf16[8,512]{1,0:T(8,128)(2,1)} %param.15), channel_id=1, source_target_pairs={{0,1},{1,0},{2,3},{3,2},{4,5},{5,4},{6,7},{7,6},{8,9},{9,8},{10,11... | collective-permute-start | bytes 24584 | tf_op jit(solution)/shard_map/ppermute | solution.py:21
  2.8 2.3 %collective-permute-start.1 = (bf16[8,512]{1,0:T(8,128)(2,1)}, bf16[8,512]{1,0:T(8,128)(2,1)S(1)}, u32[]{:S(2)}, u32[]{:S(2)}) collective-permute-start(bf16[8,512]{1,0:T(8,128)(2,1)} %param.15), channel_id=1, source_target_pairs={{0,2},{1,3},{2,0},{3,1},{4,6},{5,7},{6,4},{7,5},{8,10},{9,11},{10,... | collective-permute-start | bytes 24584 | tf_op jit(solution)/shard_map/ppermute | solution.py:21
  5.1 7.3 %pick_rows.2 = bf16[2048,512]{1,0:T(8,128)(2,1)} custom-call(s32[1,2048]{1,0:T(1,128)} %bitcast.91, bf16[2048,512]{1,0:T(8,128)(2,1)} %table_ref.1), custom_call_target="tpu_custom_call" | custom-call | flops 4294967296 | bytes 4194304 | tf_op jit(solution)/shard_map/pick_rows/pallas_call | solution.py:41
  12.7 7.1 %all-to-all-start = ((bf16[32,64,512]{2,1,0:T(8,128)(2,1)}), bf16[32,64,512]{2,1,0:T(8,128)(2,1)}, u32[]{:S(2)}, u32[]{:S(2)}) async-start(bf16[32,64,512]{2,1,0:T(8,128)(2,1)} %bitcast.100), calls=%async_computation | async-start | bytes 4194304 | tf_op jit(solution)/shard_map/all_to_all | solution.py:270
  19.9 1.5 collective-permute-start.3
  22.6 11.4 %collective-permute-done.3 = bf16[4,8,512]{2,1,0:T(8,128)(2,1)S(1)} collective-permute-done((bf16[4,8,512]{2,1,0:T(8,128)(2,1)S(1)}, bf16[4,8,512]{2,1,0:T(8,128)(2,1)S(1)}, u32[]{:S(2)}, u32[]{:S(2)}) %collective-permute-start.3) | collective-permute-done | bytes 32800 | tf_op jit(solution)/shard_map/ppermute | solution.py:16
  34.0 2.6 %collective-permute-done.5 = bf16[4,8,512]{2,1,0:T(8,128)(2,1)S(1)} collective-permute-done((bf16[4,8,512]{2,1,0:T(8,128)(2,1)S(1)}, bf16[4,8,512]{2,1,0:T(8,128)(2,1)S(1)}, u32[]{:S(2)}, u32[]{:S(2)}) %collective-permute-start.5) | collective-permute-done | bytes 32800 | tf_op jit(solution)/shard_map/ppermute | solution.py:16
  36.7 1.5 %collective-permute-start.6 = (bf16[4,4,8,512]{3,2,1,0:T(8,128)(2,1)S(1)}, bf16[4,4,8,512]{3,2,1,0:T(8,128)(2,1)S(1)}, u32[]{:S(2)}, u32[]{:S(2)}) collective-permute-start(bf16[4,4,8,512]{3,2,1,0:T(8,128)(2,1)S(1)} %bitcast_dynamic-update-slice_fusion.8), channel_id=1, source_target_pairs={{0,4},{4,0},{8,12},{12,8},{16,20},{20,16},{24,28},{28,24},{1,5},{5... | collective-permute-start | bytes 393224 | tf_op jit(solution)/shard_map/ppermute | solution.py:16
  38.2 1.6 %copy-done.1 = bf16[2048,512]{1,0:T(8,128)(2,1)S(1)} copy-done((bf16[2048,512]{1,0:T(8,128)(2,1)S(1)}, bf16[2048,512]{1,0:T(8,128)(2,1)}, u32[]{:S(2)}) %copy-start.1) | copy-done | bytes 2097176
  39.8 4.0 %slot_gate.1.gate_ref = f32[2048,512]{1,0:T(8,128)S(1)} custom-call(s32[1,32]{1,0:T(1,128)S(1)} %copy-done.9, bf16[2048,512]{1,0:T(8,128)(2,1)S(1)} %copy-done, bf16[2048,512]{1,0:T(8,128)(2,1)S(1)} %copy-done.1, bf16[512,512]{1,0:T(8,128)(2,1)S(1)} %copy-done.6, bf16[512,512]{1,0:T(8,128)(2,1)S(1)} %copy-done.7), custom_call_target="tpu_custom_call" | custom-call | flops 2147483648 | bytes 8388608 | tf_op jit(solution)/shard_map/slot_gate/pallas_call | solution.py:77
  43.9 2.0 %copy-done.3 = f32[2048,512]{1,0:T(8,128)} copy-done((f32[2048,512]{1,0:T(8,128)}, f32[2048,512]{1,0:T(8,128)S(1)}, u32[]{:S(2)}) %copy-start.3) | copy-done | bytes 4194328
  48.3 19.8 %all-to-all-done = bf16[32,64,512]{2,1,0:T(8,128)(2,1)} async-done(((bf16[32,64,512]{2,1,0:T(8,128)(2,1)}), bf16[32,64,512]{2,1,0:T(8,128)(2,1)}, u32[]{:S(2)}, u32[]{:S(2)}) %all-to-all-start) | async-done | bytes 2097184 | tf_op jit(solution)/shard_map/all_to_all | solution.py:270
  68.1 5.8 %delta_and_rows.1 = (bf16[2048,512]{1,0:T(8,128)(2,1)}, bf16[2048,384]{1,0:T(8,128)(2,1)}, bf16[2048,128]{1,0:T(8,128)(2,1)}) custom-call(bf16[2048,512]{1,0:T(8,128)(2,1)} %bitcast.8.got_ref, bf16[2048,512]{1,0:T(8,128)(2,1)} %copy-done.5, f32[2048,512]{1,0:T(8,128)} %copy-done.3, bf16[512,512]{1,0:T(8,128)(2,1)} %weight_ref.1), custom_call_target="tpu_custom_call" | custom-call | flops 1073741824 | bytes 12582912 | tf_op jit(solution)/shard_map/delta_and_rows/pallas_call | solution.py:204
  73.9 3.4 %all-to-all-start.1 = ((bf16[32,64,384]{2,1,0:T(8,128)(2,1)}), bf16[32,64,384]{2,1,0:T(8,128)(2,1)}, u32[]{:S(2)}, u32[]{:S(2)}) async-start(bf16[32,64,384]{2,1,0:T(8,128)(2,1)} %bitcast.101), calls=%async_computation.1 | async-start | bytes 3145728 | tf_op jit(solution)/shard_map/all_to_all | solution.py:287
  77.3 1.6 %copy-done.2 = bf16[2048,512]{1,0:T(8,128)(2,1)S(1)} copy-done((bf16[2048,512]{1,0:T(8,128)(2,1)S(1)}, bf16[2048,512]{1,0:T(8,128)(2,1)}, u32[]{:S(2)}) %copy-start.2) | copy-done | bytes 2097176
  78.9 1.6 %copy-done.4 = bf16[2048,512]{1,0:T(8,128)(2,1)S(1)} copy-done((bf16[2048,512]{1,0:T(8,128)(2,1)S(1)}, bf16[2048,512]{1,0:T(8,128)(2,1)}, u32[]{:S(2)}) %copy-start.4) | copy-done | bytes 2097176
  80.5 1.5 %half_terms.3 = f32[640,512]{1,0:T(8,128)S(1)} custom-call(s32[1]{0:T(128)} %bitcast.16.half_ref, s32[1,2048]{1,0:T(1,128)S(1)} %bitcast.89, bf16[2048,512]{1,0:T(8,128)(2,1)S(1)} %copy-done, bf16[2048,512]{1,0:T(8,128)(2,1)S(1)} %copy-done.2, bf16[2048,512]{1,0:T(8,128)(2,1)S(1)} %copy-done.4), custom_call_target="tpu_custom_call" | custom-call | flops 1342177280 | bytes 4194304 | tf_op jit(solution)/shard_map/half_terms/pallas_call | solution.py:127
  82.4 1.5 %half_terms.2 = f32[640,512]{1,0:T(8,128)S(1)} custom-call(s32[1]{0:T(128)} %bitcast.half_ref, s32[1,2048]{1,0:T(1,128)S(1)} %bitcast.90, bf16[2048,512]{1,0:T(8,128)(2,1)S(1)} %copy-done, bf16[2048,512]{1,0:T(8,128)(2,1)S(1)} %copy-done.2, bf16[2048,512]{1,0:T(8,128)(2,1)S(1)} %copy-done.4), custom_call_target="tpu_custom_call" | custom-call | flops 1342177280 | bytes 4194304 | tf_op jit(solution)/shard_map/half_terms/pallas_call | solution.py:127
  85.6 2.4 %collective-permute-start.10 = (bf16[4,40,512]{2,1,0:T(8,128)(2,1)S(1)}, bf16[4,40,512]{2,1,0:T(8,128)(2,1)S(1)}, u32[]{:S(2)}, u32[]{:S(2)}) collective-permute-start(bf16[4,40,512]{2,1,0:T(8,128)(2,1)S(1)} %get-tuple-element.47), channel_id=1, source_target_pairs={{0,24},{4,28},{8,16},{12,20},{16,8},{20,12},{24,0},{28,4},{1,25},{... | collective-permute-start | bytes 491528 | tf_op jit(solution)/shard_map/ppermute | solution.py:16
  88.6 7.7 %collective-permute-done.10 = bf16[4,40,512]{2,1,0:T(8,128)(2,1)S(1)} collective-permute-done((bf16[4,40,512]{2,1,0:T(8,128)(2,1)S(1)}, bf16[4,40,512]{2,1,0:T(8,128)(2,1)S(1)}, u32[]{:S(2)}, u32[]{:S(2)}) %collective-permute-start.10) | collective-permute-done | bytes 163872 | tf_op jit(solution)/shard_map/ppermute | solution.py:16
  96.2 4.0 %collective-permute-done.8 = bf16[4,40,512]{2,1,0:T(8,128)(2,1)S(1)} collective-permute-done((bf16[4,40,512]{2,1,0:T(8,128)(2,1)S(1)}, bf16[4,40,512]{2,1,0:T(8,128)(2,1)S(1)}, u32[]{:S(2)}, u32[]{:S(2)}) %collective-permute-start.8) | collective-permute-done | bytes 163872 | tf_op jit(solution)/shard_map/ppermute | solution.py:16
  100.5 1.8 %collective-permute-start.11 = (bf16[40,512]{1,0:T(8,128)(2,1)S(1)}, bf16[40,512]{1,0:T(8,128)(2,1)S(1)}, u32[]{:S(2)}, u32[]{:S(2)}) collective-permute-start(bf16[40,512]{1,0:T(8,128)(2,1)S(1)} %get-tuple-element.51), channel_id=1, source_target_pairs={{0,1},{1,0},{2,3},{3,2},{4,5},{5,4},{6,7},{7,6},{8,9},{9,8},{10,11... | collective-permute-start | bytes 122888 | tf_op jit(solution)/shard_map/ppermute | solution.py:21
  102.2 3.8 %collective-permute-start.12 = (bf16[40,512]{1,0:T(8,128)(2,1)S(1)}, bf16[40,512]{1,0:T(8,128)(2,1)S(1)}, u32[]{:S(2)}, u32[]{:S(2)}) collective-permute-start(bf16[40,512]{1,0:T(8,128)(2,1)S(1)} %get-tuple-element.53), channel_id=1, source_target_pairs={{0,2},{1,3},{2,0},{3,1},{4,6},{5,7},{6,4},{7,5},{8,10},{9,11},{10,... | collective-permute-start | bytes 122888 | tf_op jit(solution)/shard_map/ppermute | solution.py:21
  106.3 10.2 %collective-permute-done.12 = bf16[40,512]{1,0:T(8,128)(2,1)S(1)} collective-permute-done((bf16[40,512]{1,0:T(8,128)(2,1)S(1)}, bf16[40,512]{1,0:T(8,128)(2,1)S(1)}, u32[]{:S(2)}, u32[]{:S(2)}) %collective-permute-start.12) | collective-permute-done | bytes 40992 | tf_op jit(solution)/shard_map/ppermute | solution.py:21
  116.5 1.6 %collective-permute-start.14 = (bf16[32,512]{1,0:T(8,128)(2,1)S(1)}, bf16[32,512]{1,0:T(8,128)(2,1)S(1)}, u32[]{:S(2)}, u32[]{:S(2)}) collective-permute-start(bf16[32,512]{1,0:T(8,128)(2,1)S(1)} %get-tuple-element.37), channel_id=1, source_target_pairs={{0,1},{1,0},{2,3},{3,2},{4,5},{5,4},{6,7},{7,6},{8,9},{9,8},{10,11... | collective-permute-start | bytes 98312 | tf_op jit(solution)/shard_map/ppermute | solution.py:21
  118.3 1.9 %collective-permute-start.16 = (bf16[32,512]{1,0:T(8,128)(2,1)S(1)}, bf16[32,512]{1,0:T(8,128)(2,1)S(1)}, u32[]{:S(2)}, u32[]{:S(2)}) collective-permute-start(bf16[32,512]{1,0:T(8,128)(2,1)S(1)} %get-tuple-element.37), channel_id=1, source_target_pairs={{0,3},{1,2},{2,1},{3,0},{4,7},{5,6},{6,5},{7,4},{8,11},{9,10},{10,... | collective-permute-start | bytes 98312 | tf_op jit(solution)/shard_map/ppermute | solution.py:21
  120.3 5.6 %all-to-all-start.2 = ((bf16[32,64,128]{2,1,0:T(8,128)(2,1)}), bf16[32,64,128]{2,1,0:T(8,128)(2,1)S(1)}, u32[]{:S(2)}, u32[]{:S(2)}) async-start(bf16[32,64,128]{2,1,0:T(8,128)(2,1)} %bitcast.38), calls=%async_computation.2 | async-start | bytes 1048576 | tf_op jit(solution)/shard_map/all_to_all | solution.py:287
  126.0 1.5 collective-permute-start.17
  128.7 7.2 %owner_sum.2.refs_0_ = f32[2048,512]{1,0:T(8,128)} custom-call(s32[1,2048]{1,0:T(1,128)S(1)} %bitcast.92, bf16[2048,384]{1,0:T(8,128)(2,1)} %bitcast.29.rows_ref), custom_call_target="tpu_custom_call" | custom-call | tf_op jit(solution)/shard_map/owner_sum/pallas_call | solution.py:170
  137.2 2.5 %collective-permute-done.19 = bf16[4,32,512]{2,1,0:T(8,128)(2,1)S(1)} collective-permute-done((bf16[4,32,512]{2,1,0:T(8,128)(2,1)S(1)}, bf16[4,32,512]{2,1,0:T(8,128)(2,1)S(1)}, u32[]{:S(2)}, u32[]{:S(2)}) %collective-permute-start.19) | collective-permute-done | bytes 131104 | tf_op jit(solution)/shard_map/ppermute | solution.py:16
  141.2 3.3 %owner_sum.3 = f32[2048,512]{1,0:T(8,128)} custom-call(s32[1,2048]{1,0:T(1,128)S(1)} %bitcast.93, bf16[2048,128]{1,0:T(8,128)(2,1)S(1)} %bitcast.86, f32[2048,512]{1,0:T(8,128)} %owner_sum.2.refs_0_), custom_call_target="tpu_custom_call", output_to_operand_aliasing={{}: (2, {})} | custom-call | flops 1073741824 | bytes 1572864 | tf_op jit(solution)/shard_map/owner_sum/pallas_call | solution.py:170
  144.6 1.6 %convert_multiply_fusion = (f32[2,4,4,16,512]{4,3,2,1,0:T(8,128)}, f32[2,4,4,16,512]{4,3,2,1,0:T(8,128)}) fusion(bf16[1,4,4,16,512]{4,3,2,1,0:T(8,128)(2,1)S(1)} %get-tuple-element.44, bf16[1,4,4,16,512]{4,3,2,1,0:T(8,128)(2,1)S(1)} %get-tuple-element.42, bf16[1,4,4,16,512]{4,3,2,1,0:T(8,128)(2,1)S(1)} %get-tuple-element.43, ...), kind=kLoop, calls=%fused_computation.2 | loop fusion | flops 1572864 | bytes 3145728 | tf_op jit(solution)/shard_map/mul | solution.py:337
  (83 shorter events, 11.2 us)
Async XLA Ops:
  0.6 11.9 %collective-permute-start = (bf16[8,512]{1,0:T(8,128)(2,1)}, bf16[8,512]{1,0:T(8,128)(2,1)S(1)}, u32[]{:S(2)}, u32[]{:S(2)}) collective-permute-start(bf16[8,512]{1,0:T(8,128)(2,1)} %param.15), channel_id=1, source_target_pairs={{0,1},{1,0},{2,3},{3,2},{4,5},{5,4},{6,7},{7,6},{8,9},{9,8},{10,11... | collective-permute-start | bytes 24584 | tf_op jit(solution)/shard_map/ppermute | solution.py:21
  2.8 9.7 %collective-permute-start.1 = (bf16[8,512]{1,0:T(8,128)(2,1)}, bf16[8,512]{1,0:T(8,128)(2,1)S(1)}, u32[]{:S(2)}, u32[]{:S(2)}) collective-permute-start(bf16[8,512]{1,0:T(8,128)(2,1)} %param.15), channel_id=1, source_target_pairs={{0,2},{1,3},{2,0},{3,1},{4,6},{5,7},{6,4},{7,5},{8,10},{9,11},{10,... | collective-permute-start | bytes 24584 | tf_op jit(solution)/shard_map/ppermute | solution.py:21
  5.1 7.5 %collective-permute-start.2 = (bf16[8,512]{1,0:T(8,128)(2,1)}, bf16[8,512]{1,0:T(8,128)(2,1)S(1)}, u32[]{:S(2)}, u32[]{:S(2)}) collective-permute-start(bf16[8,512]{1,0:T(8,128)(2,1)} %param.15), channel_id=1, source_target_pairs={{0,3},{1,2},{2,1},{3,0},{4,7},{5,6},{6,5},{7,4},{8,11},{9,10},{10,... | collective-permute-start | bytes 24584 | tf_op jit(solution)/shard_map/ppermute | solution.py:21
  5.1 7.4 %copy-start.10 = (bf16[8,512]{1,0:T(8,128)(2,1)S(1)}, bf16[8,512]{1,0:T(8,128)(2,1)}, u32[]{:S(2)}) copy-start(bf16[8,512]{1,0:T(8,128)(2,1)} %param.15) | copy-start | bytes 24580
  12.6 7.2 %copy-start.11 = (s32[2048]{0:T(1024)S(1)}, s32[2048]{0:T(1024)}, u32[]{:S(2)}) copy-start(s32[2048]{0:T(1024)} %param.13) | copy-start | bytes 24580
  12.6 25.6 %copy-start = (bf16[2048,512]{1,0:T(8,128)(2,1)S(1)}, bf16[2048,512]{1,0:T(8,128)(2,1)}, u32[]{:S(2)}) copy-start(bf16[2048,512]{1,0:T(8,128)(2,1)} %hc_ref.5) | copy-start | bytes 6291460
  12.6 25.6 %copy-start.6 = (bf16[512,512]{1,0:T(8,128)(2,1)S(1)}, bf16[512,512]{1,0:T(8,128)(2,1)}, u32[]{:S(2)}) copy-start(bf16[512,512]{1,0:T(8,128)(2,1)} %weight_ref.1) | copy-start | bytes 1572868
  12.6 25.6 %copy-start.7 = (bf16[512,512]{1,0:T(8,128)(2,1)S(1)}, bf16[512,512]{1,0:T(8,128)(2,1)}, u32[]{:S(2)}) copy-start(bf16[512,512]{1,0:T(8,128)(2,1)} %wp_ref.1) | copy-start | bytes 1572868
  12.7 25.5 %copy-start.9 = (s32[1,32]{1,0:T(1,128)S(1)}, s32[1,32]{1,0:T(1,128)}, u32[]{:S(2)}) copy-start(s32[1,32]{1,0:T(1,128)} %count_ref.1) | copy-start | bytes 388
  12.7 55.4 %all-to-all-start = ((bf16[32,64,512]{2,1,0:T(8,128)(2,1)}), bf16[32,64,512]{2,1,0:T(8,128)(2,1)}, u32[]{:S(2)}, u32[]{:S(2)}) async-start(bf16[32,64,512]{2,1,0:T(8,128)(2,1)} %bitcast.100), calls=%async_computation | async-start | bytes 4194304 | tf_op jit(solution)/shard_map/all_to_all | solution.py:270
  19.9 14.1 %collective-permute-start.3 = (bf16[4,8,512]{2,1,0:T(8,128)(2,1)S(1)}, bf16[4,8,512]{2,1,0:T(8,128)(2,1)S(1)}, u32[]{:S(2)}, u32[]{:S(2)}) collective-permute-start(bf16[4,8,512]{2,1,0:T(8,128)(2,1)S(1)} %bitcast_dynamic-update-slice_fusion.12), channel_id=1, source_target_pairs={{0,8},{4,12},{8,0},{12,4},{16,24},{20,28},{24,16},{28,20},{1,9},{5... | collective-permute-start | bytes 98312 | tf_op jit(solution)/shard_map/ppermute | solution.py:16
  21.3 12.7 %collective-permute-start.4 = (bf16[4,8,512]{2,1,0:T(8,128)(2,1)S(1)}, bf16[4,8,512]{2,1,0:T(8,128)(2,1)S(1)}, u32[]{:S(2)}, u32[]{:S(2)}) collective-permute-start(bf16[4,8,512]{2,1,0:T(8,128)(2,1)S(1)} %bitcast_dynamic-update-slice_fusion.12), channel_id=1, source_target_pairs={{0,16},{4,20},{8,24},{12,28},{16,0},{20,4},{24,8},{28,12},{1,17},{... | collective-permute-start | bytes 98312 | tf_op jit(solution)/shard_map/ppermute | solution.py:16
  22.5 14.2 %collective-permute-start.5 = (bf16[4,8,512]{2,1,0:T(8,128)(2,1)S(1)}, bf16[4,8,512]{2,1,0:T(8,128)(2,1)S(1)}, u32[]{:S(2)}, u32[]{:S(2)}) collective-permute-start(bf16[4,8,512]{2,1,0:T(8,128)(2,1)S(1)} %bitcast_dynamic-update-slice_fusion.12), channel_id=1, source_target_pairs={{0,24},{4,28},{8,16},{12,20},{16,8},{20,12},{24,0},{28,4},{1,25},{... | collective-permute-start | bytes 98312 | tf_op jit(solution)/shard_map/ppermute | solution.py:16
  36.7 9.2 %collective-permute-start.6 = (bf16[4,4,8,512]{3,2,1,0:T(8,128)(2,1)S(1)}, bf16[4,4,8,512]{3,2,1,0:T(8,128)(2,1)S(1)}, u32[]{:S(2)}, u32[]{:S(2)}) collective-permute-start(bf16[4,4,8,512]{3,2,1,0:T(8,128)(2,1)S(1)} %bitcast_dynamic-update-slice_fusion.8), channel_id=1, source_target_pairs={{0,4},{4,0},{8,12},{12,8},{16,20},{20,16},{24,28},{28,24},{1,5},{5... | collective-permute-start | bytes 393224 | tf_op jit(solution)/shard_map/ppermute | solution.py:16
  43.8 2.0 %copy-start.3 = (f32[2048,512]{1,0:T(8,128)}, f32[2048,512]{1,0:T(8,128)S(1)}, u32[]{:S(2)}) copy-start(f32[2048,512]{1,0:T(8,128)S(1)} %slot_gate.1.gate_ref) | copy-start | bytes 12582916
  73.9 42.6 %all-to-all-start.1 = ((bf16[32,64,384]{2,1,0:T(8,128)(2,1)}), bf16[32,64,384]{2,1,0:T(8,128)(2,1)}, u32[]{:S(2)}, u32[]{:S(2)}) async-start(bf16[32,64,384]{2,1,0:T(8,128)(2,1)} %bitcast.101), calls=%async_computation.1 | async-start | bytes 3145728 | tf_op jit(solution)/shard_map/all_to_all | solution.py:287
  82.0 3.1 %collective-permute-start.7 = (f32[640,512]{1,0:T(8,128)S(1)}, f32[640,512]{1,0:T(8,128)S(1)}, u32[]{:S(2)}, u32[]{:S(2)}) collective-permute-start(f32[640,512]{1,0:T(8,128)S(1)} %half_terms.3), channel_id=1, source_target_pairs={{0,4},{4,0},{8,12},{12,8},{16,20},{20,16},{24,28},{28,24},{1,5},{5... | collective-permute-start | bytes 3932168 | tf_op jit(solution)/shard_map/ppermute | solution.py:16
  85.6 10.6 %collective-permute-start.10 = (bf16[4,40,512]{2,1,0:T(8,128)(2,1)S(1)}, bf16[4,40,512]{2,1,0:T(8,128)(2,1)S(1)}, u32[]{:S(2)}, u32[]{:S(2)}) collective-permute-start(bf16[4,40,512]{2,1,0:T(8,128)(2,1)S(1)} %get-tuple-element.47), channel_id=1, source_target_pairs={{0,24},{4,28},{8,16},{12,20},{16,8},{20,12},{24,0},{28,4},{1,25},{... | collective-permute-start | bytes 491528 | tf_op jit(solution)/shard_map/ppermute | solution.py:16
  88.0 12.3 %collective-permute-start.8 = (bf16[4,40,512]{2,1,0:T(8,128)(2,1)S(1)}, bf16[4,40,512]{2,1,0:T(8,128)(2,1)S(1)}, u32[]{:S(2)}, u32[]{:S(2)}) collective-permute-start(bf16[4,40,512]{2,1,0:T(8,128)(2,1)S(1)} %get-tuple-element.46), channel_id=1, source_target_pairs={{0,8},{4,12},{8,0},{12,4},{16,24},{20,28},{24,16},{28,20},{1,9},{5... | collective-permute-start | bytes 491528 | tf_op jit(solution)/shard_map/ppermute | solution.py:16
  88.3 12.1 %collective-permute-start.9 = (bf16[4,40,512]{2,1,0:T(8,128)(2,1)S(1)}, bf16[4,40,512]{2,1,0:T(8,128)(2,1)S(1)}, u32[]{:S(2)}, u32[]{:S(2)}) collective-permute-start(bf16[4,40,512]{2,1,0:T(8,128)(2,1)S(1)} %get-tuple-element.48), channel_id=1, source_target_pairs={{0,16},{4,20},{8,24},{12,28},{16,0},{20,4},{24,8},{28,12},{1,17},{... | collective-permute-start | bytes 491528 | tf_op jit(solution)/shard_map/ppermute | solution.py:16
  100.4 28.3 %copy-start.8 = (s32[2048]{0:T(1024)S(1)}, s32[2048]{0:T(1024)}, u32[]{:S(2)}) copy-start(s32[2048]{0:T(1024)} %param.12) | copy-start | bytes 24580
  100.5 5.8 %collective-permute-start.11 = (bf16[40,512]{1,0:T(8,128)(2,1)S(1)}, bf16[40,512]{1,0:T(8,128)(2,1)S(1)}, u32[]{:S(2)}, u32[]{:S(2)}) collective-permute-start(bf16[40,512]{1,0:T(8,128)(2,1)S(1)} %get-tuple-element.51), channel_id=1, source_target_pairs={{0,1},{1,0},{2,3},{3,2},{4,5},{5,4},{6,7},{7,6},{8,9},{9,8},{10,11... | collective-permute-start | bytes 122888 | tf_op jit(solution)/shard_map/ppermute | solution.py:21
  102.2 14.2 %collective-permute-start.12 = (bf16[40,512]{1,0:T(8,128)(2,1)S(1)}, bf16[40,512]{1,0:T(8,128)(2,1)S(1)}, u32[]{:S(2)}, u32[]{:S(2)}) collective-permute-start(bf16[40,512]{1,0:T(8,128)(2,1)S(1)} %get-tuple-element.53), channel_id=1, source_target_pairs={{0,2},{1,3},{2,0},{3,1},{4,6},{5,7},{6,4},{7,5},{8,10},{9,11},{10,... | collective-permute-start | bytes 122888 | tf_op jit(solution)/shard_map/ppermute | solution.py:21
  106.0 10.4 %collective-permute-start.13 = (bf16[40,512]{1,0:T(8,128)(2,1)S(1)}, bf16[40,512]{1,0:T(8,128)(2,1)S(1)}, u32[]{:S(2)}, u32[]{:S(2)}) collective-permute-start(bf16[40,512]{1,0:T(8,128)(2,1)S(1)} %get-tuple-element.52), channel_id=1, source_target_pairs={{0,3},{1,2},{2,1},{3,0},{4,7},{5,6},{6,5},{7,4},{8,11},{9,10},{10,... | collective-permute-start | bytes 122888 | tf_op jit(solution)/shard_map/ppermute | solution.py:21
  116.5 9.4 %collective-permute-start.14 = (bf16[32,512]{1,0:T(8,128)(2,1)S(1)}, bf16[32,512]{1,0:T(8,128)(2,1)S(1)}, u32[]{:S(2)}, u32[]{:S(2)}) collective-permute-start(bf16[32,512]{1,0:T(8,128)(2,1)S(1)} %get-tuple-element.37), channel_id=1, source_target_pairs={{0,1},{1,0},{2,3},{3,2},{4,5},{5,4},{6,7},{7,6},{8,9},{9,8},{10,11... | collective-permute-start | bytes 98312 | tf_op jit(solution)/shard_map/ppermute | solution.py:21
  118.1 7.8 %collective-permute-start.15 = (bf16[32,512]{1,0:T(8,128)(2,1)S(1)}, bf16[32,512]{1,0:T(8,128)(2,1)S(1)}, u32[]{:S(2)}, u32[]{:S(2)}) collective-permute-start(bf16[32,512]{1,0:T(8,128)(2,1)S(1)} %get-tuple-element.37), channel_id=1, source_target_pairs={{0,2},{1,3},{2,0},{3,1},{4,6},{5,7},{6,4},{7,5},{8,10},{9,11},{10,... | collective-permute-start | bytes 98312 | tf_op jit(solution)/shard_map/ppermute | solution.py:21
  118.3 7.7 %collective-permute-start.16 = (bf16[32,512]{1,0:T(8,128)(2,1)S(1)}, bf16[32,512]{1,0:T(8,128)(2,1)S(1)}, u32[]{:S(2)}, u32[]{:S(2)}) collective-permute-start(bf16[32,512]{1,0:T(8,128)(2,1)S(1)} %get-tuple-element.37), channel_id=1, source_target_pairs={{0,3},{1,2},{2,1},{3,0},{4,7},{5,6},{6,5},{7,4},{8,11},{9,10},{10,... | collective-permute-start | bytes 98312 | tf_op jit(solution)/shard_map/ppermute | solution.py:21
  120.3 20.9 %all-to-all-start.2 = ((bf16[32,64,128]{2,1,0:T(8,128)(2,1)}), bf16[32,64,128]{2,1,0:T(8,128)(2,1)S(1)}, u32[]{:S(2)}, u32[]{:S(2)}) async-start(bf16[32,64,128]{2,1,0:T(8,128)(2,1)} %bitcast.38), calls=%async_computation.2 | async-start | bytes 1048576 | tf_op jit(solution)/shard_map/all_to_all | solution.py:287
  126.0 11.1 %collective-permute-start.17 = (bf16[4,32,512]{2,1,0:T(8,128)(2,1)S(1)}, bf16[4,32,512]{2,1,0:T(8,128)(2,1)S(1)}, u32[]{:S(2)}, u32[]{:S(2)}) collective-permute-start(bf16[4,32,512]{2,1,0:T(8,128)(2,1)S(1)} %bitcast_dynamic-update-slice_fusion.4), channel_id=1, source_target_pairs={{0,8},{4,12},{8,0},{12,4},{16,24},{20,28},{24,16},{28,20},{1,9},{5... | collective-permute-start | bytes 393224 | tf_op jit(solution)/shard_map/ppermute | solution.py:16
  127.5 9.7 %collective-permute-start.18 = (bf16[4,32,512]{2,1,0:T(8,128)(2,1)S(1)}, bf16[4,32,512]{2,1,0:T(8,128)(2,1)S(1)}, u32[]{:S(2)}, u32[]{:S(2)}) collective-permute-start(bf16[4,32,512]{2,1,0:T(8,128)(2,1)S(1)} %bitcast_dynamic-update-slice_fusion.4), channel_id=1, source_target_pairs={{0,16},{4,20},{8,24},{12,28},{16,0},{20,4},{24,8},{28,12},{1,17},{... | collective-permute-start | bytes 393224 | tf_op jit(solution)/shard_map/ppermute | solution.py:16
  128.7 11.1 %collective-permute-start.19 = (bf16[4,32,512]{2,1,0:T(8,128)(2,1)S(1)}, bf16[4,32,512]{2,1,0:T(8,128)(2,1)S(1)}, u32[]{:S(2)}, u32[]{:S(2)}) collective-permute-start(bf16[4,32,512]{2,1,0:T(8,128)(2,1)S(1)} %bitcast_dynamic-update-slice_fusion.4), channel_id=1, source_target_pairs={{0,24},{4,28},{8,16},{12,20},{16,8},{20,12},{24,0},{28,4},{1,25},{... | collective-permute-start | bytes 393224 | tf_op jit(solution)/shard_map/ppermute | solution.py:16
  139.7 4.8 %collective-permute-start.20 = (bf16[4,4,32,512]{3,2,1,0:T(8,128)(2,1)S(1)}, bf16[4,4,32,512]{3,2,1,0:T(8,128)(2,1)S(1)}, u32[]{:S(2)}, u32[]{:S(2)}) collective-permute-start(bf16[4,4,32,512]{3,2,1,0:T(8,128)(2,1)S(1)} %bitcast_dynamic-update-slice_fusion), channel_id=1, source_target_pairs={{0,4},{4,0},{8,12},{12,8},{16,20},{20,16},{24,28},{28,24},{1,5},{5... | collective-permute-start | bytes 1572872 | tf_op jit(solution)/shard_map/ppermute | solution.py:16
  (4 other events, 6.1 us)

commit v5 on v4

--- a/solution.py
+++ b/solution.py
@@ -307,16 +307,33 @@
     mine = lax.dynamic_index_in_dim(terms, plane, 0, False)
     for block in got:
         mine = mine + block.astype(jnp.float32)
-    mine = fold(mine, shift_grp, grps, 1, lax.axis_index("grp"))
-    mine, returned, second = lax.optimization_barrier((mine, returned, second))
+    here = lax.axis_index("grp")
+    sums, weights = mine[:, :product_count], mine[:, product_count:].astype(jnp.bfloat16)
+    every = weights.reshape(-1, width)
+    own_sum = lax.dynamic_index_in_dim(sums, here, 0, False)
+    blocks = [
+        shift_grp(
+            jnp.concatenate(
+                [lax.dynamic_index_in_dim(sums, here ^ k, 0, False).astype(jnp.bfloat16), every]
+            ),
+            k,
+        )
+        for k in range(1, grps)
+    ]
+    blocks, returned = lax.optimization_barrier((blocks, returned))
+    terms = [weights.astype(jnp.float32)]
+    for block in blocks:
+        own_sum = own_sum + block[:product_count].astype(jnp.float32)
+        terms.append(block[product_count:].astype(jnp.float32).reshape(weights.shape))
+    while len(terms) > 1:
+        terms = [a + b for a, b in zip(terms[::2], terms[1::2])]
+    own = terms[0].astype(jnp.bfloat16)
     returned_second = give_back(second)
     grad_scale = 1.0 / math.sqrt(slot_count * devices)
     share = width // devices
     owned = cust_grad.shape[0]
-    own = gather_grp(mine[product_count:].astype(jnp.bfloat16))
-    own, mine, returned = lax.optimization_barrier((own, mine, returned))
     prod_table_grad = lax.dot_general(
-        mine[:product_count],
+        own_sum,
         w_prod.astype(jnp.float32),
         (((1,), (1,)), ((), ())),
         precision=lax.Precision.HIGHEST,

time: 147 us -> 145 us (0.986)
  starting transfers between devices: 41.5 us -> 35.4 us
  waiting for transfers between devices: 59.8 us -> 64 us
    all_to_all x2, waiting for transfers between devices: 0.31 us -> 14.7 us  [give_back(): lax.all_to_all(rows.reshape(devices, capacity, -1), AXES, split_axis=0, c...]
    ppermute x9 -> x6, waiting for transfers between devices: 10.2 us -> 0.02 us  [shift_grp(): return lax.ppermute(value, 'grp', [(i, i ^ mask) for i in range(size)])]
    ppermute x9 -> x6, starting transfers between devices: 14.1 us -> 10.3 us  [shift_grp(): return lax.ppermute(value, 'grp', [(i, i ^ mask) for i in range(size)])]
    all_to_all x2, starting transfers between devices: 9.03 us -> 6.67 us  [give_back(): lax.all_to_all(rows.reshape(devices, capacity, -1), AXES, split_axis=0, c...]
  transfers between devices with their start and end apart: 24 -> 21, of which waited for: 10 -> 10; matrix products, arithmetic and copies ran while one was open for 1% -> 2% of each run, Pallas kernels for 18% -> 18%
where the time goes in v5:
time: 145 us; the launch traced here: 144 us
  waiting for transfers between devices  64 us (44%)
  starting transfers between devices  35.4 us (24%)
  Pallas kernels  31.8 us (22%)
  local copies, waits for them, and re-layouts  8.47 us (6%)
  other arithmetic  2.45 us (2%)
    ppermute x12, waiting for transfers between devices, shift_rows(): return lax.ppermute(value, 'rows', [(i, i ^ mask) for i in range(size)])  29.4 us
    all_to_all x1, waiting for transfers between devices, body(): lax.all_to_all(owned_rows.reshape(devices, capacity, width), AXES, split_...  19.8 us
    all_to_all x2, waiting for transfers between devices, give_back(): lax.all_to_all(rows.reshape(devices, capacity, -1), AXES, split_axis=0, c...  14.7 us
    ppermute x12, starting transfers between devices, shift_rows(): return lax.ppermute(value, 'rows', [(i, i ^ mask) for i in range(size)])  11.3 us
    pallas_call x2, Pallas kernels, owner_sum(): pl.pallas_call(owner_sum_kernel, grid=(owned // tile,), out_shape=jax.Sha...  10.5 us
    ppermute x6, starting transfers between devices, shift_grp(): return lax.ppermute(value, 'grp', [(i, i ^ mask) for i in range(size)])  10.3 us
    pallas_call x2, Pallas kernels, pick(): pl.pallas_call(pick_kernel, grid=(count // tile,), out_shape=space((count...  8.38 us
    unnamed x24, local copies, waits for them, and re-layouts  8.13 us
  transfers between devices with their start and end apart: 21, of which 10 were waited for; matrix products, arithmetic and copies ran while one was open for 2% of the time, Pallas kernels for 18%

profile of v5, /device:TPU:1, one launch (start us, length us, event | category | flops | bytes accessed | tf_op | source)
XLA Modules:
  0.0 144.3 jit_solution(2569465772129570832)
XLA Ops:
  0.6 2.2 %collective-permute-start = (bf16[8,512]{1,0:T(8,128)(2,1)}, bf16[8,512]{1,0:T(8,128)(2,1)S(1)}, u32[]{:S(2)}, u32[]{:S(2)}) collective-permute-start(bf16[8,512]{1,0:T(8,128)(2,1)} %param.15), channel_id=1, source_target_pairs={{0,1},{1,0},{2,3},{3,2},{4,5},{5,4},{6,7},{7,6},{8,9},{9,8},{10,11... | collective-permute-start | bytes 24584 | tf_op jit(solution)/shard_map/ppermute | solution.py:21
  2.8 2.3 %collective-permute-start.1 = (bf16[8,512]{1,0:T(8,128)(2,1)}, bf16[8,512]{1,0:T(8,128)(2,1)S(1)}, u32[]{:S(2)}, u32[]{:S(2)}) collective-permute-start(bf16[8,512]{1,0:T(8,128)(2,1)} %param.15), channel_id=1, source_target_pairs={{0,2},{1,3},{2,0},{3,1},{4,6},{5,7},{6,4},{7,5},{8,10},{9,11},{10,... | collective-permute-start | bytes 24584 | tf_op jit(solution)/shard_map/ppermute | solution.py:21
  5.1 7.4 %pick_rows.2 = bf16[2048,512]{1,0:T(8,128)(2,1)} custom-call(s32[1,2048]{1,0:T(1,128)} %bitcast.87, bf16[2048,512]{1,0:T(8,128)(2,1)} %table_ref.1), custom_call_target="tpu_custom_call" | custom-call | flops 4294967296 | bytes 4194304 | tf_op jit(solution)/shard_map/pick_rows/pallas_call | solution.py:41
  12.7 7.1 %all-to-all-start = ((bf16[32,64,512]{2,1,0:T(8,128)(2,1)}), bf16[32,64,512]{2,1,0:T(8,128)(2,1)}, u32[]{:S(2)}, u32[]{:S(2)}) async-start(bf16[32,64,512]{2,1,0:T(8,128)(2,1)} %bitcast.96), calls=%async_computation | async-start | bytes 4194304 | tf_op jit(solution)/shard_map/all_to_all | solution.py:270
  19.9 1.5 %collective-permute-start.3 = (bf16[4,8,512]{2,1,0:T(8,128)(2,1)S(1)}, bf16[4,8,512]{2,1,0:T(8,128)(2,1)S(1)}, u32[]{:S(2)}, u32[]{:S(2)}) collective-permute-start(bf16[4,8,512]{2,1,0:T(8,128)(2,1)S(1)} %bitcast_dynamic-update-slice_fusion.8), channel_id=1, source_target_pairs={{0,8},{4,12},{8,0},{12,4},{16,24},{20,28},{24,16},{28,20},{1,9},{5... | collective-permute-start | bytes 98312 | tf_op jit(solution)/shard_map/ppermute | solution.py:16
  22.6 11.4 %collective-permute-done.3 = bf16[4,8,512]{2,1,0:T(8,128)(2,1)S(1)} collective-permute-done((bf16[4,8,512]{2,1,0:T(8,128)(2,1)S(1)}, bf16[4,8,512]{2,1,0:T(8,128)(2,1)S(1)}, u32[]{:S(2)}, u32[]{:S(2)}) %collective-permute-start.3) | collective-permute-done | bytes 32800 | tf_op jit(solution)/shard_map/ppermute | solution.py:16
  34.1 2.6 %collective-permute-done.5 = bf16[4,8,512]{2,1,0:T(8,128)(2,1)S(1)} collective-permute-done((bf16[4,8,512]{2,1,0:T(8,128)(2,1)S(1)}, bf16[4,8,512]{2,1,0:T(8,128)(2,1)S(1)}, u32[]{:S(2)}, u32[]{:S(2)}) %collective-permute-start.5) | collective-permute-done | bytes 32800 | tf_op jit(solution)/shard_map/ppermute | solution.py:16
  36.7 1.5 %collective-permute-start.6 = (bf16[4,4,8,512]{3,2,1,0:T(8,128)(2,1)S(1)}, bf16[4,4,8,512]{3,2,1,0:T(8,128)(2,1)S(1)}, u32[]{:S(2)}, u32[]{:S(2)}) collective-permute-start(bf16[4,4,8,512]{3,2,1,0:T(8,128)(2,1)S(1)} %bitcast_dynamic-update-slice_fusion.4), channel_id=1, source_target_pairs={{0,4},{4,0},{8,12},{12,8},{16,20},{20,16},{24,28},{28,24},{1,5},{5... | collective-permute-start | bytes 393224 | tf_op jit(solution)/shard_map/ppermute | solution.py:16
  38.2 1.6 %copy-done.1 = bf16[2048,512]{1,0:T(8,128)(2,1)S(1)} copy-done((bf16[2048,512]{1,0:T(8,128)(2,1)S(1)}, bf16[2048,512]{1,0:T(8,128)(2,1)}, u32[]{:S(2)}) %copy-start.1) | copy-done | bytes 2097176
  39.8 4.0 %slot_gate.1.gate_ref = f32[2048,512]{1,0:T(8,128)S(1)} custom-call(s32[1,32]{1,0:T(1,128)S(1)} %copy-done.9, bf16[2048,512]{1,0:T(8,128)(2,1)S(1)} %copy-done, bf16[2048,512]{1,0:T(8,128)(2,1)S(1)} %copy-done.1, bf16[512,512]{1,0:T(8,128)(2,1)S(1)} %copy-done.6, bf16[512,512]{1,0:T(8,128)(2,1)S(1)} %copy-done.7), custom_call_target="tpu_custom_call" | custom-call | flops 2147483648 | bytes 8388608 | tf_op jit(solution)/shard_map/slot_gate/pallas_call | solution.py:77
  43.9 2.0 %copy-done.3 = f32[2048,512]{1,0:T(8,128)} copy-done((f32[2048,512]{1,0:T(8,128)}, f32[2048,512]{1,0:T(8,128)S(1)}, u32[]{:S(2)}) %copy-start.3) | copy-done | bytes 4194328
  47.0 1.3 copy-done.5
  48.3 19.8 %all-to-all-done = bf16[32,64,512]{2,1,0:T(8,128)(2,1)} async-done(((bf16[32,64,512]{2,1,0:T(8,128)(2,1)}), bf16[32,64,512]{2,1,0:T(8,128)(2,1)}, u32[]{:S(2)}, u32[]{:S(2)}) %all-to-all-start) | async-done | bytes 2097184 | tf_op jit(solution)/shard_map/all_to_all | solution.py:270
  68.1 5.8 %delta_and_rows.1 = (bf16[2048,512]{1,0:T(8,128)(2,1)}, bf16[2048,384]{1,0:T(8,128)(2,1)}, bf16[2048,128]{1,0:T(8,128)(2,1)}) custom-call(bf16[2048,512]{1,0:T(8,128)(2,1)} %bitcast.8.got_ref, bf16[2048,512]{1,0:T(8,128)(2,1)} %copy-done.5, f32[2048,512]{1,0:T(8,128)} %copy-done.3, bf16[512,512]{1,0:T(8,128)(2,1)} %weight_ref.1), custom_call_target="tpu_custom_call" | custom-call | flops 1073741824 | bytes 12582912 | tf_op jit(solution)/shard_map/delta_and_rows/pallas_call | solution.py:204
  73.9 3.4 %all-to-all-start.1 = ((bf16[32,64,384]{2,1,0:T(8,128)(2,1)}), bf16[32,64,384]{2,1,0:T(8,128)(2,1)}, u32[]{:S(2)}, u32[]{:S(2)}) async-start(bf16[32,64,384]{2,1,0:T(8,128)(2,1)} %bitcast.97), calls=%async_computation.1 | async-start | bytes 3145728 | tf_op jit(solution)/shard_map/all_to_all | solution.py:287
  77.3 1.6 %copy-done.2 = bf16[2048,512]{1,0:T(8,128)(2,1)S(1)} copy-done((bf16[2048,512]{1,0:T(8,128)(2,1)S(1)}, bf16[2048,512]{1,0:T(8,128)(2,1)}, u32[]{:S(2)}) %copy-start.2) | copy-done | bytes 2097176
  78.9 1.6 %copy-done.4 = bf16[2048,512]{1,0:T(8,128)(2,1)S(1)} copy-done((bf16[2048,512]{1,0:T(8,128)(2,1)S(1)}, bf16[2048,512]{1,0:T(8,128)(2,1)}, u32[]{:S(2)}) %copy-start.4) | copy-done | bytes 2097176
  80.5 1.5 %half_terms.3 = f32[640,512]{1,0:T(8,128)S(1)} custom-call(s32[1]{0:T(128)} %bitcast.16.half_ref, s32[1,2048]{1,0:T(1,128)S(1)} %bitcast.85, bf16[2048,512]{1,0:T(8,128)(2,1)S(1)} %copy-done, bf16[2048,512]{1,0:T(8,128)(2,1)S(1)} %copy-done.2, bf16[2048,512]{1,0:T(8,128)(2,1)S(1)} %copy-done.4), custom_call_target="tpu_custom_call" | custom-call | flops 1342177280 | bytes 4194304 | tf_op jit(solution)/shard_map/half_terms/pallas_call | solution.py:127
  82.4 1.5 %half_terms.2 = f32[640,512]{1,0:T(8,128)S(1)} custom-call(s32[1]{0:T(128)} %bitcast.half_ref, s32[1,2048]{1,0:T(1,128)S(1)} %bitcast.86, bf16[2048,512]{1,0:T(8,128)(2,1)S(1)} %copy-done, bf16[2048,512]{1,0:T(8,128)(2,1)S(1)} %copy-done.2, bf16[2048,512]{1,0:T(8,128)(2,1)S(1)} %copy-done.4), custom_call_target="tpu_custom_call" | custom-call | flops 1342177280 | bytes 4194304 | tf_op jit(solution)/shard_map/half_terms/pallas_call | solution.py:127
  85.7 2.4 %collective-permute-start.10 = (bf16[4,40,512]{2,1,0:T(8,128)(2,1)S(1)}, bf16[4,40,512]{2,1,0:T(8,128)(2,1)S(1)}, u32[]{:S(2)}, u32[]{:S(2)}) collective-permute-start(bf16[4,40,512]{2,1,0:T(8,128)(2,1)S(1)} %get-tuple-element.41), channel_id=1, source_target_pairs={{0,24},{4,28},{8,16},{12,20},{16,8},{20,12},{24,0},{28,4},{1,25},{... | collective-permute-start | bytes 491528 | tf_op jit(solution)/shard_map/ppermute | solution.py:16
  88.6 7.7 %collective-permute-done.10 = bf16[4,40,512]{2,1,0:T(8,128)(2,1)S(1)} collective-permute-done((bf16[4,40,512]{2,1,0:T(8,128)(2,1)S(1)}, bf16[4,40,512]{2,1,0:T(8,128)(2,1)S(1)}, u32[]{:S(2)}, u32[]{:S(2)}) %collective-permute-start.10) | collective-permute-done | bytes 163872 | tf_op jit(solution)/shard_map/ppermute | solution.py:16
  96.3 4.0 %collective-permute-done.8 = bf16[4,40,512]{2,1,0:T(8,128)(2,1)S(1)} collective-permute-done((bf16[4,40,512]{2,1,0:T(8,128)(2,1)S(1)}, bf16[4,40,512]{2,1,0:T(8,128)(2,1)S(1)}, u32[]{:S(2)}, u32[]{:S(2)}) %collective-permute-start.8) | collective-permute-done | bytes 163872 | tf_op jit(solution)/shard_map/ppermute | solution.py:16
  100.6 1.8 %collective-permute-start.11 = (bf16[136,512]{1,0:T(8,128)(2,1)S(1)}, bf16[136,512]{1,0:T(8,128)(2,1)S(1)}, u32[]{:S(2)}, u32[]{:S(2)}) collective-permute-start(bf16[136,512]{1,0:T(8,128)(2,1)S(1)} %get-tuple-element.47), channel_id=1, source_target_pairs={{0,1},{1,0},{2,3},{3,2},{4,5},{5,4},{6,7},{7,6},{8,9},{9,8},{10,11... | collective-permute-start | bytes 417800 | tf_op jit(solution)/shard_map/ppermute | solution.py:21
  102.3 3.8 %collective-permute-start.12 = (bf16[136,512]{1,0:T(8,128)(2,1)S(1)}, bf16[136,512]{1,0:T(8,128)(2,1)S(1)}, u32[]{:S(2)}, u32[]{:S(2)}) collective-permute-start(bf16[136,512]{1,0:T(8,128)(2,1)S(1)} %get-tuple-element.46), channel_id=1, source_target_pairs={{0,2},{1,3},{2,0},{3,1},{4,6},{5,7},{6,4},{7,5},{8,10},{9,11},{10,... | collective-permute-start | bytes 417800 | tf_op jit(solution)/shard_map/ppermute | solution.py:21
  106.3 14.3 %all-to-all-done.1 = bf16[32,64,384]{2,1,0:T(8,128)(2,1)} async-done(((bf16[32,64,384]{2,1,0:T(8,128)(2,1)}), bf16[32,64,384]{2,1,0:T(8,128)(2,1)}, u32[]{:S(2)}, u32[]{:S(2)}) %all-to-all-start.1) | async-done | bytes 1572896 | tf_op jit(solution)/shard_map/all_to_all | solution.py:287
  120.7 3.3 %all-to-all-start.2 = ((bf16[32,64,128]{2,1,0:T(8,128)(2,1)}), bf16[32,64,128]{2,1,0:T(8,128)(2,1)S(1)}, u32[]{:S(2)}, u32[]{:S(2)}) async-start(bf16[32,64,128]{2,1,0:T(8,128)(2,1)} %bitcast.37), calls=%async_computation.2 | async-start | bytes 1048576 | tf_op jit(solution)/shard_map/all_to_all | solution.py:287
  124.2 1.5 %collective-permute-start.14 = (bf16[4,32,512]{2,1,0:T(8,128)(2,1)S(1)}, bf16[4,32,512]{2,1,0:T(8,128)(2,1)S(1)}, u32[]{:S(2)}, u32[]{:S(2)}) collective-permute-start(bf16[4,32,512]{2,1,0:T(8,128)(2,1)S(1)} %get-tuple-element.33), channel_id=1, source_target_pairs={{0,8},{4,12},{8,0},{12,4},{16,24},{20,28},{24,16},{28,20},{1,9},{5... | collective-permute-start | bytes 393224 | tf_op jit(solution)/shard_map/ppermute | solution.py:16
  126.9 7.2 %owner_sum.2.refs_0_ = f32[2048,512]{1,0:T(8,128)} custom-call(s32[1,2048]{1,0:T(1,128)S(1)} %bitcast.88, bf16[2048,384]{1,0:T(8,128)(2,1)} %bitcast.29.rows_ref), custom_call_target="tpu_custom_call" | custom-call | tf_op jit(solution)/shard_map/owner_sum/pallas_call | solution.py:170
  135.3 2.4 %collective-permute-done.16 = bf16[4,32,512]{2,1,0:T(8,128)(2,1)S(1)} collective-permute-done((bf16[4,32,512]{2,1,0:T(8,128)(2,1)S(1)}, bf16[4,32,512]{2,1,0:T(8,128)(2,1)S(1)}, u32[]{:S(2)}, u32[]{:S(2)}) %collective-permute-start.16) | collective-permute-done | bytes 131104 | tf_op jit(solution)/shard_map/ppermute | solution.py:16
  137.8 1.2 collective-permute-start.17
  139.3 3.3 %owner_sum.3 = f32[2048,512]{1,0:T(8,128)} custom-call(s32[1,2048]{1,0:T(1,128)S(1)} %bitcast.89, bf16[2048,128]{1,0:T(8,128)(2,1)S(1)} %bitcast.82, f32[2048,512]{1,0:T(8,128)} %owner_sum.2.refs_0_), custom_call_target="tpu_custom_call", output_to_operand_aliasing={{}: (2, {})} | custom-call | flops 1073741824 | bytes 1572864 | tf_op jit(solution)/shard_map/owner_sum/pallas_call | solution.py:170
  142.7 1.6 %convert_multiply_fusion = (f32[2,4,4,16,512]{4,3,2,1,0:T(8,128)}, f32[2,4,4,16,512]{4,3,2,1,0:T(8,128)}) fusion(bf16[1,4,4,16,512]{4,3,2,1,0:T(8,128)(2,1)S(1)} %get-tuple-element.38, bf16[1,4,4,16,512]{4,3,2,1,0:T(8,128)(2,1)S(1)} %get-tuple-element.36, bf16[1,4,4,16,512]{4,3,2,1,0:T(8,128)(2,1)S(1)} %get-tuple-element.37, ...), kind=kLoop, calls=%fused_computation.2 | loop fusion | flops 1572864 | bytes 3145728 | tf_op jit(solution)/shard_map/mul | solution.py:354
  (76 shorter events, 8.6 us)
Async XLA Ops:
  0.6 11.9 %collective-permute-start = (bf16[8,512]{1,0:T(8,128)(2,1)}, bf16[8,512]{1,0:T(8,128)(2,1)S(1)}, u32[]{:S(2)}, u32[]{:S(2)}) collective-permute-start(bf16[8,512]{1,0:T(8,128)(2,1)} %param.15), channel_id=1, source_target_pairs={{0,1},{1,0},{2,3},{3,2},{4,5},{5,4},{6,7},{7,6},{8,9},{9,8},{10,11... | collective-permute-start | bytes 24584 | tf_op jit(solution)/shard_map/ppermute | solution.py:21
  2.8 9.8 %collective-permute-start.1 = (bf16[8,512]{1,0:T(8,128)(2,1)}, bf16[8,512]{1,0:T(8,128)(2,1)S(1)}, u32[]{:S(2)}, u32[]{:S(2)}) collective-permute-start(bf16[8,512]{1,0:T(8,128)(2,1)} %param.15), channel_id=1, source_target_pairs={{0,2},{1,3},{2,0},{3,1},{4,6},{5,7},{6,4},{7,5},{8,10},{9,11},{10,... | collective-permute-start | bytes 24584 | tf_op jit(solution)/shard_map/ppermute | solution.py:21
  5.1 7.5 %collective-permute-start.2 = (bf16[8,512]{1,0:T(8,128)(2,1)}, bf16[8,512]{1,0:T(8,128)(2,1)S(1)}, u32[]{:S(2)}, u32[]{:S(2)}) collective-permute-start(bf16[8,512]{1,0:T(8,128)(2,1)} %param.15), channel_id=1, source_target_pairs={{0,3},{1,2},{2,1},{3,0},{4,7},{5,6},{6,5},{7,4},{8,11},{9,10},{10,... | collective-permute-start | bytes 24584 | tf_op jit(solution)/shard_map/ppermute | solution.py:21
  5.1 7.4 %copy-start.10 = (bf16[8,512]{1,0:T(8,128)(2,1)S(1)}, bf16[8,512]{1,0:T(8,128)(2,1)}, u32[]{:S(2)}) copy-start(bf16[8,512]{1,0:T(8,128)(2,1)} %param.15) | copy-start | bytes 24580
  12.6 7.2 %copy-start.11 = (s32[2048]{0:T(1024)S(1)}, s32[2048]{0:T(1024)}, u32[]{:S(2)}) copy-start(s32[2048]{0:T(1024)} %param.13) | copy-start | bytes 24580
  12.6 25.6 %copy-start = (bf16[2048,512]{1,0:T(8,128)(2,1)S(1)}, bf16[2048,512]{1,0:T(8,128)(2,1)}, u32[]{:S(2)}) copy-start(bf16[2048,512]{1,0:T(8,128)(2,1)} %hc_ref.5) | copy-start | bytes 6291460
  12.7 25.6 %copy-start.6 = (bf16[512,512]{1,0:T(8,128)(2,1)S(1)}, bf16[512,512]{1,0:T(8,128)(2,1)}, u32[]{:S(2)}) copy-start(bf16[512,512]{1,0:T(8,128)(2,1)} %weight_ref.1) | copy-start | bytes 1572868
  12.7 25.6 %copy-start.7 = (bf16[512,512]{1,0:T(8,128)(2,1)S(1)}, bf16[512,512]{1,0:T(8,128)(2,1)}, u32[]{:S(2)}) copy-start(bf16[512,512]{1,0:T(8,128)(2,1)} %wp_ref.1) | copy-start | bytes 1572868
  12.7 25.5 %copy-start.9 = (s32[1,32]{1,0:T(1,128)S(1)}, s32[1,32]{1,0:T(1,128)}, u32[]{:S(2)}) copy-start(s32[1,32]{1,0:T(1,128)} %count_ref.1) | copy-start | bytes 388
  12.7 55.4 %all-to-all-start = ((bf16[32,64,512]{2,1,0:T(8,128)(2,1)}), bf16[32,64,512]{2,1,0:T(8,128)(2,1)}, u32[]{:S(2)}, u32[]{:S(2)}) async-start(bf16[32,64,512]{2,1,0:T(8,128)(2,1)} %bitcast.96), calls=%async_computation | async-start | bytes 4194304 | tf_op jit(solution)/shard_map/all_to_all | solution.py:270
  19.9 14.1 %collective-permute-start.3 = (bf16[4,8,512]{2,1,0:T(8,128)(2,1)S(1)}, bf16[4,8,512]{2,1,0:T(8,128)(2,1)S(1)}, u32[]{:S(2)}, u32[]{:S(2)}) collective-permute-start(bf16[4,8,512]{2,1,0:T(8,128)(2,1)S(1)} %bitcast_dynamic-update-slice_fusion.8), channel_id=1, source_target_pairs={{0,8},{4,12},{8,0},{12,4},{16,24},{20,28},{24,16},{28,20},{1,9},{5... | collective-permute-start | bytes 98312 | tf_op jit(solution)/shard_map/ppermute | solution.py:16
  21.4 12.7 %collective-permute-start.4 = (bf16[4,8,512]{2,1,0:T(8,128)(2,1)S(1)}, bf16[4,8,512]{2,1,0:T(8,128)(2,1)S(1)}, u32[]{:S(2)}, u32[]{:S(2)}) collective-permute-start(bf16[4,8,512]{2,1,0:T(8,128)(2,1)S(1)} %bitcast_dynamic-update-slice_fusion.8), channel_id=1, source_target_pairs={{0,16},{4,20},{8,24},{12,28},{16,0},{20,4},{24,8},{28,12},{1,17},{... | collective-permute-start | bytes 98312 | tf_op jit(solution)/shard_map/ppermute | solution.py:16
  22.5 14.2 %collective-permute-start.5 = (bf16[4,8,512]{2,1,0:T(8,128)(2,1)S(1)}, bf16[4,8,512]{2,1,0:T(8,128)(2,1)S(1)}, u32[]{:S(2)}, u32[]{:S(2)}) collective-permute-start(bf16[4,8,512]{2,1,0:T(8,128)(2,1)S(1)} %bitcast_dynamic-update-slice_fusion.8), channel_id=1, source_target_pairs={{0,24},{4,28},{8,16},{12,20},{16,8},{20,12},{24,0},{28,4},{1,25},{... | collective-permute-start | bytes 98312 | tf_op jit(solution)/shard_map/ppermute | solution.py:16
  36.7 9.2 %collective-permute-start.6 = (bf16[4,4,8,512]{3,2,1,0:T(8,128)(2,1)S(1)}, bf16[4,4,8,512]{3,2,1,0:T(8,128)(2,1)S(1)}, u32[]{:S(2)}, u32[]{:S(2)}) collective-permute-start(bf16[4,4,8,512]{3,2,1,0:T(8,128)(2,1)S(1)} %bitcast_dynamic-update-slice_fusion.4), channel_id=1, source_target_pairs={{0,4},{4,0},{8,12},{12,8},{16,20},{20,16},{24,28},{28,24},{1,5},{5... | collective-permute-start | bytes 393224 | tf_op jit(solution)/shard_map/ppermute | solution.py:16
  38.2 1.6 %copy-start.1 = (bf16[2048,512]{1,0:T(8,128)(2,1)S(1)}, bf16[2048,512]{1,0:T(8,128)(2,1)}, u32[]{:S(2)}) copy-start(bf16[2048,512]{1,0:T(8,128)(2,1)} %hp_ref.5) | copy-start | bytes 6291460
  43.9 2.0 %copy-start.3 = (f32[2048,512]{1,0:T(8,128)}, f32[2048,512]{1,0:T(8,128)S(1)}, u32[]{:S(2)}) copy-start(f32[2048,512]{1,0:T(8,128)S(1)} %slot_gate.1.gate_ref) | copy-start | bytes 12582916
  73.9 46.8 %all-to-all-start.1 = ((bf16[32,64,384]{2,1,0:T(8,128)(2,1)}), bf16[32,64,384]{2,1,0:T(8,128)(2,1)}, u32[]{:S(2)}, u32[]{:S(2)}) async-start(bf16[32,64,384]{2,1,0:T(8,128)(2,1)} %bitcast.97), calls=%async_computation.1 | async-start | bytes 3145728 | tf_op jit(solution)/shard_map/all_to_all | solution.py:287
  77.3 1.6 %copy-start.2 = (bf16[2048,512]{1,0:T(8,128)(2,1)S(1)}, bf16[2048,512]{1,0:T(8,128)(2,1)}, u32[]{:S(2)}) copy-start(bf16[2048,512]{1,0:T(8,128)(2,1)} %hp_ref.5) | copy-start | bytes 6291460
  78.9 1.6 %copy-start.4 = (bf16[2048,512]{1,0:T(8,128)(2,1)S(1)}, bf16[2048,512]{1,0:T(8,128)(2,1)}, u32[]{:S(2)}) copy-start(bf16[2048,512]{1,0:T(8,128)(2,1)} %get-tuple-element.20.delta_ref) | copy-start | bytes 6291460
  82.0 3.1 %collective-permute-start.7 = (f32[640,512]{1,0:T(8,128)S(1)}, f32[640,512]{1,0:T(8,128)S(1)}, u32[]{:S(2)}, u32[]{:S(2)}) collective-permute-start(f32[640,512]{1,0:T(8,128)S(1)} %half_terms.3), channel_id=1, source_target_pairs={{0,4},{4,0},{8,12},{12,8},{16,20},{20,16},{24,28},{28,24},{1,5},{5... | collective-permute-start | bytes 3932168 | tf_op jit(solution)/shard_map/ppermute | solution.py:16
  85.7 10.6 %collective-permute-start.10 = (bf16[4,40,512]{2,1,0:T(8,128)(2,1)S(1)}, bf16[4,40,512]{2,1,0:T(8,128)(2,1)S(1)}, u32[]{:S(2)}, u32[]{:S(2)}) collective-permute-start(bf16[4,40,512]{2,1,0:T(8,128)(2,1)S(1)} %get-tuple-element.41), channel_id=1, source_target_pairs={{0,24},{4,28},{8,16},{12,20},{16,8},{20,12},{24,0},{28,4},{1,25},{... | collective-permute-start | bytes 491528 | tf_op jit(solution)/shard_map/ppermute | solution.py:16
  88.0 12.3 %collective-permute-start.8 = (bf16[4,40,512]{2,1,0:T(8,128)(2,1)S(1)}, bf16[4,40,512]{2,1,0:T(8,128)(2,1)S(1)}, u32[]{:S(2)}, u32[]{:S(2)}) collective-permute-start(bf16[4,40,512]{2,1,0:T(8,128)(2,1)S(1)} %get-tuple-element.40), channel_id=1, source_target_pairs={{0,8},{4,12},{8,0},{12,4},{16,24},{20,28},{24,16},{28,20},{1,9},{5... | collective-permute-start | bytes 491528 | tf_op jit(solution)/shard_map/ppermute | solution.py:16
  88.3 12.1 %collective-permute-start.9 = (bf16[4,40,512]{2,1,0:T(8,128)(2,1)S(1)}, bf16[4,40,512]{2,1,0:T(8,128)(2,1)S(1)}, u32[]{:S(2)}, u32[]{:S(2)}) collective-permute-start(bf16[4,40,512]{2,1,0:T(8,128)(2,1)S(1)} %get-tuple-element.42), channel_id=1, source_target_pairs={{0,16},{4,20},{8,24},{12,28},{16,0},{20,4},{24,8},{28,12},{1,17},{... | collective-permute-start | bytes 491528 | tf_op jit(solution)/shard_map/ppermute | solution.py:16
  100.6 23.4 %collective-permute-start.11 = (bf16[136,512]{1,0:T(8,128)(2,1)S(1)}, bf16[136,512]{1,0:T(8,128)(2,1)S(1)}, u32[]{:S(2)}, u32[]{:S(2)}) collective-permute-start(bf16[136,512]{1,0:T(8,128)(2,1)S(1)} %get-tuple-element.47), channel_id=1, source_target_pairs={{0,1},{1,0},{2,3},{3,2},{4,5},{5,4},{6,7},{7,6},{8,9},{9,8},{10,11... | collective-permute-start | bytes 417800 | tf_op jit(solution)/shard_map/ppermute | solution.py:21
  102.3 21.7 %collective-permute-start.12 = (bf16[136,512]{1,0:T(8,128)(2,1)S(1)}, bf16[136,512]{1,0:T(8,128)(2,1)S(1)}, u32[]{:S(2)}, u32[]{:S(2)}) collective-permute-start(bf16[136,512]{1,0:T(8,128)(2,1)S(1)} %get-tuple-element.46), channel_id=1, source_target_pairs={{0,2},{1,3},{2,0},{3,1},{4,6},{5,7},{6,4},{7,5},{8,10},{9,11},{10,... | collective-permute-start | bytes 417800 | tf_op jit(solution)/shard_map/ppermute | solution.py:21
  106.1 17.9 %collective-permute-start.13 = (bf16[136,512]{1,0:T(8,128)(2,1)S(1)}, bf16[136,512]{1,0:T(8,128)(2,1)S(1)}, u32[]{:S(2)}, u32[]{:S(2)}) collective-permute-start(bf16[136,512]{1,0:T(8,128)(2,1)S(1)} %get-tuple-element.45), channel_id=1, source_target_pairs={{0,3},{1,2},{2,1},{3,0},{4,7},{5,6},{6,5},{7,4},{8,11},{9,10},{10,... | collective-permute-start | bytes 417800 | tf_op jit(solution)/shard_map/ppermute | solution.py:21
  120.7 18.6 %all-to-all-start.2 = ((bf16[32,64,128]{2,1,0:T(8,128)(2,1)}), bf16[32,64,128]{2,1,0:T(8,128)(2,1)S(1)}, u32[]{:S(2)}, u32[]{:S(2)}) async-start(bf16[32,64,128]{2,1,0:T(8,128)(2,1)} %bitcast.37), calls=%async_computation.2 | async-start | bytes 1048576 | tf_op jit(solution)/shard_map/all_to_all | solution.py:287
  124.0 2.9 %copy-start.8 = (s32[2048]{0:T(1024)S(1)}, s32[2048]{0:T(1024)}, u32[]{:S(2)}) copy-start(s32[2048]{0:T(1024)} %param.12) | copy-start | bytes 24580
  124.2 11.1 %collective-permute-start.14 = (bf16[4,32,512]{2,1,0:T(8,128)(2,1)S(1)}, bf16[4,32,512]{2,1,0:T(8,128)(2,1)S(1)}, u32[]{:S(2)}, u32[]{:S(2)}) collective-permute-start(bf16[4,32,512]{2,1,0:T(8,128)(2,1)S(1)} %get-tuple-element.33), channel_id=1, source_target_pairs={{0,8},{4,12},{8,0},{12,4},{16,24},{20,28},{24,16},{28,20},{1,9},{5... | collective-permute-start | bytes 393224 | tf_op jit(solution)/shard_map/ppermute | solution.py:16
  125.7 9.6 %collective-permute-start.15 = (bf16[4,32,512]{2,1,0:T(8,128)(2,1)S(1)}, bf16[4,32,512]{2,1,0:T(8,128)(2,1)S(1)}, u32[]{:S(2)}, u32[]{:S(2)}) collective-permute-start(bf16[4,32,512]{2,1,0:T(8,128)(2,1)S(1)} %get-tuple-element.33), channel_id=1, source_target_pairs={{0,16},{4,20},{8,24},{12,28},{16,0},{20,4},{24,8},{28,12},{1,17},{... | collective-permute-start | bytes 393224 | tf_op jit(solution)/shard_map/ppermute | solution.py:16
  126.9 10.9 %collective-permute-start.16 = (bf16[4,32,512]{2,1,0:T(8,128)(2,1)S(1)}, bf16[4,32,512]{2,1,0:T(8,128)(2,1)S(1)}, u32[]{:S(2)}, u32[]{:S(2)}) collective-permute-start(bf16[4,32,512]{2,1,0:T(8,128)(2,1)S(1)} %get-tuple-element.33), channel_id=1, source_target_pairs={{0,24},{4,28},{8,16},{12,20},{16,8},{20,12},{24,0},{28,4},{1,25},{... | collective-permute-start | bytes 393224 | tf_op jit(solution)/shard_map/ppermute | solution.py:16
  137.8 4.8 %collective-permute-start.17 = (bf16[4,4,32,512]{3,2,1,0:T(8,128)(2,1)S(1)}, bf16[4,4,32,512]{3,2,1,0:T(8,128)(2,1)S(1)}, u32[]{:S(2)}, u32[]{:S(2)}) collective-permute-start(bf16[4,4,32,512]{3,2,1,0:T(8,128)(2,1)S(1)} %bitcast_dynamic-update-slice_fusion), channel_id=1, source_target_pairs={{0,4},{4,0},{8,12},{12,8},{16,20},{20,16},{24,28},{28,24},{1,5},{5... | collective-permute-start | bytes 1572872 | tf_op jit(solution)/shard_map/ppermute | solution.py:16
  (1 other events, 1.3 us)

commit v6 on v5

--- a/solution.py
+++ b/solution.py
@@ -184,25 +184,24 @@
     )(*operands)
 
 
-def delta_kernel(got_ref, product_ref, gate_ref, weight_ref, delta_ref, *out_refs):
+def delta_kernel(keep, at, got_ref, product_ref, gate_ref, weight_ref, *out_refs):
     upstream = got_ref[...].astype(jnp.float32) + product_ref[...].astype(jnp.float32)
     delta = (upstream * gate_ref[...]).astype(jnp.bfloat16)
-    delta_ref[...] = delta
-    at = 0
-    for out_ref in out_refs:
-        part = weight_ref[at : at + out_ref.shape[1], :]
-        at += out_ref.shape[1]
-        out_ref[...] = lax.dot_general(
-            delta, part, (((1,), (1,)), ((), ())), preferred_element_type=jnp.float32
-        ).astype(jnp.bfloat16)
-
-
-def delta_and_rows(got, product_rows, gate, weight, cuts, tile=1024):
+    if keep:
+        out_refs[1][...] = delta
+    out_ref = out_refs[0]
+    part = weight_ref[at : at + out_ref.shape[1], :]
+    out_ref[...] = lax.dot_general(
+        delta, part, (((1,), (1,)), ((), ())), preferred_element_type=jnp.float32
+    ).astype(jnp.bfloat16)
+
+
+def delta_and_rows(got, product_rows, gate, weight, at, columns, keep, tile=1024):
     count, width = got.shape
     tile = min(tile, count)
-    slots = lambda columns: pl.BlockSpec((tile, columns), lambda i: (i, 0))
-    return pl.pallas_call(
-        delta_kernel,
+    slots = lambda wide: pl.BlockSpec((tile, wide), lambda i: (i, 0))
+    return pl.pallas_call(
+        functools.partial(delta_kernel, keep, at),
         grid=(count // tile,),
         in_specs=[
             slots(width),
@@ -210,9 +209,9 @@
             slots(width),
             pl.BlockSpec((width, width), lambda i: (0, 0)),
         ],
-        out_specs=[slots(width)] + [slots(columns) for columns in cuts],
-        out_shape=[jax.ShapeDtypeStruct((count, width), jnp.bfloat16)]
-        + [pltpu.HBM((count, columns), jnp.bfloat16) for columns in cuts],
+        out_specs=[slots(columns)] + [slots(width)] * keep,
+        out_shape=[pltpu.HBM((count, columns), jnp.bfloat16)]
+        + [jax.ShapeDtypeStruct((count, width), jnp.bfloat16)] * keep,
         compiler_params=pltpu.CompilerParams(vmem_limit_bytes=56 << 20),
         cost_estimate=pl.CostEstimate(
             flops=2 * count * width * width, bytes_accessed=12 * count * width, transcendentals=0
@@ -279,9 +278,9 @@
 
     gate = slot_gate(cust_count, hc_edge, hp_edge, w_cust, w_prod)
     cut = width * 3 // 4
-    delta, first, second = delta_and_rows(
-        fetched, product_rows, gate, w_cust, (cut, width - cut)
-    )
+    parts = (fetched, product_rows, gate, w_cust)
+    (first,) = delta_and_rows(*parts, 0, cut, False)
+    second, delta = delta_and_rows(*parts, cut, width - cut, True)
 
     def give_back(rows):
         return lax.all_to_all(

time: 145 us -> 143 us (0.986)
  Pallas kernels: 31.8 us -> 36.6 us
  waiting for transfers between devices: 64 us -> 59.3 us
  local copies, waits for them, and re-layouts: 8.47 us -> 6.89 us
    pallas_call x1 -> x2, Pallas kernels: 5.79 us -> 10.5 us  [delta_and_rows(): pl.pallas_call(functools.partial(delta_kernel, keep, at), grid=(count //...]
    all_to_all x2, waiting for transfers between devices: 14.7 us -> 11 us  [give_back(): lax.all_to_all(rows.reshape(devices, capacity, -1), AXES, split_axis=0, c...]
    ppermute x12, waiting for transfers between devices: 29.4 us -> 26.3 us  [shift_rows(): return lax.ppermute(value, 'rows', [(i, i ^ mask) for i in range(size)])]
    ppermute x6, waiting for transfers between devices: 0.02 us -> 2.13 us  [shift_grp(): return lax.ppermute(value, 'grp', [(i, i ^ mask) for i in range(size)])]
    unnamed x24, local copies, waits for them, and re-layouts: 8.13 us -> 6.54 us
  transfers between devices with their start and end apart: 21 -> 21, of which waited for: 10 -> 9; matrix products, arithmetic and copies ran while one was open for 2% -> 2% of each run, Pallas kernels for 18% -> 22%
where the time goes in v6:
time: 143 us
  waiting for transfers between devices  59.3 us (41%)
  Pallas kernels  36.6 us (26%)
  starting transfers between devices  35.5 us (25%)
  local copies, waits for them, and re-layouts  6.89 us (5%)
  other arithmetic  2.45 us (2%)
    ppermute x12, waiting for transfers between devices, shift_rows(): return lax.ppermute(value, 'rows', [(i, i ^ mask) for i in range(size)])  26.3 us
    all_to_all x1, waiting for transfers between devices, body(): lax.all_to_all(owned_rows.reshape(devices, capacity, width), AXES, split_...  19.9 us
    ppermute x12, starting transfers between devices, shift_rows(): return lax.ppermute(value, 'rows', [(i, i ^ mask) for i in range(size)])  12.3 us
    all_to_all x2, waiting for transfers between devices, give_back(): lax.all_to_all(rows.reshape(devices, capacity, -1), AXES, split_axis=0, c...  11 us
    pallas_call x2, Pallas kernels, delta_and_rows(): pl.pallas_call(functools.partial(delta_kernel, keep, at), grid=(count //...  10.5 us
    pallas_call x2, Pallas kernels, owner_sum(): pl.pallas_call(owner_sum_kernel, grid=(owned // tile,), out_shape=jax.Sha...  10.5 us
    ppermute x6, starting transfers between devices, shift_grp(): return lax.ppermute(value, 'grp', [(i, i ^ mask) for i in range(size)])  10.4 us
    pallas_call x2, Pallas kernels, pick(): pl.pallas_call(pick_kernel, grid=(count // tile,), out_shape=space((count...  8.38 us
  transfers between devices with their start and end apart: 21, of which 9 were waited for; matrix products, arithmetic and copies ran while one was open for 2% of the time, Pallas kernels for 22%

profile of v6, /device:TPU:1, one launch (start us, length us, event | category | flops | bytes accessed | tf_op | source)
XLA Modules:
  0.0 142.9 jit_solution(13602314229363350468)
XLA Ops:
  0.6 2.2 %collective-permute-start = (bf16[8,512]{1,0:T(8,128)(2,1)}, bf16[8,512]{1,0:T(8,128)(2,1)S(1)}, u32[]{:S(2)}, u32[]{:S(2)}) collective-permute-start(bf16[8,512]{1,0:T(8,128)(2,1)} %param.15), channel_id=1, source_target_pairs={{0,1},{1,0},{2,3},{3,2},{4,5},{5,4},{6,7},{7,6},{8,9},{9,8},{10,11... | collective-permute-start | bytes 24584 | tf_op jit(solution)/shard_map/ppermute | solution.py:21
  2.8 2.2 %collective-permute-start.2 = (bf16[8,512]{1,0:T(8,128)(2,1)}, bf16[8,512]{1,0:T(8,128)(2,1)S(1)}, u32[]{:S(2)}, u32[]{:S(2)}) collective-permute-start(bf16[8,512]{1,0:T(8,128)(2,1)} %param.15), channel_id=1, source_target_pairs={{0,3},{1,2},{2,1},{3,0},{4,7},{5,6},{6,5},{7,4},{8,11},{9,10},{10,... | collective-permute-start | bytes 24584 | tf_op jit(solution)/shard_map/ppermute | solution.py:21
  5.1 7.4 %pick_rows.2 = bf16[2048,512]{1,0:T(8,128)(2,1)} custom-call(s32[1,2048]{1,0:T(1,128)} %bitcast.87, bf16[2048,512]{1,0:T(8,128)(2,1)} %table_ref.1), custom_call_target="tpu_custom_call" | custom-call | flops 4294967296 | bytes 4194304 | tf_op jit(solution)/shard_map/pick_rows/pallas_call | solution.py:41
  12.7 6.2 %all-to-all-start = ((bf16[32,64,512]{2,1,0:T(8,128)(2,1)}), bf16[32,64,512]{2,1,0:T(8,128)(2,1)}, u32[]{:S(2)}, u32[]{:S(2)}) async-start(bf16[32,64,512]{2,1,0:T(8,128)(2,1)} %bitcast.97), calls=%async_computation | async-start | bytes 4194304 | tf_op jit(solution)/shard_map/all_to_all | solution.py:269
  19.0 2.4 %collective-permute-start.5 = (bf16[4,8,512]{2,1,0:T(8,128)(2,1)S(1)}, bf16[4,8,512]{2,1,0:T(8,128)(2,1)S(1)}, u32[]{:S(2)}, u32[]{:S(2)}) collective-permute-start(bf16[4,8,512]{2,1,0:T(8,128)(2,1)S(1)} %bitcast_dynamic-update-slice_fusion.8), channel_id=1, source_target_pairs={{0,24},{4,28},{8,16},{12,20},{16,8},{20,12},{24,0},{28,4},{1,25},{... | collective-permute-start | bytes 98312 | tf_op jit(solution)/shard_map/ppermute | solution.py:16
  21.7 12.8 %collective-permute-done.3 = bf16[4,8,512]{2,1,0:T(8,128)(2,1)S(1)} collective-permute-done((bf16[4,8,512]{2,1,0:T(8,128)(2,1)S(1)}, bf16[4,8,512]{2,1,0:T(8,128)(2,1)S(1)}, u32[]{:S(2)}, u32[]{:S(2)}) %collective-permute-start.3) | collective-permute-done | bytes 32800 | tf_op jit(solution)/shard_map/ppermute | solution.py:16
  35.4 1.9 %collective-permute-start.6 = (bf16[4,4,8,512]{3,2,1,0:T(8,128)(2,1)S(1)}, bf16[4,4,8,512]{3,2,1,0:T(8,128)(2,1)S(1)}, u32[]{:S(2)}, u32[]{:S(2)}) collective-permute-start(bf16[4,4,8,512]{3,2,1,0:T(8,128)(2,1)S(1)} %bitcast_dynamic-update-slice_fusion.4), channel_id=1, source_target_pairs={{0,4},{4,0},{8,12},{12,8},{16,20},{20,16},{24,28},{28,24},{1,5},{5... | collective-permute-start | bytes 393224 | tf_op jit(solution)/shard_map/ppermute | solution.py:16
  37.3 1.6 %copy-done.2 = bf16[2048,512]{1,0:T(8,128)(2,1)S(1)} copy-done((bf16[2048,512]{1,0:T(8,128)(2,1)S(1)}, bf16[2048,512]{1,0:T(8,128)(2,1)}, u32[]{:S(2)}) %copy-start.2) | copy-done | bytes 2097176
  38.9 4.0 %slot_gate.1.gate_ref = f32[2048,512]{1,0:T(8,128)S(1)} custom-call(s32[1,32]{1,0:T(1,128)S(1)} %copy-done.9, bf16[2048,512]{1,0:T(8,128)(2,1)S(1)} %copy-done.1, bf16[2048,512]{1,0:T(8,128)(2,1)S(1)} %copy-done.2, bf16[512,512]{1,0:T(8,128)(2,1)S(1)} %copy-done.6, bf16[512,512]{1,0:T(8,128)(2,1)S(1)} %copy-done.7), custom_call_target="tpu_custom_call" | custom-call | flops 2147483648 | bytes 8388608 | tf_op jit(solution)/shard_map/slot_gate/pallas_call | solution.py:77
  43.0 2.0 %copy-done = f32[2048,512]{1,0:T(8,128)} copy-done((f32[2048,512]{1,0:T(8,128)}, f32[2048,512]{1,0:T(8,128)S(1)}, u32[]{:S(2)}) %copy-start) | copy-done | bytes 4194328
  46.1 1.3 copy-done.4
  47.4 19.9 %all-to-all-done = bf16[32,64,512]{2,1,0:T(8,128)(2,1)} async-done(((bf16[32,64,512]{2,1,0:T(8,128)(2,1)}), bf16[32,64,512]{2,1,0:T(8,128)(2,1)}, u32[]{:S(2)}, u32[]{:S(2)}) %all-to-all-start) | async-done | bytes 2097184 | tf_op jit(solution)/shard_map/all_to_all | solution.py:269
  67.2 5.3 %delta_and_rows.3 = bf16[2048,384]{1,0:T(8,128)(2,1)} custom-call(bf16[2048,512]{1,0:T(8,128)(2,1)} %bitcast.8.got_ref, bf16[2048,512]{1,0:T(8,128)(2,1)} %copy-done.4, f32[2048,512]{1,0:T(8,128)} %copy-done, bf16[512,512]{1,0:T(8,128)(2,1)} %weight_ref.3), custom_call_target="tpu_custom_call" | custom-call | flops 1073741824 | bytes 12582912 | tf_op jit(solution)/shard_map/delta_and_rows/pallas_call | solution.py:203
  72.6 3.4 %all-to-all-start.1 = ((bf16[32,64,384]{2,1,0:T(8,128)(2,1)}), bf16[32,64,384]{2,1,0:T(8,128)(2,1)}, u32[]{:S(2)}, u32[]{:S(2)}) async-start(bf16[32,64,384]{2,1,0:T(8,128)(2,1)} %bitcast.90), calls=%async_computation.1 | async-start | bytes 3145728 | tf_op jit(solution)/shard_map/all_to_all | solution.py:286
  76.0 5.2 %delta_and_rows.2 = (bf16[2048,128]{1,0:T(8,128)(2,1)}, bf16[2048,512]{1,0:T(8,128)(2,1)}) custom-call(bf16[2048,512]{1,0:T(8,128)(2,1)} %bitcast.8.got_ref, bf16[2048,512]{1,0:T(8,128)(2,1)} %copy-done.4, f32[2048,512]{1,0:T(8,128)} %copy-done, bf16[512,512]{1,0:T(8,128)(2,1)} %weight_ref.3), custom_call_target="tpu_custom_call" | custom-call | flops 1073741824 | bytes 12582912 | tf_op jit(solution)/shard_map/delta_and_rows/pallas_call | solution.py:203
  81.3 1.6 %copy-done.5 = bf16[2048,512]{1,0:T(8,128)(2,1)S(1)} copy-done((bf16[2048,512]{1,0:T(8,128)(2,1)S(1)}, bf16[2048,512]{1,0:T(8,128)(2,1)}, u32[]{:S(2)}) %copy-start.5) | copy-done | bytes 2097176
  82.8 1.5 %half_terms.3 = f32[640,512]{1,0:T(8,128)S(1)} custom-call(s32[1]{0:T(128)} %bitcast.16.half_ref, s32[1,2048]{1,0:T(1,128)S(1)} %bitcast.85, bf16[2048,512]{1,0:T(8,128)(2,1)S(1)} %copy-done.1, bf16[2048,512]{1,0:T(8,128)(2,1)S(1)} %copy-done.3, bf16[2048,512]{1,0:T(8,128)(2,1)S(1)} %copy-done.5), custom_call_target="tpu_custom_call" | custom-call | flops 1342177280 | bytes 4194304 | tf_op jit(solution)/shard_map/half_terms/pallas_call | solution.py:127
  84.8 1.5 %half_terms.2 = f32[640,512]{1,0:T(8,128)S(1)} custom-call(s32[1]{0:T(128)} %bitcast.half_ref, s32[1,2048]{1,0:T(1,128)S(1)} %bitcast.86, bf16[2048,512]{1,0:T(8,128)(2,1)S(1)} %copy-done.1, bf16[2048,512]{1,0:T(8,128)(2,1)S(1)} %copy-done.3, bf16[2048,512]{1,0:T(8,128)(2,1)S(1)} %copy-done.5), custom_call_target="tpu_custom_call" | custom-call | flops 1342177280 | bytes 4194304 | tf_op jit(solution)/shard_map/half_terms/pallas_call | solution.py:127
  88.0 1.6 %collective-permute-start.8 = (bf16[4,40,512]{2,1,0:T(8,128)(2,1)S(1)}, bf16[4,40,512]{2,1,0:T(8,128)(2,1)S(1)}, u32[]{:S(2)}, u32[]{:S(2)}) collective-permute-start(bf16[4,40,512]{2,1,0:T(8,128)(2,1)S(1)} %get-tuple-element.38), channel_id=1, source_target_pairs={{0,8},{4,12},{8,0},{12,4},{16,24},{20,28},{24,16},{28,20},{1,9},{5... | collective-permute-start | bytes 491528 | tf_op jit(solution)/shard_map/ppermute | solution.py:16
  91.0 5.2 %collective-permute-done.8 = bf16[4,40,512]{2,1,0:T(8,128)(2,1)S(1)} collective-permute-done((bf16[4,40,512]{2,1,0:T(8,128)(2,1)S(1)}, bf16[4,40,512]{2,1,0:T(8,128)(2,1)S(1)}, u32[]{:S(2)}, u32[]{:S(2)}) %collective-permute-start.8) | collective-permute-done | bytes 163872 | tf_op jit(solution)/shard_map/ppermute | solution.py:16
  96.2 6.1 %collective-permute-done.10 = bf16[4,40,512]{2,1,0:T(8,128)(2,1)S(1)} collective-permute-done((bf16[4,40,512]{2,1,0:T(8,128)(2,1)S(1)}, bf16[4,40,512]{2,1,0:T(8,128)(2,1)S(1)}, u32[]{:S(2)}, u32[]{:S(2)}) %collective-permute-start.10) | collective-permute-done | bytes 163872 | tf_op jit(solution)/shard_map/ppermute | solution.py:16
  102.5 3.3 %collective-permute-start.13 = (bf16[136,512]{1,0:T(8,128)(2,1)S(1)}, bf16[136,512]{1,0:T(8,128)(2,1)S(1)}, u32[]{:S(2)}, u32[]{:S(2)}) collective-permute-start(bf16[136,512]{1,0:T(8,128)(2,1)S(1)} %get-tuple-element.43), channel_id=1, source_target_pairs={{0,3},{1,2},{2,1},{3,0},{4,7},{5,6},{6,5},{7,4},{8,11},{9,10},{10,... | collective-permute-start | bytes 417800 | tf_op jit(solution)/shard_map/ppermute | solution.py:21
  105.9 2.4 %collective-permute-start.12 = (bf16[136,512]{1,0:T(8,128)(2,1)S(1)}, bf16[136,512]{1,0:T(8,128)(2,1)S(1)}, u32[]{:S(2)}, u32[]{:S(2)}) collective-permute-start(bf16[136,512]{1,0:T(8,128)(2,1)S(1)} %get-tuple-element.44), channel_id=1, source_target_pairs={{0,2},{1,3},{2,0},{3,1},{4,6},{5,7},{6,4},{7,5},{8,10},{9,11},{10,... | collective-permute-start | bytes 417800 | tf_op jit(solution)/shard_map/ppermute | solution.py:21
  108.4 11.0 %all-to-all-done.1 = bf16[32,64,384]{2,1,0:T(8,128)(2,1)} async-done(((bf16[32,64,384]{2,1,0:T(8,128)(2,1)}), bf16[32,64,384]{2,1,0:T(8,128)(2,1)}, u32[]{:S(2)}, u32[]{:S(2)}) %all-to-all-start.1) | async-done | bytes 1572896 | tf_op jit(solution)/shard_map/all_to_all | solution.py:286
  119.4 3.2 %all-to-all-start.2 = ((bf16[32,64,128]{2,1,0:T(8,128)(2,1)}), bf16[32,64,128]{2,1,0:T(8,128)(2,1)S(1)}, u32[]{:S(2)}, u32[]{:S(2)}) async-start(bf16[32,64,128]{2,1,0:T(8,128)(2,1)} %bitcast.37), calls=%async_computation.2 | async-start | bytes 1048576 | tf_op jit(solution)/shard_map/all_to_all | solution.py:286
  122.6 2.1 %collective-permute-done.12 = bf16[136,512]{1,0:T(8,128)(2,1)S(1)} collective-permute-done((bf16[136,512]{1,0:T(8,128)(2,1)S(1)}, bf16[136,512]{1,0:T(8,128)(2,1)S(1)}, u32[]{:S(2)}, u32[]{:S(2)}) %collective-permute-start.12) | collective-permute-done | bytes 139296 | tf_op jit(solution)/shard_map/ppermute | solution.py:21
  124.9 1.3 collective-permute-start.15
  126.2 1.2 collective-permute-start.14
  127.6 7.2 %owner_sum.2.refs_0_ = f32[2048,512]{1,0:T(8,128)} custom-call(s32[1,2048]{1,0:T(1,128)S(1)} %bitcast.88, bf16[2048,384]{1,0:T(8,128)(2,1)} %bitcast.29.rows_ref), custom_call_target="tpu_custom_call" | custom-call | tf_op jit(solution)/shard_map/owner_sum/pallas_call | solution.py:170
  136.3 1.6 %collective-permute-start.17 = (bf16[4,4,32,512]{3,2,1,0:T(8,128)(2,1)S(1)}, bf16[4,4,32,512]{3,2,1,0:T(8,128)(2,1)S(1)}, u32[]{:S(2)}, u32[]{:S(2)}) collective-permute-start(bf16[4,4,32,512]{3,2,1,0:T(8,128)(2,1)S(1)} %bitcast_dynamic-update-slice_fusion), channel_id=1, source_target_pairs={{0,4},{4,0},{8,12},{12,8},{16,20},{20,16},{24,28},{28,24},{1,5},{5... | collective-permute-start | bytes 1572872 | tf_op jit(solution)/shard_map/ppermute | solution.py:16
  137.9 3.3 %owner_sum.3 = f32[2048,512]{1,0:T(8,128)} custom-call(s32[1,2048]{1,0:T(1,128)S(1)} %bitcast.89, bf16[2048,128]{1,0:T(8,128)(2,1)S(1)} %bitcast.82, f32[2048,512]{1,0:T(8,128)} %owner_sum.2.refs_0_), custom_call_target="tpu_custom_call", output_to_operand_aliasing={{}: (2, {})} | custom-call | flops 1073741824 | bytes 1572864 | tf_op jit(solution)/shard_map/owner_sum/pallas_call | solution.py:170
  141.3 1.6 %convert_multiply_fusion = (f32[2,4,4,16,512]{4,3,2,1,0:T(8,128)}, f32[2,4,4,16,512]{4,3,2,1,0:T(8,128)}) fusion(bf16[1,4,4,16,512]{4,3,2,1,0:T(8,128)(2,1)S(1)} %get-tuple-element.36, bf16[1,4,4,16,512]{4,3,2,1,0:T(8,128)(2,1)S(1)} %get-tuple-element.34, bf16[1,4,4,16,512]{4,3,2,1,0:T(8,128)(2,1)S(1)} %get-tuple-element.35, ...), kind=kLoop, calls=%fused_computation.2 | loop fusion | flops 1572864 | bytes 3145728 | tf_op jit(solution)/shard_map/mul | solution.py:353
  (77 shorter events, 8.1 us)
Async XLA Ops:
  0.6 11.9 %collective-permute-start = (bf16[8,512]{1,0:T(8,128)(2,1)}, bf16[8,512]{1,0:T(8,128)(2,1)S(1)}, u32[]{:S(2)}, u32[]{:S(2)}) collective-permute-start(bf16[8,512]{1,0:T(8,128)(2,1)} %param.15), channel_id=1, source_target_pairs={{0,1},{1,0},{2,3},{3,2},{4,5},{5,4},{6,7},{7,6},{8,9},{9,8},{10,11... | collective-permute-start | bytes 24584 | tf_op jit(solution)/shard_map/ppermute | solution.py:21
  2.8 9.8 %collective-permute-start.2 = (bf16[8,512]{1,0:T(8,128)(2,1)}, bf16[8,512]{1,0:T(8,128)(2,1)S(1)}, u32[]{:S(2)}, u32[]{:S(2)}) collective-permute-start(bf16[8,512]{1,0:T(8,128)(2,1)} %param.15), channel_id=1, source_target_pairs={{0,3},{1,2},{2,1},{3,0},{4,7},{5,6},{6,5},{7,4},{8,11},{9,10},{10,... | collective-permute-start | bytes 24584 | tf_op jit(solution)/shard_map/ppermute | solution.py:21
  5.0 7.6 %collective-permute-start.1 = (bf16[8,512]{1,0:T(8,128)(2,1)}, bf16[8,512]{1,0:T(8,128)(2,1)S(1)}, u32[]{:S(2)}, u32[]{:S(2)}) collective-permute-start(bf16[8,512]{1,0:T(8,128)(2,1)} %param.15), channel_id=1, source_target_pairs={{0,2},{1,3},{2,0},{3,1},{4,6},{5,7},{6,4},{7,5},{8,10},{9,11},{10,... | collective-permute-start | bytes 24584 | tf_op jit(solution)/shard_map/ppermute | solution.py:21
  5.1 7.4 %copy-start.10 = (bf16[8,512]{1,0:T(8,128)(2,1)S(1)}, bf16[8,512]{1,0:T(8,128)(2,1)}, u32[]{:S(2)}) copy-start(bf16[8,512]{1,0:T(8,128)(2,1)} %param.15) | copy-start | bytes 24580
  12.6 6.3 %copy-start.11 = (s32[2048]{0:T(1024)S(1)}, s32[2048]{0:T(1024)}, u32[]{:S(2)}) copy-start(s32[2048]{0:T(1024)} %param.13) | copy-start | bytes 24580
  12.6 24.7 %copy-start.1 = (bf16[2048,512]{1,0:T(8,128)(2,1)S(1)}, bf16[2048,512]{1,0:T(8,128)(2,1)}, u32[]{:S(2)}) copy-start(bf16[2048,512]{1,0:T(8,128)(2,1)} %hc_ref.5) | copy-start | bytes 6291460
  12.7 24.6 %copy-start.6 = (bf16[512,512]{1,0:T(8,128)(2,1)S(1)}, bf16[512,512]{1,0:T(8,128)(2,1)}, u32[]{:S(2)}) copy-start(bf16[512,512]{1,0:T(8,128)(2,1)} %weight_ref.3) | copy-start | bytes 1572868
  12.7 24.6 %copy-start.7 = (bf16[512,512]{1,0:T(8,128)(2,1)S(1)}, bf16[512,512]{1,0:T(8,128)(2,1)}, u32[]{:S(2)}) copy-start(bf16[512,512]{1,0:T(8,128)(2,1)} %wp_ref.1) | copy-start | bytes 1572868
  12.7 24.6 %copy-start.9 = (s32[1,32]{1,0:T(1,128)S(1)}, s32[1,32]{1,0:T(1,128)}, u32[]{:S(2)}) copy-start(s32[1,32]{1,0:T(1,128)} %count_ref.1) | copy-start | bytes 388
  12.7 54.5 %all-to-all-start = ((bf16[32,64,512]{2,1,0:T(8,128)(2,1)}), bf16[32,64,512]{2,1,0:T(8,128)(2,1)}, u32[]{:S(2)}, u32[]{:S(2)}) async-start(bf16[32,64,512]{2,1,0:T(8,128)(2,1)} %bitcast.97), calls=%async_computation | async-start | bytes 4194304 | tf_op jit(solution)/shard_map/all_to_all | solution.py:269
  19.0 16.4 %collective-permute-start.5 = (bf16[4,8,512]{2,1,0:T(8,128)(2,1)S(1)}, bf16[4,8,512]{2,1,0:T(8,128)(2,1)S(1)}, u32[]{:S(2)}, u32[]{:S(2)}) collective-permute-start(bf16[4,8,512]{2,1,0:T(8,128)(2,1)S(1)} %bitcast_dynamic-update-slice_fusion.8), channel_id=1, source_target_pairs={{0,24},{4,28},{8,16},{12,20},{16,8},{20,12},{24,0},{28,4},{1,25},{... | collective-permute-start | bytes 98312 | tf_op jit(solution)/shard_map/ppermute | solution.py:16
  21.4 13.2 %collective-permute-start.4 = (bf16[4,8,512]{2,1,0:T(8,128)(2,1)S(1)}, bf16[4,8,512]{2,1,0:T(8,128)(2,1)S(1)}, u32[]{:S(2)}, u32[]{:S(2)}) collective-permute-start(bf16[4,8,512]{2,1,0:T(8,128)(2,1)S(1)} %bitcast_dynamic-update-slice_fusion.8), channel_id=1, source_target_pairs={{0,16},{4,20},{8,24},{12,28},{16,0},{20,4},{24,8},{28,12},{1,17},{... | collective-permute-start | bytes 98312 | tf_op jit(solution)/shard_map/ppermute | solution.py:16
  21.6 12.9 %collective-permute-start.3 = (bf16[4,8,512]{2,1,0:T(8,128)(2,1)S(1)}, bf16[4,8,512]{2,1,0:T(8,128)(2,1)S(1)}, u32[]{:S(2)}, u32[]{:S(2)}) collective-permute-start(bf16[4,8,512]{2,1,0:T(8,128)(2,1)S(1)} %bitcast_dynamic-update-slice_fusion.8), channel_id=1, source_target_pairs={{0,8},{4,12},{8,0},{12,4},{16,24},{20,28},{24,16},{28,20},{1,9},{5... | collective-permute-start | bytes 98312 | tf_op jit(solution)/shard_map/ppermute | solution.py:16
  35.4 9.6 %collective-permute-start.6 = (bf16[4,4,8,512]{3,2,1,0:T(8,128)(2,1)S(1)}, bf16[4,4,8,512]{3,2,1,0:T(8,128)(2,1)S(1)}, u32[]{:S(2)}, u32[]{:S(2)}) collective-permute-start(bf16[4,4,8,512]{3,2,1,0:T(8,128)(2,1)S(1)} %bitcast_dynamic-update-slice_fusion.4), channel_id=1, source_target_pairs={{0,4},{4,0},{8,12},{12,8},{16,20},{20,16},{24,28},{28,24},{1,5},{5... | collective-permute-start | bytes 393224 | tf_op jit(solution)/shard_map/ppermute | solution.py:16
  37.3 1.6 %copy-start.2 = (bf16[2048,512]{1,0:T(8,128)(2,1)S(1)}, bf16[2048,512]{1,0:T(8,128)(2,1)}, u32[]{:S(2)}) copy-start(bf16[2048,512]{1,0:T(8,128)(2,1)} %hp_ref.5) | copy-start | bytes 6291460
  43.0 2.0 %copy-start = (f32[2048,512]{1,0:T(8,128)}, f32[2048,512]{1,0:T(8,128)S(1)}, u32[]{:S(2)}) copy-start(f32[2048,512]{1,0:T(8,128)S(1)} %slot_gate.1.gate_ref) | copy-start | bytes 12582916
  72.6 46.8 %all-to-all-start.1 = ((bf16[32,64,384]{2,1,0:T(8,128)(2,1)}), bf16[32,64,384]{2,1,0:T(8,128)(2,1)}, u32[]{:S(2)}, u32[]{:S(2)}) async-start(bf16[32,64,384]{2,1,0:T(8,128)(2,1)} %bitcast.90), calls=%async_computation.1 | async-start | bytes 3145728 | tf_op jit(solution)/shard_map/all_to_all | solution.py:286
  76.0 5.2 %copy-start.3 = (bf16[2048,512]{1,0:T(8,128)(2,1)S(1)}, bf16[2048,512]{1,0:T(8,128)(2,1)}, u32[]{:S(2)}) copy-start(bf16[2048,512]{1,0:T(8,128)(2,1)} %hp_ref.5) | copy-start | bytes 6291460
  81.2 1.6 %copy-start.5 = (bf16[2048,512]{1,0:T(8,128)(2,1)S(1)}, bf16[2048,512]{1,0:T(8,128)(2,1)}, u32[]{:S(2)}) copy-start(bf16[2048,512]{1,0:T(8,128)(2,1)} %get-tuple-element.19.delta_ref) | copy-start | bytes 6291460
  84.4 3.1 %collective-permute-start.7 = (f32[640,512]{1,0:T(8,128)S(1)}, f32[640,512]{1,0:T(8,128)S(1)}, u32[]{:S(2)}, u32[]{:S(2)}) collective-permute-start(f32[640,512]{1,0:T(8,128)S(1)} %half_terms.3), channel_id=1, source_target_pairs={{0,4},{4,0},{8,12},{12,8},{16,20},{20,16},{24,28},{28,24},{1,5},{5... | collective-permute-start | bytes 3932168 | tf_op jit(solution)/shard_map/ppermute | solution.py:16
  88.0 8.2 %collective-permute-start.8 = (bf16[4,40,512]{2,1,0:T(8,128)(2,1)S(1)}, bf16[4,40,512]{2,1,0:T(8,128)(2,1)S(1)}, u32[]{:S(2)}, u32[]{:S(2)}) collective-permute-start(bf16[4,40,512]{2,1,0:T(8,128)(2,1)S(1)} %get-tuple-element.38), channel_id=1, source_target_pairs={{0,8},{4,12},{8,0},{12,4},{16,24},{20,28},{24,16},{28,20},{1,9},{5... | collective-permute-start | bytes 491528 | tf_op jit(solution)/shard_map/ppermute | solution.py:16
  89.6 12.7 %collective-permute-start.10 = (bf16[4,40,512]{2,1,0:T(8,128)(2,1)S(1)}, bf16[4,40,512]{2,1,0:T(8,128)(2,1)S(1)}, u32[]{:S(2)}, u32[]{:S(2)}) collective-permute-start(bf16[4,40,512]{2,1,0:T(8,128)(2,1)S(1)} %get-tuple-element.39), channel_id=1, source_target_pairs={{0,24},{4,28},{8,16},{12,20},{16,8},{20,12},{24,0},{28,4},{1,25},{... | collective-permute-start | bytes 491528 | tf_op jit(solution)/shard_map/ppermute | solution.py:16
  90.6 11.7 %collective-permute-start.9 = (bf16[4,40,512]{2,1,0:T(8,128)(2,1)S(1)}, bf16[4,40,512]{2,1,0:T(8,128)(2,1)S(1)}, u32[]{:S(2)}, u32[]{:S(2)}) collective-permute-start(bf16[4,40,512]{2,1,0:T(8,128)(2,1)S(1)} %get-tuple-element.40), channel_id=1, source_target_pairs={{0,16},{4,20},{8,24},{12,28},{16,0},{20,4},{24,8},{28,12},{1,17},{... | collective-permute-start | bytes 491528 | tf_op jit(solution)/shard_map/ppermute | solution.py:16
  102.5 20.1 %collective-permute-start.13 = (bf16[136,512]{1,0:T(8,128)(2,1)S(1)}, bf16[136,512]{1,0:T(8,128)(2,1)S(1)}, u32[]{:S(2)}, u32[]{:S(2)}) collective-permute-start(bf16[136,512]{1,0:T(8,128)(2,1)S(1)} %get-tuple-element.43), channel_id=1, source_target_pairs={{0,3},{1,2},{2,1},{3,0},{4,7},{5,6},{6,5},{7,4},{8,11},{9,10},{10,... | collective-permute-start | bytes 417800 | tf_op jit(solution)/shard_map/ppermute | solution.py:21
  105.9 18.9 %collective-permute-start.12 = (bf16[136,512]{1,0:T(8,128)(2,1)S(1)}, bf16[136,512]{1,0:T(8,128)(2,1)S(1)}, u32[]{:S(2)}, u32[]{:S(2)}) collective-permute-start(bf16[136,512]{1,0:T(8,128)(2,1)S(1)} %get-tuple-element.44), channel_id=1, source_target_pairs={{0,2},{1,3},{2,0},{3,1},{4,6},{5,7},{6,4},{7,5},{8,10},{9,11},{10,... | collective-permute-start | bytes 417800 | tf_op jit(solution)/shard_map/ppermute | solution.py:21
  108.2 16.5 %collective-permute-start.11 = (bf16[136,512]{1,0:T(8,128)(2,1)S(1)}, bf16[136,512]{1,0:T(8,128)(2,1)S(1)}, u32[]{:S(2)}, u32[]{:S(2)}) collective-permute-start(bf16[136,512]{1,0:T(8,128)(2,1)S(1)} %get-tuple-element.45), channel_id=1, source_target_pairs={{0,1},{1,0},{2,3},{3,2},{4,5},{5,4},{6,7},{7,6},{8,9},{9,8},{10,11... | collective-permute-start | bytes 417800 | tf_op jit(solution)/shard_map/ppermute | solution.py:21
  119.4 18.5 %all-to-all-start.2 = ((bf16[32,64,128]{2,1,0:T(8,128)(2,1)}), bf16[32,64,128]{2,1,0:T(8,128)(2,1)S(1)}, u32[]{:S(2)}, u32[]{:S(2)}) async-start(bf16[32,64,128]{2,1,0:T(8,128)(2,1)} %bitcast.37), calls=%async_computation.2 | async-start | bytes 1048576 | tf_op jit(solution)/shard_map/all_to_all | solution.py:286
  122.6 5.0 %copy-start.8 = (s32[2048]{0:T(1024)S(1)}, s32[2048]{0:T(1024)}, u32[]{:S(2)}) copy-start(s32[2048]{0:T(1024)} %param.12) | copy-start | bytes 24580
  124.9 11.1 %collective-permute-start.15 = (bf16[4,32,512]{2,1,0:T(8,128)(2,1)S(1)}, bf16[4,32,512]{2,1,0:T(8,128)(2,1)S(1)}, u32[]{:S(2)}, u32[]{:S(2)}) collective-permute-start(bf16[4,32,512]{2,1,0:T(8,128)(2,1)S(1)} %get-tuple-element.31), channel_id=1, source_target_pairs={{0,16},{4,20},{8,24},{12,28},{16,0},{20,4},{24,8},{28,12},{1,17},{... | collective-permute-start | bytes 393224 | tf_op jit(solution)/shard_map/ppermute | solution.py:16
  126.2 9.8 %collective-permute-start.14 = (bf16[4,32,512]{2,1,0:T(8,128)(2,1)S(1)}, bf16[4,32,512]{2,1,0:T(8,128)(2,1)S(1)}, u32[]{:S(2)}, u32[]{:S(2)}) collective-permute-start(bf16[4,32,512]{2,1,0:T(8,128)(2,1)S(1)} %get-tuple-element.31), channel_id=1, source_target_pairs={{0,8},{4,12},{8,0},{12,4},{16,24},{20,28},{24,16},{28,20},{1,9},{5... | collective-permute-start | bytes 393224 | tf_op jit(solution)/shard_map/ppermute | solution.py:16
  127.4 8.9 %collective-permute-start.16 = (bf16[4,32,512]{2,1,0:T(8,128)(2,1)S(1)}, bf16[4,32,512]{2,1,0:T(8,128)(2,1)S(1)}, u32[]{:S(2)}, u32[]{:S(2)}) collective-permute-start(bf16[4,32,512]{2,1,0:T(8,128)(2,1)S(1)} %get-tuple-element.31), channel_id=1, source_target_pairs={{0,24},{4,28},{8,16},{12,20},{16,8},{20,12},{24,0},{28,4},{1,25},{... | collective-permute-start | bytes 393224 | tf_op jit(solution)/shard_map/ppermute | solution.py:16
  136.3 4.9 %collective-permute-start.17 = (bf16[4,4,32,512]{3,2,1,0:T(8,128)(2,1)S(1)}, bf16[4,4,32,512]{3,2,1,0:T(8,128)(2,1)S(1)}, u32[]{:S(2)}, u32[]{:S(2)}) collective-permute-start(bf16[4,4,32,512]{3,2,1,0:T(8,128)(2,1)S(1)} %bitcast_dynamic-update-slice_fusion), channel_id=1, source_target_pairs={{0,4},{4,0},{8,12},{12,8},{16,20},{20,16},{24,28},{28,24},{1,5},{5... | collective-permute-start | bytes 1572872 | tf_op jit(solution)/shard_map/ppermute | solution.py:16
  (1 other events, 1.3 us)

commit v7 on v6

--- a/solution.py
+++ b/solution.py
@@ -307,37 +307,43 @@
     for block in got:
         mine = mine + block.astype(jnp.float32)
     here = lax.axis_index("grp")
-    sums, weights = mine[:, :product_count], mine[:, product_count:].astype(jnp.bfloat16)
-    every = weights.reshape(-1, width)
-    own_sum = lax.dynamic_index_in_dim(sums, here, 0, False)
-    blocks = [
-        shift_grp(
-            jnp.concatenate(
-                [lax.dynamic_index_in_dim(sums, here ^ k, 0, False).astype(jnp.bfloat16), every]
-            ),
-            k,
-        )
-        for k in range(1, grps)
+    weights = mine[:, product_count:]
+    asked = [
+        lax.dynamic_index_in_dim(mine[:, :product_count], here ^ k, 0, False) for k in range(grps)
     ]
-    blocks, returned = lax.optimization_barrier((blocks, returned))
-    terms = [weights.astype(jnp.float32)]
-    for block in blocks:
-        own_sum = own_sum + block[:product_count].astype(jnp.float32)
-        terms.append(block[product_count:].astype(jnp.float32).reshape(weights.shape))
-    while len(terms) > 1:
-        terms = [a + b for a, b in zip(terms[::2], terms[1::2])]
-    own = terms[0].astype(jnp.bfloat16)
+    step = 1
+    while step < grps:
+        kept, sent = asked[0 :: 2 * step], asked[step :: 2 * step]
+        packed = jnp.concatenate(sent + [weights.reshape(-1, width)])
+        if 2 * step >= grps:
+            packed = packed.astype(jnp.bfloat16)
+            weights = weights.astype(jnp.bfloat16).astype(jnp.float32)
+        packed = shift_grp(packed, step)
+        if step == 1:
+            packed, returned, second = lax.optimization_barrier((packed, returned, second))
+        block = packed.astype(jnp.float32)
+        for k in range(len(kept)):
+            asked[2 * step * k] = kept[k] + block[k * product_count : (k + 1) * product_count]
+        weights = weights + block[len(kept) * product_count :].reshape(weights.shape)
+        step *= 2
+    own_sum = asked[0]
+    own = weights.astype(jnp.bfloat16)
+    own, own_sum, returned = lax.optimization_barrier((own, own_sum, returned))
     returned_second = give_back(second)
     grad_scale = 1.0 / math.sqrt(slot_count * devices)
     share = width // devices
     owned = cust_grad.shape[0]
-    prod_table_grad = lax.dot_general(
-        own_sum,
-        w_prod.astype(jnp.float32),
+    high = own_sum.astype(jnp.bfloat16)
+    low_part = (own_sum - high.astype(jnp.float32)).astype(jnp.bfloat16)
+    both_parts = lax.dot_general(
+        jnp.concatenate([high, low_part]),
+        w_prod,
         (((1,), (1,)), ((), ())),
-        precision=lax.Precision.HIGHEST,
         preferred_element_type=jnp.float32,
-    ) * math.sqrt(product_count / slot_count)
+    )
+    prod_table_grad = (both_parts[:product_count] + both_parts[product_count:]) * math.sqrt(
+        product_count / slot_count
+    )
     table = owner_sum(recv_key, returned, owned, width, 0)
     own = spread(own, shift_rows, planes, 2, plane)
     own, table, prod_table_grad = lax.optimization_barrier((own, table, prod_table_grad))

time: 143 us -> 143 us (level)
    all_to_all x2, waiting for transfers between devices: 11 us -> 0.01 us  [give_back(): lax.all_to_all(rows.reshape(devices, capacity, -1), AXES, split_axis=0, c...]
    ppermute x6 -> x5, waiting for transfers between devices: 2.13 us -> 12.3 us  [shift_grp(): return lax.ppermute(value, 'grp', [(i, i ^ mask) for i in range(size)])]
    ppermute x6 -> x5, starting transfers between devices: 10.4 us -> 8.66 us  [shift_grp(): return lax.ppermute(value, 'grp', [(i, i ^ mask) for i in range(size)])]
    all_to_all x2, starting transfers between devices: 6.65 us -> 8.23 us  [give_back(): lax.all_to_all(rows.reshape(devices, capacity, -1), AXES, split_axis=0, c...]
  transfers between devices with their start and end apart: 21 -> 20, of which waited for: 9 -> 9; matrix products, arithmetic and copies ran while one was open for 2% -> 1% of each run, Pallas kernels for 22% -> 22%
where the time goes in v7:
time: 143 us; the launch traced here: 142 us
  waiting for transfers between devices  59 us (41%)
  Pallas kernels  36.6 us (26%)
  starting transfers between devices  35.2 us (25%)
  local copies, waits for them, and re-layouts  6.93 us (5%)
  other arithmetic  3.11 us (2%)
    ppermute x12, waiting for transfers between devices, shift_rows(): return lax.ppermute(value, 'rows', [(i, i ^ mask) for i in range(size)])  26.9 us
    all_to_all x1, waiting for transfers between devices, body(): lax.all_to_all(owned_rows.reshape(devices, capacity, width), AXES, split_...  19.9 us
    ppermute x5, waiting for transfers between devices, shift_grp(): return lax.ppermute(value, 'grp', [(i, i ^ mask) for i in range(size)])  12.3 us
    ppermute x12, starting transfers between devices, shift_rows(): return lax.ppermute(value, 'rows', [(i, i ^ mask) for i in range(size)])  12.2 us
    pallas_call x2, Pallas kernels, owner_sum(): pl.pallas_call(owner_sum_kernel, grid=(owned // tile,), out_shape=jax.Sha...  10.5 us
    pallas_call x2, Pallas kernels, delta_and_rows(): pl.pallas_call(functools.partial(delta_kernel, keep, at), grid=(count //...  10.5 us
    ppermute x5, starting transfers between devices, shift_grp(): return lax.ppermute(value, 'grp', [(i, i ^ mask) for i in range(size)])  8.66 us
    pallas_call x2, Pallas kernels, pick(): pl.pallas_call(pick_kernel, grid=(count // tile,), out_shape=space((count...  8.38 us
  transfers between devices with their start and end apart: 20, of which 9 were waited for; matrix products, arithmetic and copies ran while one was open for 1% of the time, Pallas kernels for 22%

profile of v7, /device:TPU:1, one launch (start us, length us, event | category | flops | bytes accessed | tf_op | source)
XLA Modules:
  0.0 142.3 jit_solution(13632201645079519192)
XLA Ops:
  0.6 2.2 %collective-permute-start = (bf16[8,512]{1,0:T(8,128)(2,1)}, bf16[8,512]{1,0:T(8,128)(2,1)S(1)}, u32[]{:S(2)}, u32[]{:S(2)}) collective-permute-start(bf16[8,512]{1,0:T(8,128)(2,1)} %param.15), channel_id=1, source_target_pairs={{0,1},{1,0},{2,3},{3,2},{4,5},{5,4},{6,7},{7,6},{8,9},{9,8},{10,11... | collective-permute-start | bytes 24584 | tf_op jit(solution)/shard_map/ppermute | solution.py:21
  2.8 2.2 %collective-permute-start.2 = (bf16[8,512]{1,0:T(8,128)(2,1)}, bf16[8,512]{1,0:T(8,128)(2,1)S(1)}, u32[]{:S(2)}, u32[]{:S(2)}) collective-permute-start(bf16[8,512]{1,0:T(8,128)(2,1)} %param.15), channel_id=1, source_target_pairs={{0,3},{1,2},{2,1},{3,0},{4,7},{5,6},{6,5},{7,4},{8,11},{9,10},{10,... | collective-permute-start | bytes 24584 | tf_op jit(solution)/shard_map/ppermute | solution.py:21
  5.1 7.4 %pick_rows.2 = bf16[2048,512]{1,0:T(8,128)(2,1)} custom-call(s32[1,2048]{1,0:T(1,128)} %bitcast.86, bf16[2048,512]{1,0:T(8,128)(2,1)} %table_ref.1), custom_call_target="tpu_custom_call" | custom-call | flops 4294967296 | bytes 4194304 | tf_op jit(solution)/shard_map/pick_rows/pallas_call | solution.py:41
  12.7 6.2 %all-to-all-start = ((bf16[32,64,512]{2,1,0:T(8,128)(2,1)}), bf16[32,64,512]{2,1,0:T(8,128)(2,1)}, u32[]{:S(2)}, u32[]{:S(2)}) async-start(bf16[32,64,512]{2,1,0:T(8,128)(2,1)} %bitcast.96), calls=%async_computation | async-start | bytes 4194304 | tf_op jit(solution)/shard_map/all_to_all | solution.py:269
  19.0 2.4 %collective-permute-start.5 = (bf16[4,8,512]{2,1,0:T(8,128)(2,1)S(1)}, bf16[4,8,512]{2,1,0:T(8,128)(2,1)S(1)}, u32[]{:S(2)}, u32[]{:S(2)}) collective-permute-start(bf16[4,8,512]{2,1,0:T(8,128)(2,1)S(1)} %bitcast_dynamic-update-slice_fusion.8), channel_id=1, source_target_pairs={{0,24},{4,28},{8,16},{12,20},{16,8},{20,12},{24,0},{28,4},{1,25},{... | collective-permute-start | bytes 98312 | tf_op jit(solution)/shard_map/ppermute | solution.py:16
  21.7 12.8 %collective-permute-done.3 = bf16[4,8,512]{2,1,0:T(8,128)(2,1)S(1)} collective-permute-done((bf16[4,8,512]{2,1,0:T(8,128)(2,1)S(1)}, bf16[4,8,512]{2,1,0:T(8,128)(2,1)S(1)}, u32[]{:S(2)}, u32[]{:S(2)}) %collective-permute-start.3) | collective-permute-done | bytes 32800 | tf_op jit(solution)/shard_map/ppermute | solution.py:16
  35.4 1.9 %collective-permute-start.6 = (bf16[4,4,8,512]{3,2,1,0:T(8,128)(2,1)S(1)}, bf16[4,4,8,512]{3,2,1,0:T(8,128)(2,1)S(1)}, u32[]{:S(2)}, u32[]{:S(2)}) collective-permute-start(bf16[4,4,8,512]{3,2,1,0:T(8,128)(2,1)S(1)} %bitcast_dynamic-update-slice_fusion.4), channel_id=1, source_target_pairs={{0,4},{4,0},{8,12},{12,8},{16,20},{20,16},{24,28},{28,24},{1,5},{5... | collective-permute-start | bytes 393224 | tf_op jit(solution)/shard_map/ppermute | solution.py:16
  37.3 1.6 %copy-done.2 = bf16[2048,512]{1,0:T(8,128)(2,1)S(1)} copy-done((bf16[2048,512]{1,0:T(8,128)(2,1)S(1)}, bf16[2048,512]{1,0:T(8,128)(2,1)}, u32[]{:S(2)}) %copy-start.2) | copy-done | bytes 2097176
  38.9 4.0 %slot_gate.1.gate_ref = f32[2048,512]{1,0:T(8,128)S(1)} custom-call(s32[1,32]{1,0:T(1,128)S(1)} %copy-done.9, bf16[2048,512]{1,0:T(8,128)(2,1)S(1)} %copy-done.1, bf16[2048,512]{1,0:T(8,128)(2,1)S(1)} %copy-done.2, bf16[512,512]{1,0:T(8,128)(2,1)S(1)} %copy-done.6, bf16[512,512]{1,0:T(8,128)(2,1)S(1)} %copy-done.7), custom_call_target="tpu_custom_call" | custom-call | flops 2147483648 | bytes 8388608 | tf_op jit(solution)/shard_map/slot_gate/pallas_call | solution.py:77
  43.0 2.0 %copy-done = f32[2048,512]{1,0:T(8,128)} copy-done((f32[2048,512]{1,0:T(8,128)}, f32[2048,512]{1,0:T(8,128)S(1)}, u32[]{:S(2)}) %copy-start) | copy-done | bytes 4194328
  46.1 1.3 copy-done.4
  47.4 19.9 %all-to-all-done = bf16[32,64,512]{2,1,0:T(8,128)(2,1)} async-done(((bf16[32,64,512]{2,1,0:T(8,128)(2,1)}), bf16[32,64,512]{2,1,0:T(8,128)(2,1)}, u32[]{:S(2)}, u32[]{:S(2)}) %all-to-all-start) | async-done | bytes 2097184 | tf_op jit(solution)/shard_map/all_to_all | solution.py:269
  67.2 5.3 %delta_and_rows.3 = bf16[2048,384]{1,0:T(8,128)(2,1)} custom-call(bf16[2048,512]{1,0:T(8,128)(2,1)} %bitcast.8.got_ref, bf16[2048,512]{1,0:T(8,128)(2,1)} %copy-done.4, f32[2048,512]{1,0:T(8,128)} %copy-done, bf16[512,512]{1,0:T(8,128)(2,1)} %weight_ref.3), custom_call_target="tpu_custom_call" | custom-call | flops 1073741824 | bytes 12582912 | tf_op jit(solution)/shard_map/delta_and_rows/pallas_call | solution.py:203
  72.6 3.4 %all-to-all-start.1 = ((bf16[32,64,384]{2,1,0:T(8,128)(2,1)}), bf16[32,64,384]{2,1,0:T(8,128)(2,1)}, u32[]{:S(2)}, u32[]{:S(2)}) async-start(bf16[32,64,384]{2,1,0:T(8,128)(2,1)} %bitcast.89), calls=%async_computation.1 | async-start | bytes 3145728 | tf_op jit(solution)/shard_map/all_to_all | solution.py:286
  76.0 5.2 %delta_and_rows.2 = (bf16[2048,128]{1,0:T(8,128)(2,1)}, bf16[2048,512]{1,0:T(8,128)(2,1)}) custom-call(bf16[2048,512]{1,0:T(8,128)(2,1)} %bitcast.8.got_ref, bf16[2048,512]{1,0:T(8,128)(2,1)} %copy-done.4, f32[2048,512]{1,0:T(8,128)} %copy-done, bf16[512,512]{1,0:T(8,128)(2,1)} %weight_ref.3), custom_call_target="tpu_custom_call" | custom-call | flops 1073741824 | bytes 12582912 | tf_op jit(solution)/shard_map/delta_and_rows/pallas_call | solution.py:203
  81.2 1.6 %copy-done.5 = bf16[2048,512]{1,0:T(8,128)(2,1)S(1)} copy-done((bf16[2048,512]{1,0:T(8,128)(2,1)S(1)}, bf16[2048,512]{1,0:T(8,128)(2,1)}, u32[]{:S(2)}) %copy-start.5) | copy-done | bytes 2097176
  82.8 1.5 %half_terms.3 = f32[640,512]{1,0:T(8,128)S(1)} custom-call(s32[1]{0:T(128)} %bitcast.16.half_ref, s32[1,2048]{1,0:T(1,128)S(1)} %bitcast.84, bf16[2048,512]{1,0:T(8,128)(2,1)S(1)} %copy-done.1, bf16[2048,512]{1,0:T(8,128)(2,1)S(1)} %copy-done.3, bf16[2048,512]{1,0:T(8,128)(2,1)S(1)} %copy-done.5), custom_call_target="tpu_custom_call" | custom-call | flops 1342177280 | bytes 4194304 | tf_op jit(solution)/shard_map/half_terms/pallas_call | solution.py:127
  84.8 1.5 %half_terms.2 = f32[640,512]{1,0:T(8,128)S(1)} custom-call(s32[1]{0:T(128)} %bitcast.half_ref, s32[1,2048]{1,0:T(1,128)S(1)} %bitcast.85, bf16[2048,512]{1,0:T(8,128)(2,1)S(1)} %copy-done.1, bf16[2048,512]{1,0:T(8,128)(2,1)S(1)} %copy-done.3, bf16[2048,512]{1,0:T(8,128)(2,1)S(1)} %copy-done.5), custom_call_target="tpu_custom_call" | custom-call | flops 1342177280 | bytes 4194304 | tf_op jit(solution)/shard_map/half_terms/pallas_call | solution.py:127
  88.0 1.6 %collective-permute-start.8 = (bf16[4,40,512]{2,1,0:T(8,128)(2,1)S(1)}, bf16[4,40,512]{2,1,0:T(8,128)(2,1)S(1)}, u32[]{:S(2)}, u32[]{:S(2)}) collective-permute-start(bf16[4,40,512]{2,1,0:T(8,128)(2,1)S(1)} %get-tuple-element.42), channel_id=1, source_target_pairs={{0,8},{4,12},{8,0},{12,4},{16,24},{20,28},{24,16},{28,20},{1,9},{5... | collective-permute-start | bytes 491528 | tf_op jit(solution)/shard_map/ppermute | solution.py:16
  91.0 5.2 %collective-permute-done.8 = bf16[4,40,512]{2,1,0:T(8,128)(2,1)S(1)} collective-permute-done((bf16[4,40,512]{2,1,0:T(8,128)(2,1)S(1)}, bf16[4,40,512]{2,1,0:T(8,128)(2,1)S(1)}, u32[]{:S(2)}, u32[]{:S(2)}) %collective-permute-start.8) | collective-permute-done | bytes 163872 | tf_op jit(solution)/shard_map/ppermute | solution.py:16
  96.2 6.1 %collective-permute-done.10 = bf16[4,40,512]{2,1,0:T(8,128)(2,1)S(1)} collective-permute-done((bf16[4,40,512]{2,1,0:T(8,128)(2,1)S(1)}, bf16[4,40,512]{2,1,0:T(8,128)(2,1)S(1)}, u32[]{:S(2)}, u32[]{:S(2)}) %collective-permute-start.10) | collective-permute-done | bytes 163872 | tf_op jit(solution)/shard_map/ppermute | solution.py:16
  102.5 2.9 %collective-permute-start.11 = (f32[144,512]{1,0:T(8,128)S(1)}, f32[144,512]{1,0:T(8,128)S(1)}, u32[]{:S(2)}, u32[]{:S(2)}) collective-permute-start(f32[144,512]{1,0:T(8,128)S(1)} %pad_maximum_fusion.1), channel_id=1, source_target_pairs={{0,1},{1,0},{2,3},{3,2},{4,5},{5,4},{6,7},{7,6},{8,9},{9,8},{10,11... | collective-permute-start | bytes 884744 | tf_op jit(solution)/shard_map/ppermute | solution.py:21
  105.4 9.6 %collective-permute-done.11 = f32[144,512]{1,0:T(8,128)S(1)} collective-permute-done((f32[144,512]{1,0:T(8,128)S(1)}, f32[144,512]{1,0:T(8,128)S(1)}, u32[]{:S(2)}, u32[]{:S(2)}) %collective-permute-start.11) | collective-permute-done | bytes 294944 | tf_op jit(solution)/shard_map/ppermute | solution.py:21
  115.1 1.2 collective-permute-start.12
  116.4 4.8 %all-to-all-start.2 = ((bf16[32,64,128]{2,1,0:T(8,128)(2,1)}), bf16[32,64,128]{2,1,0:T(8,128)(2,1)S(1)}, u32[]{:S(2)}, u32[]{:S(2)}) async-start(bf16[32,64,128]{2,1,0:T(8,128)(2,1)} %bitcast.38), calls=%async_computation.2 | async-start | bytes 1048576 | tf_op jit(solution)/shard_map/all_to_all | solution.py:286
  121.2 2.7 %collective-permute-done.12 = bf16[136,512]{1,0:T(8,128)(2,1)S(1)} collective-permute-done((bf16[136,512]{1,0:T(8,128)(2,1)S(1)}, bf16[136,512]{1,0:T(8,128)(2,1)S(1)}, u32[]{:S(2)}, u32[]{:S(2)}) %collective-permute-start.12) | collective-permute-done | bytes 139296 | tf_op jit(solution)/shard_map/ppermute | solution.py:21
  124.0 1.5 %collective-permute-start.15 = (bf16[4,32,512]{2,1,0:T(8,128)(2,1)S(1)}, bf16[4,32,512]{2,1,0:T(8,128)(2,1)S(1)}, u32[]{:S(2)}, u32[]{:S(2)}) collective-permute-start(bf16[4,32,512]{2,1,0:T(8,128)(2,1)S(1)} %add_convert_fusion), channel_id=1, source_target_pairs={{0,24},{4,28},{8,16},{12,20},{16,8},{20,12},{24,0},{28,4},{1,25},{... | collective-permute-start | bytes 393224 | tf_op jit(solution)/shard_map/ppermute | solution.py:16
  125.5 1.2 collective-permute-start.13
  126.8 7.2 %owner_sum.2.refs_0_ = f32[2048,512]{1,0:T(8,128)} custom-call(s32[1,2048]{1,0:T(1,128)S(1)} %bitcast.87, bf16[2048,384]{1,0:T(8,128)(2,1)} %bitcast.28.rows_ref), custom_call_target="tpu_custom_call" | custom-call | tf_op jit(solution)/shard_map/owner_sum/pallas_call | solution.py:170
  135.8 1.5 %collective-permute-start.16 = (bf16[4,4,32,512]{3,2,1,0:T(8,128)(2,1)S(1)}, bf16[4,4,32,512]{3,2,1,0:T(8,128)(2,1)S(1)}, u32[]{:S(2)}, u32[]{:S(2)}) collective-permute-start(bf16[4,4,32,512]{3,2,1,0:T(8,128)(2,1)S(1)} %bitcast_dynamic-update-slice_fusion), channel_id=1, source_target_pairs={{0,4},{4,0},{8,12},{12,8},{16,20},{20,16},{24,28},{28,24},{1,5},{5... | collective-permute-start | bytes 1572872 | tf_op jit(solution)/shard_map/ppermute | solution.py:16
  137.3 3.3 %owner_sum.3 = f32[2048,512]{1,0:T(8,128)} custom-call(s32[1,2048]{1,0:T(1,128)S(1)} %bitcast.88, bf16[2048,128]{1,0:T(8,128)(2,1)S(1)} %bitcast.81, f32[2048,512]{1,0:T(8,128)} %owner_sum.2.refs_0_), custom_call_target="tpu_custom_call", output_to_operand_aliasing={{}: (2, {})} | custom-call | flops 1073741824 | bytes 1572864 | tf_op jit(solution)/shard_map/owner_sum/pallas_call | solution.py:170
  140.7 1.6 %convert_multiply_fusion = (f32[2,4,4,16,512]{4,3,2,1,0:T(8,128)}, f32[2,4,4,16,512]{4,3,2,1,0:T(8,128)}) fusion(bf16[1,4,4,16,512]{4,3,2,1,0:T(8,128)(2,1)S(1)} %get-tuple-element.40, bf16[1,4,4,16,512]{4,3,2,1,0:T(8,128)(2,1)S(1)} %get-tuple-element.38, bf16[1,4,4,16,512]{4,3,2,1,0:T(8,128)(2,1)S(1)} %get-tuple-element.39, ...), kind=kLoop, calls=%fused_computation.1 | loop fusion | flops 1572864 | bytes 3145728 | tf_op jit(solution)/shard_map/mul | solution.py:359
  (83 shorter events, 8.1 us)
Async XLA Ops:
  0.6 11.9 %collective-permute-start = (bf16[8,512]{1,0:T(8,128)(2,1)}, bf16[8,512]{1,0:T(8,128)(2,1)S(1)}, u32[]{:S(2)}, u32[]{:S(2)}) collective-permute-start(bf16[8,512]{1,0:T(8,128)(2,1)} %param.15), channel_id=1, source_target_pairs={{0,1},{1,0},{2,3},{3,2},{4,5},{5,4},{6,7},{7,6},{8,9},{9,8},{10,11... | collective-permute-start | bytes 24584 | tf_op jit(solution)/shard_map/ppermute | solution.py:21
  2.8 9.8 %collective-permute-start.2 = (bf16[8,512]{1,0:T(8,128)(2,1)}, bf16[8,512]{1,0:T(8,128)(2,1)S(1)}, u32[]{:S(2)}, u32[]{:S(2)}) collective-permute-start(bf16[8,512]{1,0:T(8,128)(2,1)} %param.15), channel_id=1, source_target_pairs={{0,3},{1,2},{2,1},{3,0},{4,7},{5,6},{6,5},{7,4},{8,11},{9,10},{10,... | collective-permute-start | bytes 24584 | tf_op jit(solution)/shard_map/ppermute | solution.py:21
  5.0 7.6 %collective-permute-start.1 = (bf16[8,512]{1,0:T(8,128)(2,1)}, bf16[8,512]{1,0:T(8,128)(2,1)S(1)}, u32[]{:S(2)}, u32[]{:S(2)}) collective-permute-start(bf16[8,512]{1,0:T(8,128)(2,1)} %param.15), channel_id=1, source_target_pairs={{0,2},{1,3},{2,0},{3,1},{4,6},{5,7},{6,4},{7,5},{8,10},{9,11},{10,... | collective-permute-start | bytes 24584 | tf_op jit(solution)/shard_map/ppermute | solution.py:21
  5.1 7.4 %copy-start.10 = (bf16[8,512]{1,0:T(8,128)(2,1)S(1)}, bf16[8,512]{1,0:T(8,128)(2,1)}, u32[]{:S(2)}) copy-start(bf16[8,512]{1,0:T(8,128)(2,1)} %param.15) | copy-start | bytes 24580
  12.6 6.3 %copy-start.11 = (s32[2048]{0:T(1024)S(1)}, s32[2048]{0:T(1024)}, u32[]{:S(2)}) copy-start(s32[2048]{0:T(1024)} %param.13) | copy-start | bytes 24580
  12.6 24.7 %copy-start.1 = (bf16[2048,512]{1,0:T(8,128)(2,1)S(1)}, bf16[2048,512]{1,0:T(8,128)(2,1)}, u32[]{:S(2)}) copy-start(bf16[2048,512]{1,0:T(8,128)(2,1)} %hc_ref.5) | copy-start | bytes 6291460
  12.7 24.6 %copy-start.6 = (bf16[512,512]{1,0:T(8,128)(2,1)S(1)}, bf16[512,512]{1,0:T(8,128)(2,1)}, u32[]{:S(2)}) copy-start(bf16[512,512]{1,0:T(8,128)(2,1)} %weight_ref.3) | copy-start | bytes 1572868
  12.7 24.6 %copy-start.7 = (bf16[512,512]{1,0:T(8,128)(2,1)S(1)}, bf16[512,512]{1,0:T(8,128)(2,1)}, u32[]{:S(2)}) copy-start(bf16[512,512]{1,0:T(8,128)(2,1)} %wp_ref.1) | copy-start | bytes 1572868
  12.7 24.6 %copy-start.9 = (s32[1,32]{1,0:T(1,128)S(1)}, s32[1,32]{1,0:T(1,128)}, u32[]{:S(2)}) copy-start(s32[1,32]{1,0:T(1,128)} %count_ref.1) | copy-start | bytes 388
  12.7 54.5 %all-to-all-start = ((bf16[32,64,512]{2,1,0:T(8,128)(2,1)}), bf16[32,64,512]{2,1,0:T(8,128)(2,1)}, u32[]{:S(2)}, u32[]{:S(2)}) async-start(bf16[32,64,512]{2,1,0:T(8,128)(2,1)} %bitcast.96), calls=%async_computation | async-start | bytes 4194304 | tf_op jit(solution)/shard_map/all_to_all | solution.py:269
  19.0 16.4 %collective-permute-start.5 = (bf16[4,8,512]{2,1,0:T(8,128)(2,1)S(1)}, bf16[4,8,512]{2,1,0:T(8,128)(2,1)S(1)}, u32[]{:S(2)}, u32[]{:S(2)}) collective-permute-start(bf16[4,8,512]{2,1,0:T(8,128)(2,1)S(1)} %bitcast_dynamic-update-slice_fusion.8), channel_id=1, source_target_pairs={{0,24},{4,28},{8,16},{12,20},{16,8},{20,12},{24,0},{28,4},{1,25},{... | collective-permute-start | bytes 98312 | tf_op jit(solution)/shard_map/ppermute | solution.py:16
  21.4 13.2 %collective-permute-start.4 = (bf16[4,8,512]{2,1,0:T(8,128)(2,1)S(1)}, bf16[4,8,512]{2,1,0:T(8,128)(2,1)S(1)}, u32[]{:S(2)}, u32[]{:S(2)}) collective-permute-start(bf16[4,8,512]{2,1,0:T(8,128)(2,1)S(1)} %bitcast_dynamic-update-slice_fusion.8), channel_id=1, source_target_pairs={{0,16},{4,20},{8,24},{12,28},{16,0},{20,4},{24,8},{28,12},{1,17},{... | collective-permute-start | bytes 98312 | tf_op jit(solution)/shard_map/ppermute | solution.py:16
  21.6 12.9 %collective-permute-start.3 = (bf16[4,8,512]{2,1,0:T(8,128)(2,1)S(1)}, bf16[4,8,512]{2,1,0:T(8,128)(2,1)S(1)}, u32[]{:S(2)}, u32[]{:S(2)}) collective-permute-start(bf16[4,8,512]{2,1,0:T(8,128)(2,1)S(1)} %bitcast_dynamic-update-slice_fusion.8), channel_id=1, source_target_pairs={{0,8},{4,12},{8,0},{12,4},{16,24},{20,28},{24,16},{28,20},{1,9},{5... | collective-permute-start | bytes 98312 | tf_op jit(solution)/shard_map/ppermute | solution.py:16
  35.4 9.6 %collective-permute-start.6 = (bf16[4,4,8,512]{3,2,1,0:T(8,128)(2,1)S(1)}, bf16[4,4,8,512]{3,2,1,0:T(8,128)(2,1)S(1)}, u32[]{:S(2)}, u32[]{:S(2)}) collective-permute-start(bf16[4,4,8,512]{3,2,1,0:T(8,128)(2,1)S(1)} %bitcast_dynamic-update-slice_fusion.4), channel_id=1, source_target_pairs={{0,4},{4,0},{8,12},{12,8},{16,20},{20,16},{24,28},{28,24},{1,5},{5... | collective-permute-start | bytes 393224 | tf_op jit(solution)/shard_map/ppermute | solution.py:16
  37.3 1.6 %copy-start.2 = (bf16[2048,512]{1,0:T(8,128)(2,1)S(1)}, bf16[2048,512]{1,0:T(8,128)(2,1)}, u32[]{:S(2)}) copy-start(bf16[2048,512]{1,0:T(8,128)(2,1)} %hp_ref.5) | copy-start | bytes 6291460
  43.0 2.0 %copy-start = (f32[2048,512]{1,0:T(8,128)}, f32[2048,512]{1,0:T(8,128)S(1)}, u32[]{:S(2)}) copy-start(f32[2048,512]{1,0:T(8,128)S(1)} %slot_gate.1.gate_ref) | copy-start | bytes 12582916
  46.1 1.3 copy-start.4
  72.6 42.5 %all-to-all-start.1 = ((bf16[32,64,384]{2,1,0:T(8,128)(2,1)}), bf16[32,64,384]{2,1,0:T(8,128)(2,1)}, u32[]{:S(2)}, u32[]{:S(2)}) async-start(bf16[32,64,384]{2,1,0:T(8,128)(2,1)} %bitcast.89), calls=%async_computation.1 | async-start | bytes 3145728 | tf_op jit(solution)/shard_map/all_to_all | solution.py:286
  76.0 5.2 %copy-start.3 = (bf16[2048,512]{1,0:T(8,128)(2,1)S(1)}, bf16[2048,512]{1,0:T(8,128)(2,1)}, u32[]{:S(2)}) copy-start(bf16[2048,512]{1,0:T(8,128)(2,1)} %hp_ref.5) | copy-start | bytes 6291460
  81.2 1.6 %copy-start.5 = (bf16[2048,512]{1,0:T(8,128)(2,1)S(1)}, bf16[2048,512]{1,0:T(8,128)(2,1)}, u32[]{:S(2)}) copy-start(bf16[2048,512]{1,0:T(8,128)(2,1)} %get-tuple-element.21.delta_ref) | copy-start | bytes 6291460
  84.3 3.1 %collective-permute-start.7 = (f32[640,512]{1,0:T(8,128)S(1)}, f32[640,512]{1,0:T(8,128)S(1)}, u32[]{:S(2)}, u32[]{:S(2)}) collective-permute-start(f32[640,512]{1,0:T(8,128)S(1)} %half_terms.3), channel_id=1, source_target_pairs={{0,4},{4,0},{8,12},{12,8},{16,20},{20,16},{24,28},{28,24},{1,5},{5... | collective-permute-start | bytes 3932168 | tf_op jit(solution)/shard_map/ppermute | solution.py:16
  88.0 8.2 %collective-permute-start.8 = (bf16[4,40,512]{2,1,0:T(8,128)(2,1)S(1)}, bf16[4,40,512]{2,1,0:T(8,128)(2,1)S(1)}, u32[]{:S(2)}, u32[]{:S(2)}) collective-permute-start(bf16[4,40,512]{2,1,0:T(8,128)(2,1)S(1)} %get-tuple-element.42), channel_id=1, source_target_pairs={{0,8},{4,12},{8,0},{12,4},{16,24},{20,28},{24,16},{28,20},{1,9},{5... | collective-permute-start | bytes 491528 | tf_op jit(solution)/shard_map/ppermute | solution.py:16
  89.6 12.7 %collective-permute-start.10 = (bf16[4,40,512]{2,1,0:T(8,128)(2,1)S(1)}, bf16[4,40,512]{2,1,0:T(8,128)(2,1)S(1)}, u32[]{:S(2)}, u32[]{:S(2)}) collective-permute-start(bf16[4,40,512]{2,1,0:T(8,128)(2,1)S(1)} %get-tuple-element.43), channel_id=1, source_target_pairs={{0,24},{4,28},{8,16},{12,20},{16,8},{20,12},{24,0},{28,4},{1,25},{... | collective-permute-start | bytes 491528 | tf_op jit(solution)/shard_map/ppermute | solution.py:16
  90.6 11.7 %collective-permute-start.9 = (bf16[4,40,512]{2,1,0:T(8,128)(2,1)S(1)}, bf16[4,40,512]{2,1,0:T(8,128)(2,1)S(1)}, u32[]{:S(2)}, u32[]{:S(2)}) collective-permute-start(bf16[4,40,512]{2,1,0:T(8,128)(2,1)S(1)} %get-tuple-element.44), channel_id=1, source_target_pairs={{0,16},{4,20},{8,24},{12,28},{16,0},{20,4},{24,8},{28,12},{1,17},{... | collective-permute-start | bytes 491528 | tf_op jit(solution)/shard_map/ppermute | solution.py:16
  102.5 12.5 %collective-permute-start.11 = (f32[144,512]{1,0:T(8,128)S(1)}, f32[144,512]{1,0:T(8,128)S(1)}, u32[]{:S(2)}, u32[]{:S(2)}) collective-permute-start(f32[144,512]{1,0:T(8,128)S(1)} %pad_maximum_fusion.1), channel_id=1, source_target_pairs={{0,1},{1,0},{2,3},{3,2},{4,5},{5,4},{6,7},{7,6},{8,9},{9,8},{10,11... | collective-permute-start | bytes 884744 | tf_op jit(solution)/shard_map/ppermute | solution.py:21
  115.1 8.7 %collective-permute-start.12 = (bf16[136,512]{1,0:T(8,128)(2,1)S(1)}, bf16[136,512]{1,0:T(8,128)(2,1)S(1)}, u32[]{:S(2)}, u32[]{:S(2)}) collective-permute-start(bf16[136,512]{1,0:T(8,128)(2,1)S(1)} %pad_maximum_fusion.3), channel_id=1, source_target_pairs={{0,2},{1,3},{2,0},{3,1},{4,6},{5,7},{6,4},{7,5},{8,10},{9,11},{10,... | collective-permute-start | bytes 417800 | tf_op jit(solution)/shard_map/ppermute | solution.py:21
  116.4 20.9 %all-to-all-start.2 = ((bf16[32,64,128]{2,1,0:T(8,128)(2,1)}), bf16[32,64,128]{2,1,0:T(8,128)(2,1)S(1)}, u32[]{:S(2)}, u32[]{:S(2)}) async-start(bf16[32,64,128]{2,1,0:T(8,128)(2,1)} %bitcast.38), calls=%async_computation.2 | async-start | bytes 1048576 | tf_op jit(solution)/shard_map/all_to_all | solution.py:286
  121.2 5.6 %copy-start.8 = (s32[2048]{0:T(1024)S(1)}, s32[2048]{0:T(1024)}, u32[]{:S(2)}) copy-start(s32[2048]{0:T(1024)} %param.12) | copy-start | bytes 24580
  124.0 11.8 %collective-permute-start.15 = (bf16[4,32,512]{2,1,0:T(8,128)(2,1)S(1)}, bf16[4,32,512]{2,1,0:T(8,128)(2,1)S(1)}, u32[]{:S(2)}, u32[]{:S(2)}) collective-permute-start(bf16[4,32,512]{2,1,0:T(8,128)(2,1)S(1)} %add_convert_fusion), channel_id=1, source_target_pairs={{0,24},{4,28},{8,16},{12,20},{16,8},{20,12},{24,0},{28,4},{1,25},{... | collective-permute-start | bytes 393224 | tf_op jit(solution)/shard_map/ppermute | solution.py:16
  125.5 10.2 %collective-permute-start.14 = (bf16[4,32,512]{2,1,0:T(8,128)(2,1)S(1)}, bf16[4,32,512]{2,1,0:T(8,128)(2,1)S(1)}, u32[]{:S(2)}, u32[]{:S(2)}) collective-permute-start(bf16[4,32,512]{2,1,0:T(8,128)(2,1)S(1)} %add_convert_fusion), channel_id=1, source_target_pairs={{0,16},{4,20},{8,24},{12,28},{16,0},{20,4},{24,8},{28,12},{1,17},{... | collective-permute-start | bytes 393224 | tf_op jit(solution)/shard_map/ppermute | solution.py:16
  125.5 9.4 %collective-permute-start.13 = (bf16[4,32,512]{2,1,0:T(8,128)(2,1)S(1)}, bf16[4,32,512]{2,1,0:T(8,128)(2,1)S(1)}, u32[]{:S(2)}, u32[]{:S(2)}) collective-permute-start(bf16[4,32,512]{2,1,0:T(8,128)(2,1)S(1)} %add_convert_fusion), channel_id=1, source_target_pairs={{0,8},{4,12},{8,0},{12,4},{16,24},{20,28},{24,16},{28,20},{1,9},{5... | collective-permute-start | bytes 393224 | tf_op jit(solution)/shard_map/ppermute | solution.py:16
  135.8 4.8 %collective-permute-start.16 = (bf16[4,4,32,512]{3,2,1,0:T(8,128)(2,1)S(1)}, bf16[4,4,32,512]{3,2,1,0:T(8,128)(2,1)S(1)}, u32[]{:S(2)}, u32[]{:S(2)}) collective-permute-start(bf16[4,4,32,512]{3,2,1,0:T(8,128)(2,1)S(1)} %bitcast_dynamic-update-slice_fusion), channel_id=1, source_target_pairs={{0,4},{4,0},{8,12},{12,8},{16,20},{20,16},{24,28},{28,24},{1,5},{5... | collective-permute-start | bytes 1572872 | tf_op jit(solution)/shard_map/ppermute | solution.py:16

commit v8 on v6

--- a/solution.py
+++ b/solution.py
@@ -331,13 +331,17 @@
     grad_scale = 1.0 / math.sqrt(slot_count * devices)
     share = width // devices
     owned = cust_grad.shape[0]
-    prod_table_grad = lax.dot_general(
-        own_sum,
-        w_prod.astype(jnp.float32),
+    high = own_sum.astype(jnp.bfloat16)
+    low_part = (own_sum - high.astype(jnp.float32)).astype(jnp.bfloat16)
+    both_parts = lax.dot_general(
+        jnp.concatenate([high, low_part]),
+        w_prod,
         (((1,), (1,)), ((), ())),
-        precision=lax.Precision.HIGHEST,
         preferred_element_type=jnp.float32,
-    ) * math.sqrt(product_count / slot_count)
+    )
+    prod_table_grad = (both_parts[:product_count] + both_parts[product_count:]) * math.sqrt(
+        product_count / slot_count
+    )
     table = owner_sum(recv_key, returned, owned, width, 0)
     own = spread(own, shift_rows, planes, 2, plane)
     own, table, prod_table_grad = lax.optimization_barrier((own, table, prod_table_grad))

time: 143 us -> 143 us (level)
  transfers between devices with their start and end apart: 21 -> 21, of which waited for: 9 -> 9; matrix products, arithmetic and copies ran while one was open for 2% -> 1% of each run, Pallas kernels for 22% -> 22%
where the time goes in v8:
time: 143 us
  waiting for transfers between devices  59.5 us (42%)
  Pallas kernels  36.5 us (26%)
  starting transfers between devices  35.5 us (25%)
  local copies, waits for them, and re-layouts  6.9 us (5%)
  other arithmetic  3.1 us (2%)
    ppermute x12, waiting for transfers between devices, shift_rows(): return lax.ppermute(value, 'rows', [(i, i ^ mask) for i in range(size)])  26.6 us
    all_to_all x1, waiting for transfers between devices, body(): lax.all_to_all(owned_rows.reshape(devices, capacity, width), AXES, split_...  19.9 us
    ppermute x12, starting transfers between devices, shift_rows(): return lax.ppermute(value, 'rows', [(i, i ^ mask) for i in range(size)])  12.3 us
    all_to_all x2, waiting for transfers between devices, give_back(): lax.all_to_all(rows.reshape(devices, capacity, -1), AXES, split_axis=0, c...  11 us
    pallas_call x2, Pallas kernels, delta_and_rows(): pl.pallas_call(functools.partial(delta_kernel, keep, at), grid=(count //...  10.5 us
    pallas_call x2, Pallas kernels, owner_sum(): pl.pallas_call(owner_sum_kernel, grid=(owned // tile,), out_shape=jax.Sha...  10.5 us
    ppermute x6, starting transfers between devices, shift_grp(): return lax.ppermute(value, 'grp', [(i, i ^ mask) for i in range(size)])  10.4 us
    pallas_call x2, Pallas kernels, pick(): pl.pallas_call(pick_kernel, grid=(count // tile,), out_shape=space((count...  8.37 us
  transfers between devices with their start and end apart: 21, of which 9 were waited for; matrix products, arithmetic and copies ran while one was open for 1% of the time, Pallas kernels for 22%

profile of v8, /device:TPU:1, one launch (start us, length us, event | category | flops | bytes accessed | tf_op | source)
XLA Modules:
  0.0 142.9 jit_solution(15783361467290987274)
XLA Ops:
  0.6 2.2 %collective-permute-start = (bf16[8,512]{1,0:T(8,128)(2,1)}, bf16[8,512]{1,0:T(8,128)(2,1)S(1)}, u32[]{:S(2)}, u32[]{:S(2)}) collective-permute-start(bf16[8,512]{1,0:T(8,128)(2,1)} %param.15), channel_id=1, source_target_pairs={{0,1},{1,0},{2,3},{3,2},{4,5},{5,4},{6,7},{7,6},{8,9},{9,8},{10,11... | collective-permute-start | bytes 24584 | tf_op jit(solution)/shard_map/ppermute | solution.py:21
  2.8 2.2 %collective-permute-start.2 = (bf16[8,512]{1,0:T(8,128)(2,1)}, bf16[8,512]{1,0:T(8,128)(2,1)S(1)}, u32[]{:S(2)}, u32[]{:S(2)}) collective-permute-start(bf16[8,512]{1,0:T(8,128)(2,1)} %param.15), channel_id=1, source_target_pairs={{0,3},{1,2},{2,1},{3,0},{4,7},{5,6},{6,5},{7,4},{8,11},{9,10},{10,... | collective-permute-start | bytes 24584 | tf_op jit(solution)/shard_map/ppermute | solution.py:21
  5.1 7.4 %pick_rows.2 = bf16[2048,512]{1,0:T(8,128)(2,1)} custom-call(s32[1,2048]{1,0:T(1,128)} %bitcast.91, bf16[2048,512]{1,0:T(8,128)(2,1)} %table_ref.1), custom_call_target="tpu_custom_call" | custom-call | flops 4294967296 | bytes 4194304 | tf_op jit(solution)/shard_map/pick_rows/pallas_call | solution.py:41
  12.7 6.2 %all-to-all-start = ((bf16[32,64,512]{2,1,0:T(8,128)(2,1)}), bf16[32,64,512]{2,1,0:T(8,128)(2,1)}, u32[]{:S(2)}, u32[]{:S(2)}) async-start(bf16[32,64,512]{2,1,0:T(8,128)(2,1)} %bitcast.101), calls=%async_computation | async-start | bytes 4194304 | tf_op jit(solution)/shard_map/all_to_all | solution.py:269
  19.0 2.4 %collective-permute-start.5 = (bf16[4,8,512]{2,1,0:T(8,128)(2,1)S(1)}, bf16[4,8,512]{2,1,0:T(8,128)(2,1)S(1)}, u32[]{:S(2)}, u32[]{:S(2)}) collective-permute-start(bf16[4,8,512]{2,1,0:T(8,128)(2,1)S(1)} %bitcast_dynamic-update-slice_fusion.8), channel_id=1, source_target_pairs={{0,24},{4,28},{8,16},{12,20},{16,8},{20,12},{24,0},{28,4},{1,25},{... | collective-permute-start | bytes 98312 | tf_op jit(solution)/shard_map/ppermute | solution.py:16
  21.7 12.8 %collective-permute-done.3 = bf16[4,8,512]{2,1,0:T(8,128)(2,1)S(1)} collective-permute-done((bf16[4,8,512]{2,1,0:T(8,128)(2,1)S(1)}, bf16[4,8,512]{2,1,0:T(8,128)(2,1)S(1)}, u32[]{:S(2)}, u32[]{:S(2)}) %collective-permute-start.3) | collective-permute-done | bytes 32800 | tf_op jit(solution)/shard_map/ppermute | solution.py:16
  35.4 1.9 %collective-permute-start.6 = (bf16[4,4,8,512]{3,2,1,0:T(8,128)(2,1)S(1)}, bf16[4,4,8,512]{3,2,1,0:T(8,128)(2,1)S(1)}, u32[]{:S(2)}, u32[]{:S(2)}) collective-permute-start(bf16[4,4,8,512]{3,2,1,0:T(8,128)(2,1)S(1)} %bitcast_dynamic-update-slice_fusion.4), channel_id=1, source_target_pairs={{0,4},{4,0},{8,12},{12,8},{16,20},{20,16},{24,28},{28,24},{1,5},{5... | collective-permute-start | bytes 393224 | tf_op jit(solution)/shard_map/ppermute | solution.py:16
  37.3 1.6 %copy-done.2 = bf16[2048,512]{1,0:T(8,128)(2,1)S(1)} copy-done((bf16[2048,512]{1,0:T(8,128)(2,1)S(1)}, bf16[2048,512]{1,0:T(8,128)(2,1)}, u32[]{:S(2)}) %copy-start.2) | copy-done | bytes 2097176
  38.9 4.0 %slot_gate.1.gate_ref = f32[2048,512]{1,0:T(8,128)S(1)} custom-call(s32[1,32]{1,0:T(1,128)S(1)} %copy-done.9, bf16[2048,512]{1,0:T(8,128)(2,1)S(1)} %copy-done.1, bf16[2048,512]{1,0:T(8,128)(2,1)S(1)} %copy-done.2, bf16[512,512]{1,0:T(8,128)(2,1)S(1)} %copy-done.6, bf16[512,512]{1,0:T(8,128)(2,1)S(1)} %copy-done.7), custom_call_target="tpu_custom_call" | custom-call | flops 2147483648 | bytes 8388608 | tf_op jit(solution)/shard_map/slot_gate/pallas_call | solution.py:77
  43.0 2.0 %copy-done = f32[2048,512]{1,0:T(8,128)} copy-done((f32[2048,512]{1,0:T(8,128)}, f32[2048,512]{1,0:T(8,128)S(1)}, u32[]{:S(2)}) %copy-start) | copy-done | bytes 4194328
  46.1 1.3 copy-done.4
  47.4 19.9 %all-to-all-done = bf16[32,64,512]{2,1,0:T(8,128)(2,1)} async-done(((bf16[32,64,512]{2,1,0:T(8,128)(2,1)}), bf16[32,64,512]{2,1,0:T(8,128)(2,1)}, u32[]{:S(2)}, u32[]{:S(2)}) %all-to-all-start) | async-done | bytes 2097184 | tf_op jit(solution)/shard_map/all_to_all | solution.py:269
  67.2 5.3 %delta_and_rows.3 = bf16[2048,384]{1,0:T(8,128)(2,1)} custom-call(bf16[2048,512]{1,0:T(8,128)(2,1)} %bitcast.8.got_ref, bf16[2048,512]{1,0:T(8,128)(2,1)} %copy-done.4, f32[2048,512]{1,0:T(8,128)} %copy-done, bf16[512,512]{1,0:T(8,128)(2,1)} %weight_ref.3), custom_call_target="tpu_custom_call" | custom-call | flops 1073741824 | bytes 12582912 | tf_op jit(solution)/shard_map/delta_and_rows/pallas_call | solution.py:203
  72.5 3.4 %all-to-all-start.1 = ((bf16[32,64,384]{2,1,0:T(8,128)(2,1)}), bf16[32,64,384]{2,1,0:T(8,128)(2,1)}, u32[]{:S(2)}, u32[]{:S(2)}) async-start(bf16[32,64,384]{2,1,0:T(8,128)(2,1)} %bitcast.94), calls=%async_computation.1 | async-start | bytes 3145728 | tf_op jit(solution)/shard_map/all_to_all | solution.py:286
  76.0 5.2 %delta_and_rows.2 = (bf16[2048,128]{1,0:T(8,128)(2,1)}, bf16[2048,512]{1,0:T(8,128)(2,1)}) custom-call(bf16[2048,512]{1,0:T(8,128)(2,1)} %bitcast.8.got_ref, bf16[2048,512]{1,0:T(8,128)(2,1)} %copy-done.4, f32[2048,512]{1,0:T(8,128)} %copy-done, bf16[512,512]{1,0:T(8,128)(2,1)} %weight_ref.3), custom_call_target="tpu_custom_call" | custom-call | flops 1073741824 | bytes 12582912 | tf_op jit(solution)/shard_map/delta_and_rows/pallas_call | solution.py:203
  81.2 1.6 %copy-done.5 = bf16[2048,512]{1,0:T(8,128)(2,1)S(1)} copy-done((bf16[2048,512]{1,0:T(8,128)(2,1)S(1)}, bf16[2048,512]{1,0:T(8,128)(2,1)}, u32[]{:S(2)}) %copy-start.5) | copy-done | bytes 2097176
  82.8 1.5 %half_terms.3 = f32[640,512]{1,0:T(8,128)S(1)} custom-call(s32[1]{0:T(128)} %bitcast.16.half_ref, s32[1,2048]{1,0:T(1,128)S(1)} %bitcast.89, bf16[2048,512]{1,0:T(8,128)(2,1)S(1)} %copy-done.1, bf16[2048,512]{1,0:T(8,128)(2,1)S(1)} %copy-done.3, bf16[2048,512]{1,0:T(8,128)(2,1)S(1)} %copy-done.5), custom_call_target="tpu_custom_call" | custom-call | flops 1342177280 | bytes 4194304 | tf_op jit(solution)/shard_map/half_terms/pallas_call | solution.py:127
  84.8 1.5 %half_terms.2 = f32[640,512]{1,0:T(8,128)S(1)} custom-call(s32[1]{0:T(128)} %bitcast.half_ref, s32[1,2048]{1,0:T(1,128)S(1)} %bitcast.90, bf16[2048,512]{1,0:T(8,128)(2,1)S(1)} %copy-done.1, bf16[2048,512]{1,0:T(8,128)(2,1)S(1)} %copy-done.3, bf16[2048,512]{1,0:T(8,128)(2,1)S(1)} %copy-done.5), custom_call_target="tpu_custom_call" | custom-call | flops 1342177280 | bytes 4194304 | tf_op jit(solution)/shard_map/half_terms/pallas_call | solution.py:127
  88.0 1.6 %collective-permute-start.8 = (bf16[4,40,512]{2,1,0:T(8,128)(2,1)S(1)}, bf16[4,40,512]{2,1,0:T(8,128)(2,1)S(1)}, u32[]{:S(2)}, u32[]{:S(2)}) collective-permute-start(bf16[4,40,512]{2,1,0:T(8,128)(2,1)S(1)} %get-tuple-element.40), channel_id=1, source_target_pairs={{0,8},{4,12},{8,0},{12,4},{16,24},{20,28},{24,16},{28,20},{1,9},{5... | collective-permute-start | bytes 491528 | tf_op jit(solution)/shard_map/ppermute | solution.py:16
  91.0 5.2 %collective-permute-done.8 = bf16[4,40,512]{2,1,0:T(8,128)(2,1)S(1)} collective-permute-done((bf16[4,40,512]{2,1,0:T(8,128)(2,1)S(1)}, bf16[4,40,512]{2,1,0:T(8,128)(2,1)S(1)}, u32[]{:S(2)}, u32[]{:S(2)}) %collective-permute-start.8) | collective-permute-done | bytes 163872 | tf_op jit(solution)/shard_map/ppermute | solution.py:16
  96.2 6.1 %collective-permute-done.10 = bf16[4,40,512]{2,1,0:T(8,128)(2,1)S(1)} collective-permute-done((bf16[4,40,512]{2,1,0:T(8,128)(2,1)S(1)}, bf16[4,40,512]{2,1,0:T(8,128)(2,1)S(1)}, u32[]{:S(2)}, u32[]{:S(2)}) %collective-permute-start.10) | collective-permute-done | bytes 163872 | tf_op jit(solution)/shard_map/ppermute | solution.py:16
  102.5 3.3 %collective-permute-start.13 = (bf16[136,512]{1,0:T(8,128)(2,1)S(1)}, bf16[136,512]{1,0:T(8,128)(2,1)S(1)}, u32[]{:S(2)}, u32[]{:S(2)}) collective-permute-start(bf16[136,512]{1,0:T(8,128)(2,1)S(1)} %get-tuple-element.45), channel_id=1, source_target_pairs={{0,3},{1,2},{2,1},{3,0},{4,7},{5,6},{6,5},{7,4},{8,11},{9,10},{10,... | collective-permute-start | bytes 417800 | tf_op jit(solution)/shard_map/ppermute | solution.py:21
  105.8 2.4 %collective-permute-start.12 = (bf16[136,512]{1,0:T(8,128)(2,1)S(1)}, bf16[136,512]{1,0:T(8,128)(2,1)S(1)}, u32[]{:S(2)}, u32[]{:S(2)}) collective-permute-start(bf16[136,512]{1,0:T(8,128)(2,1)S(1)} %get-tuple-element.46), channel_id=1, source_target_pairs={{0,2},{1,3},{2,0},{3,1},{4,6},{5,7},{6,4},{7,5},{8,10},{9,11},{10,... | collective-permute-start | bytes 417800 | tf_op jit(solution)/shard_map/ppermute | solution.py:21
  108.4 11.0 %all-to-all-done.1 = bf16[32,64,384]{2,1,0:T(8,128)(2,1)} async-done(((bf16[32,64,384]{2,1,0:T(8,128)(2,1)}), bf16[32,64,384]{2,1,0:T(8,128)(2,1)}, u32[]{:S(2)}, u32[]{:S(2)}) %all-to-all-start.1) | async-done | bytes 1572896 | tf_op jit(solution)/shard_map/all_to_all | solution.py:286
  119.4 3.2 %all-to-all-start.2 = ((bf16[32,64,128]{2,1,0:T(8,128)(2,1)}), bf16[32,64,128]{2,1,0:T(8,128)(2,1)S(1)}, u32[]{:S(2)}, u32[]{:S(2)}) async-start(bf16[32,64,128]{2,1,0:T(8,128)(2,1)} %bitcast.37), calls=%async_computation.2 | async-start | bytes 1048576 | tf_op jit(solution)/shard_map/all_to_all | solution.py:286
  122.6 2.1 %collective-permute-done.12 = bf16[136,512]{1,0:T(8,128)(2,1)S(1)} collective-permute-done((bf16[136,512]{1,0:T(8,128)(2,1)S(1)}, bf16[136,512]{1,0:T(8,128)(2,1)S(1)}, u32[]{:S(2)}, u32[]{:S(2)}) %collective-permute-start.12) | collective-permute-done | bytes 139296 | tf_op jit(solution)/shard_map/ppermute | solution.py:21
  124.9 1.3 collective-permute-start.15
  126.2 1.2 collective-permute-start.14
  127.7 7.2 %owner_sum.2.refs_0_ = f32[2048,512]{1,0:T(8,128)} custom-call(s32[1,2048]{1,0:T(1,128)S(1)} %bitcast.92, bf16[2048,384]{1,0:T(8,128)(2,1)} %bitcast.29.rows_ref), custom_call_target="tpu_custom_call" | custom-call | tf_op jit(solution)/shard_map/owner_sum/pallas_call | solution.py:170
  136.3 1.6 %collective-permute-start.17 = (bf16[4,4,32,512]{3,2,1,0:T(8,128)(2,1)S(1)}, bf16[4,4,32,512]{3,2,1,0:T(8,128)(2,1)S(1)}, u32[]{:S(2)}, u32[]{:S(2)}) collective-permute-start(bf16[4,4,32,512]{3,2,1,0:T(8,128)(2,1)S(1)} %bitcast_dynamic-update-slice_fusion), channel_id=1, source_target_pairs={{0,4},{4,0},{8,12},{12,8},{16,20},{20,16},{24,28},{28,24},{1,5},{5... | collective-permute-start | bytes 1572872 | tf_op jit(solution)/shard_map/ppermute | solution.py:16
  137.9 3.3 %owner_sum.3 = f32[2048,512]{1,0:T(8,128)} custom-call(s32[1,2048]{1,0:T(1,128)S(1)} %bitcast.93, bf16[2048,128]{1,0:T(8,128)(2,1)S(1)} %bitcast.86, f32[2048,512]{1,0:T(8,128)} %owner_sum.2.refs_0_), custom_call_target="tpu_custom_call", output_to_operand_aliasing={{}: (2, {})} | custom-call | flops 1073741824 | bytes 1572864 | tf_op jit(solution)/shard_map/owner_sum/pallas_call | solution.py:170
  141.3 1.6 %convert_multiply_fusion = (f32[2,4,4,16,512]{4,3,2,1,0:T(8,128)}, f32[2,4,4,16,512]{4,3,2,1,0:T(8,128)}) fusion(bf16[1,4,4,16,512]{4,3,2,1,0:T(8,128)(2,1)S(1)} %get-tuple-element.38, bf16[1,4,4,16,512]{4,3,2,1,0:T(8,128)(2,1)S(1)} %get-tuple-element.36, bf16[1,4,4,16,512]{4,3,2,1,0:T(8,128)(2,1)S(1)} %get-tuple-element.37, ...), kind=kLoop, calls=%fused_computation.1 | loop fusion | flops 1572864 | bytes 3145728 | tf_op jit(solution)/shard_map/mul | solution.py:357
  (79 shorter events, 8.1 us)
Async XLA Ops:
  0.6 11.9 %collective-permute-start = (bf16[8,512]{1,0:T(8,128)(2,1)}, bf16[8,512]{1,0:T(8,128)(2,1)S(1)}, u32[]{:S(2)}, u32[]{:S(2)}) collective-permute-start(bf16[8,512]{1,0:T(8,128)(2,1)} %param.15), channel_id=1, source_target_pairs={{0,1},{1,0},{2,3},{3,2},{4,5},{5,4},{6,7},{7,6},{8,9},{9,8},{10,11... | collective-permute-start | bytes 24584 | tf_op jit(solution)/shard_map/ppermute | solution.py:21
  2.8 9.8 %collective-permute-start.2 = (bf16[8,512]{1,0:T(8,128)(2,1)}, bf16[8,512]{1,0:T(8,128)(2,1)S(1)}, u32[]{:S(2)}, u32[]{:S(2)}) collective-permute-start(bf16[8,512]{1,0:T(8,128)(2,1)} %param.15), channel_id=1, source_target_pairs={{0,3},{1,2},{2,1},{3,0},{4,7},{5,6},{6,5},{7,4},{8,11},{9,10},{10,... | collective-permute-start | bytes 24584 | tf_op jit(solution)/shard_map/ppermute | solution.py:21
  5.0 7.6 %collective-permute-start.1 = (bf16[8,512]{1,0:T(8,128)(2,1)}, bf16[8,512]{1,0:T(8,128)(2,1)S(1)}, u32[]{:S(2)}, u32[]{:S(2)}) collective-permute-start(bf16[8,512]{1,0:T(8,128)(2,1)} %param.15), channel_id=1, source_target_pairs={{0,2},{1,3},{2,0},{3,1},{4,6},{5,7},{6,4},{7,5},{8,10},{9,11},{10,... | collective-permute-start | bytes 24584 | tf_op jit(solution)/shard_map/ppermute | solution.py:21
  5.1 7.4 %copy-start.10 = (bf16[8,512]{1,0:T(8,128)(2,1)S(1)}, bf16[8,512]{1,0:T(8,128)(2,1)}, u32[]{:S(2)}) copy-start(bf16[8,512]{1,0:T(8,128)(2,1)} %param.15) | copy-start | bytes 24580
  12.6 6.3 %copy-start.11 = (s32[2048]{0:T(1024)S(1)}, s32[2048]{0:T(1024)}, u32[]{:S(2)}) copy-start(s32[2048]{0:T(1024)} %param.13) | copy-start | bytes 24580
  12.6 24.7 %copy-start.1 = (bf16[2048,512]{1,0:T(8,128)(2,1)S(1)}, bf16[2048,512]{1,0:T(8,128)(2,1)}, u32[]{:S(2)}) copy-start(bf16[2048,512]{1,0:T(8,128)(2,1)} %hc_ref.5) | copy-start | bytes 6291460
  12.6 24.6 %copy-start.6 = (bf16[512,512]{1,0:T(8,128)(2,1)S(1)}, bf16[512,512]{1,0:T(8,128)(2,1)}, u32[]{:S(2)}) copy-start(bf16[512,512]{1,0:T(8,128)(2,1)} %weight_ref.3) | copy-start | bytes 1572868
  12.7 24.6 %copy-start.7 = (bf16[512,512]{1,0:T(8,128)(2,1)S(1)}, bf16[512,512]{1,0:T(8,128)(2,1)}, u32[]{:S(2)}) copy-start(bf16[512,512]{1,0:T(8,128)(2,1)} %wp_ref.1) | copy-start | bytes 1572868
  12.7 24.6 %copy-start.9 = (s32[1,32]{1,0:T(1,128)S(1)}, s32[1,32]{1,0:T(1,128)}, u32[]{:S(2)}) copy-start(s32[1,32]{1,0:T(1,128)} %count_ref.1) | copy-start | bytes 388
  12.7 54.5 %all-to-all-start = ((bf16[32,64,512]{2,1,0:T(8,128)(2,1)}), bf16[32,64,512]{2,1,0:T(8,128)(2,1)}, u32[]{:S(2)}, u32[]{:S(2)}) async-start(bf16[32,64,512]{2,1,0:T(8,128)(2,1)} %bitcast.101), calls=%async_computation | async-start | bytes 4194304 | tf_op jit(solution)/shard_map/all_to_all | solution.py:269
  19.0 16.4 %collective-permute-start.5 = (bf16[4,8,512]{2,1,0:T(8,128)(2,1)S(1)}, bf16[4,8,512]{2,1,0:T(8,128)(2,1)S(1)}, u32[]{:S(2)}, u32[]{:S(2)}) collective-permute-start(bf16[4,8,512]{2,1,0:T(8,128)(2,1)S(1)} %bitcast_dynamic-update-slice_fusion.8), channel_id=1, source_target_pairs={{0,24},{4,28},{8,16},{12,20},{16,8},{20,12},{24,0},{28,4},{1,25},{... | collective-permute-start | bytes 98312 | tf_op jit(solution)/shard_map/ppermute | solution.py:16
  21.3 13.2 %collective-permute-start.4 = (bf16[4,8,512]{2,1,0:T(8,128)(2,1)S(1)}, bf16[4,8,512]{2,1,0:T(8,128)(2,1)S(1)}, u32[]{:S(2)}, u32[]{:S(2)}) collective-permute-start(bf16[4,8,512]{2,1,0:T(8,128)(2,1)S(1)} %bitcast_dynamic-update-slice_fusion.8), channel_id=1, source_target_pairs={{0,16},{4,20},{8,24},{12,28},{16,0},{20,4},{24,8},{28,12},{1,17},{... | collective-permute-start | bytes 98312 | tf_op jit(solution)/shard_map/ppermute | solution.py:16
  21.6 12.9 %collective-permute-start.3 = (bf16[4,8,512]{2,1,0:T(8,128)(2,1)S(1)}, bf16[4,8,512]{2,1,0:T(8,128)(2,1)S(1)}, u32[]{:S(2)}, u32[]{:S(2)}) collective-permute-start(bf16[4,8,512]{2,1,0:T(8,128)(2,1)S(1)} %bitcast_dynamic-update-slice_fusion.8), channel_id=1, source_target_pairs={{0,8},{4,12},{8,0},{12,4},{16,24},{20,28},{24,16},{28,20},{1,9},{5... | collective-permute-start | bytes 98312 | tf_op jit(solution)/shard_map/ppermute | solution.py:16
  35.4 9.6 %collective-permute-start.6 = (bf16[4,4,8,512]{3,2,1,0:T(8,128)(2,1)S(1)}, bf16[4,4,8,512]{3,2,1,0:T(8,128)(2,1)S(1)}, u32[]{:S(2)}, u32[]{:S(2)}) collective-permute-start(bf16[4,4,8,512]{3,2,1,0:T(8,128)(2,1)S(1)} %bitcast_dynamic-update-slice_fusion.4), channel_id=1, source_target_pairs={{0,4},{4,0},{8,12},{12,8},{16,20},{20,16},{24,28},{28,24},{1,5},{5... | collective-permute-start | bytes 393224 | tf_op jit(solution)/shard_map/ppermute | solution.py:16
  37.3 1.6 %copy-start.2 = (bf16[2048,512]{1,0:T(8,128)(2,1)S(1)}, bf16[2048,512]{1,0:T(8,128)(2,1)}, u32[]{:S(2)}) copy-start(bf16[2048,512]{1,0:T(8,128)(2,1)} %hp_ref.5) | copy-start | bytes 6291460
  42.9 2.0 %copy-start = (f32[2048,512]{1,0:T(8,128)}, f32[2048,512]{1,0:T(8,128)S(1)}, u32[]{:S(2)}) copy-start(f32[2048,512]{1,0:T(8,128)S(1)} %slot_gate.1.gate_ref) | copy-start | bytes 12582916
  72.5 46.8 %all-to-all-start.1 = ((bf16[32,64,384]{2,1,0:T(8,128)(2,1)}), bf16[32,64,384]{2,1,0:T(8,128)(2,1)}, u32[]{:S(2)}, u32[]{:S(2)}) async-start(bf16[32,64,384]{2,1,0:T(8,128)(2,1)} %bitcast.94), calls=%async_computation.1 | async-start | bytes 3145728 | tf_op jit(solution)/shard_map/all_to_all | solution.py:286
  76.0 5.2 %copy-start.3 = (bf16[2048,512]{1,0:T(8,128)(2,1)S(1)}, bf16[2048,512]{1,0:T(8,128)(2,1)}, u32[]{:S(2)}) copy-start(bf16[2048,512]{1,0:T(8,128)(2,1)} %hp_ref.5) | copy-start | bytes 6291460
  81.2 1.6 %copy-start.5 = (bf16[2048,512]{1,0:T(8,128)(2,1)S(1)}, bf16[2048,512]{1,0:T(8,128)(2,1)}, u32[]{:S(2)}) copy-start(bf16[2048,512]{1,0:T(8,128)(2,1)} %get-tuple-element.19.delta_ref) | copy-start | bytes 6291460
  84.3 3.1 %collective-permute-start.7 = (f32[640,512]{1,0:T(8,128)S(1)}, f32[640,512]{1,0:T(8,128)S(1)}, u32[]{:S(2)}, u32[]{:S(2)}) collective-permute-start(f32[640,512]{1,0:T(8,128)S(1)} %half_terms.3), channel_id=1, source_target_pairs={{0,4},{4,0},{8,12},{12,8},{16,20},{20,16},{24,28},{28,24},{1,5},{5... | collective-permute-start | bytes 3932168 | tf_op jit(solution)/shard_map/ppermute | solution.py:16
  88.0 8.2 %collective-permute-start.8 = (bf16[4,40,512]{2,1,0:T(8,128)(2,1)S(1)}, bf16[4,40,512]{2,1,0:T(8,128)(2,1)S(1)}, u32[]{:S(2)}, u32[]{:S(2)}) collective-permute-start(bf16[4,40,512]{2,1,0:T(8,128)(2,1)S(1)} %get-tuple-element.40), channel_id=1, source_target_pairs={{0,8},{4,12},{8,0},{12,4},{16,24},{20,28},{24,16},{28,20},{1,9},{5... | collective-permute-start | bytes 491528 | tf_op jit(solution)/shard_map/ppermute | solution.py:16
  89.6 12.7 %collective-permute-start.10 = (bf16[4,40,512]{2,1,0:T(8,128)(2,1)S(1)}, bf16[4,40,512]{2,1,0:T(8,128)(2,1)S(1)}, u32[]{:S(2)}, u32[]{:S(2)}) collective-permute-start(bf16[4,40,512]{2,1,0:T(8,128)(2,1)S(1)} %get-tuple-element.41), channel_id=1, source_target_pairs={{0,24},{4,28},{8,16},{12,20},{16,8},{20,12},{24,0},{28,4},{1,25},{... | collective-permute-start | bytes 491528 | tf_op jit(solution)/shard_map/ppermute | solution.py:16
  90.6 11.7 %collective-permute-start.9 = (bf16[4,40,512]{2,1,0:T(8,128)(2,1)S(1)}, bf16[4,40,512]{2,1,0:T(8,128)(2,1)S(1)}, u32[]{:S(2)}, u32[]{:S(2)}) collective-permute-start(bf16[4,40,512]{2,1,0:T(8,128)(2,1)S(1)} %get-tuple-element.42), channel_id=1, source_target_pairs={{0,16},{4,20},{8,24},{12,28},{16,0},{20,4},{24,8},{28,12},{1,17},{... | collective-permute-start | bytes 491528 | tf_op jit(solution)/shard_map/ppermute | solution.py:16
  102.5 20.1 %collective-permute-start.13 = (bf16[136,512]{1,0:T(8,128)(2,1)S(1)}, bf16[136,512]{1,0:T(8,128)(2,1)S(1)}, u32[]{:S(2)}, u32[]{:S(2)}) collective-permute-start(bf16[136,512]{1,0:T(8,128)(2,1)S(1)} %get-tuple-element.45), channel_id=1, source_target_pairs={{0,3},{1,2},{2,1},{3,0},{4,7},{5,6},{6,5},{7,4},{8,11},{9,10},{10,... | collective-permute-start | bytes 417800 | tf_op jit(solution)/shard_map/ppermute | solution.py:21
  105.8 18.9 %collective-permute-start.12 = (bf16[136,512]{1,0:T(8,128)(2,1)S(1)}, bf16[136,512]{1,0:T(8,128)(2,1)S(1)}, u32[]{:S(2)}, u32[]{:S(2)}) collective-permute-start(bf16[136,512]{1,0:T(8,128)(2,1)S(1)} %get-tuple-element.46), channel_id=1, source_target_pairs={{0,2},{1,3},{2,0},{3,1},{4,6},{5,7},{6,4},{7,5},{8,10},{9,11},{10,... | collective-permute-start | bytes 417800 | tf_op jit(solution)/shard_map/ppermute | solution.py:21
  108.2 16.5 %collective-permute-start.11 = (bf16[136,512]{1,0:T(8,128)(2,1)S(1)}, bf16[136,512]{1,0:T(8,128)(2,1)S(1)}, u32[]{:S(2)}, u32[]{:S(2)}) collective-permute-start(bf16[136,512]{1,0:T(8,128)(2,1)S(1)} %get-tuple-element.47), channel_id=1, source_target_pairs={{0,1},{1,0},{2,3},{3,2},{4,5},{5,4},{6,7},{7,6},{8,9},{9,8},{10,11... | collective-permute-start | bytes 417800 | tf_op jit(solution)/shard_map/ppermute | solution.py:21
  119.4 18.5 %all-to-all-start.2 = ((bf16[32,64,128]{2,1,0:T(8,128)(2,1)}), bf16[32,64,128]{2,1,0:T(8,128)(2,1)S(1)}, u32[]{:S(2)}, u32[]{:S(2)}) async-start(bf16[32,64,128]{2,1,0:T(8,128)(2,1)} %bitcast.37), calls=%async_computation.2 | async-start | bytes 1048576 | tf_op jit(solution)/shard_map/all_to_all | solution.py:286
  122.6 5.1 %copy-start.8 = (s32[2048]{0:T(1024)S(1)}, s32[2048]{0:T(1024)}, u32[]{:S(2)}) copy-start(s32[2048]{0:T(1024)} %param.12) | copy-start | bytes 24580
  124.9 10.8 %collective-permute-start.15 = (bf16[4,32,512]{2,1,0:T(8,128)(2,1)S(1)}, bf16[4,32,512]{2,1,0:T(8,128)(2,1)S(1)}, u32[]{:S(2)}, u32[]{:S(2)}) collective-permute-start(bf16[4,32,512]{2,1,0:T(8,128)(2,1)S(1)} %get-tuple-element.33), channel_id=1, source_target_pairs={{0,16},{4,20},{8,24},{12,28},{16,0},{20,4},{24,8},{28,12},{1,17},{... | collective-permute-start | bytes 393224 | tf_op jit(solution)/shard_map/ppermute | solution.py:16
  126.2 9.5 %collective-permute-start.14 = (bf16[4,32,512]{2,1,0:T(8,128)(2,1)S(1)}, bf16[4,32,512]{2,1,0:T(8,128)(2,1)S(1)}, u32[]{:S(2)}, u32[]{:S(2)}) collective-permute-start(bf16[4,32,512]{2,1,0:T(8,128)(2,1)S(1)} %get-tuple-element.33), channel_id=1, source_target_pairs={{0,8},{4,12},{8,0},{12,4},{16,24},{20,28},{24,16},{28,20},{1,9},{5... | collective-permute-start | bytes 393224 | tf_op jit(solution)/shard_map/ppermute | solution.py:16
  127.4 8.8 %collective-permute-start.16 = (bf16[4,32,512]{2,1,0:T(8,128)(2,1)S(1)}, bf16[4,32,512]{2,1,0:T(8,128)(2,1)S(1)}, u32[]{:S(2)}, u32[]{:S(2)}) collective-permute-start(bf16[4,32,512]{2,1,0:T(8,128)(2,1)S(1)} %get-tuple-element.33), channel_id=1, source_target_pairs={{0,24},{4,28},{8,16},{12,20},{16,8},{20,12},{24,0},{28,4},{1,25},{... | collective-permute-start | bytes 393224 | tf_op jit(solution)/shard_map/ppermute | solution.py:16
  136.3 4.9 %collective-permute-start.17 = (bf16[4,4,32,512]{3,2,1,0:T(8,128)(2,1)S(1)}, bf16[4,4,32,512]{3,2,1,0:T(8,128)(2,1)S(1)}, u32[]{:S(2)}, u32[]{:S(2)}) collective-permute-start(bf16[4,4,32,512]{3,2,1,0:T(8,128)(2,1)S(1)} %bitcast_dynamic-update-slice_fusion), channel_id=1, source_target_pairs={{0,4},{4,0},{8,12},{12,8},{16,20},{20,16},{24,28},{28,24},{1,5},{5... | collective-permute-start | bytes 1572872 | tf_op jit(solution)/shard_map/ppermute | solution.py:16
  (1 other events, 1.3 us)
